TPU v7x, 32 devices: a whole 2x2x4 slice. The times are simulated.
32 devices in a mesh: areal: 16 (over z, y, x), layer: 2 (over core).
Axes of the slice: x: 2, y: 2, z: 4, core: 2. Of those that a mesh axis runs over, the one named last changes fastest.
Arguments:
- rhs: bfloat16 [16, 4, 112, 384], P('areal', 'layer'), may hold values from -6 to 6
- areal_blocks: bfloat16 [16, 4, 6, 384, 384], P('areal', 'layer'), may hold values from -0.078125 to 0.078125
- vertical_blocks: bfloat16 [16, 4, 2, 384, 384], P('areal', 'layer'), may hold values from -0.078125 to 0.078125
- conn_src: int32 [16, 2, 6], P('areal', 'layer'), may hold values from 0 to 31, as said below
- conn_count: int32 [16, 2], P('areal', 'layer'), may hold values from 1 to 6, as said below
- tile_map: int32 [32], replicated, may hold values from 0 to 31, as said below
- well_cells: int32 [16, 4, 4], P('areal', 'layer'), may hold values from 0 to 127
- well_gain: float32 [16, 4, 4], P('areal', 'layer'), may hold values from -24 to 24
- sens: float32 [16, 4, 3, 128], P('areal', 'layer'), may hold values from -6 to 6
- basis: bfloat16 [16, 4, 128, 256], P('areal', 'layer'), may hold values from -0.0625 to 0.0625
Outputs:
- adjoint: bfloat16 [16, 4, 112, 384], P('areal', 'layer')
- coefficients: bfloat16 [112, 256], P('layer', 'areal')
Inputs may be any that keep to these rules, and one draw needn't show every extreme that they name: Tile t of a layer group's plane is held by device column tile_map[t] // 2 in tile layer 2 g + tile_map[t] % 2; each value is held by one tile. `conn_src`: the 6 sources of device column c lie, in some order, on the 6 device columns (c + k) mod 16 with k one of 1 to 2, their negatives, 8 and 9, one on each. `conn_count`: the live connections of a device are its first ones. `well_cells`: cells of a tile, repeats allowed.
All inputs are finite; a program needn't handle non-finite values.
Results may differ from a plain program's by a relative error of at most 0.02.
Values may be sent and summed in bfloat16 or wider, within the bound.
No kernel may reach another device: no remote copies, remote signals or barrier semaphores. Data moves between devices by JAX's collectives and lax.ppermute only.
A program may use at most 64 MiB of HBM per device.

v0:
```python
import functools

import jax
import jax.numpy as jnp
from jax import lax
from jax.experimental import pallas as pl
from jax.experimental.pallas import tpu as pltpu
from jax.sharding import PartitionSpec as P

ITERS = 3
F32 = jnp.float32
BF16 = jnp.bfloat16
SMEM = pl.BlockSpec(memory_space=pltpu.SMEM)
VMEM = pl.BlockSpec(memory_space=pltpu.VMEM)
LIMIT = 16 * 1024 * 1024


def near_swaps(count):
    return [(k, color) for color in (1, 0) for k in range(count // 2 - 1, 0, -1)]


def swap_pairs(columns, k, color):
    return [
        (c, (c + k if (c // k) % 2 == color else c - k) % columns) for c in range(columns)
    ]


def held(x):
    return pltpu.with_memory_space_constraint(x, pltpu.VMEM)


def dot(a, b):
    return jnp.dot(a, b, preferred_element_type=F32)


def plan_kernel(columns, swaps, src, count, tile_map, me, group, rhs, table, asks, payload, pair):
    steps = [
        jnp.where(lax.rem(lax.div(me[0], k), 2) == color, k, columns - k) for k, color in swaps
    ] + [columns // 2 + 1, columns // 2]
    number = len(steps)
    conn = [0] * number
    slots = [0] * number
    for s in range(number):
        place = tile_map[src[s]]
        peer = lax.shift_right_logical(place, 1)
        slot = lax.bitwise_and(place, 1)
        away = peer - me[0]
        away = jnp.where(away < 0, away + columns, away)
        for i, k in enumerate(steps):
            hit = away == k
            conn[i] = jnp.where(hit, s, conn[i])
            slots[i] = jnp.where(hit, slot, slots[i])
    rows, width = rhs.shape
    line = lax.broadcasted_iota(jnp.int32, (16, width), 0)
    asked = jnp.zeros(line.shape, F32)
    for i in range(number):
        table[i] = conn[i]
        table[number + i] = jnp.where(conn[i] < count[0], 1, 0)
        asked = jnp.where(line == i, slots[i].astype(F32), asked)
    asked = jnp.where(line == number, group[0].astype(F32), asked)
    asked = jnp.where(line == number + 1, lax.rem(me[0], 2).astype(F32), asked)
    asks[...] = asked[0:8, 0:128]
    payload[0:rows] = rhs[...]
    payload[rows:] = asked.astype(BF16)
    pair[...] = rhs[...]


def load_kernel(number, two, table, group, blocks, vert, bands, sides, sems):
    width = vert.shape[-1]
    mine = group[0]
    ends = [(1 - mine, 1 - mine)] if two else [(0, 0), (1, 1)]
    beside = [
        pltpu.make_async_copy(vert.at[d, k], sides.at[i], sems.at[2 * number + i])
        for i, (d, k) in enumerate([(0, 1), (1, 0), *ends])
    ]
    for copy in beside:
        copy.start()

    def copies(i):
        return [
            pltpu.make_async_copy(
                blocks.at[d, table[i]],
                bands.at[i, :, pl.ds(d * width, width)],
                sems.at[2 * i + d],
            )
            for d in range(2)
        ]

    for i in range(number):

        @pl.when(table[number + i] > 0)
        def _():
            for copy in copies(i):
                copy.start()

        @pl.when(table[number + i] == 0)
        def _():
            bands[i] = jnp.zeros(bands.shape[1:], bands.dtype)

    for i in range(number):

        @pl.when(table[number + i] > 0)
        def _():
            for copy in copies(i):
                copy.wait()

    for copy in beside:
        copy.wait()


def turn_kernel(columns, basis, turned):
    _, cells, modes = basis.shape
    bands = []
    for d in range(2):
        by_mode = basis[d].astype(F32).T.reshape(columns, 2, modes // columns // 2, cells)
        bands += [by_mode[:, h].reshape(modes // 2, cells) for h in range(2)]
    turned[...] = jnp.concatenate(bands, axis=1).astype(BF16)


def weigh_kernel(wells, gains, sens, factors):
    cells = sens.shape[-1]
    spot = lax.broadcasted_iota(jnp.int32, (1, cells), 1)
    factors[...] = sens[...]
    for d in range(2):
        well = jnp.zeros((1, cells), F32)
        for w in range(wells.shape[1]):
            well = well + jnp.where(spot == wells[d, w], gains[d, w], 0.0)
        factors[0, d : d + 1, :] = sens[0, d : d + 1, :] + well


def wide(mask, width):
    return jnp.concatenate([mask] * (width // mask.shape[1]), axis=1)


def chosen(mask, low, high):
    return jnp.where(wide(mask, low.shape[1]) > 0.5, high, low).astype(BF16)


def asks_of(payload):
    return payload[payload.shape[0] - 16 :, 0:128].astype(F32)


def tile_of(ref, mask, rows):
    if ref.shape[0] == rows:
        return ref[...]
    return chosen(mask, ref[0:rows].astype(F32), ref[rows : 2 * rows].astype(F32))


def relay_ask_kernel(number, even, odd, asks, relayed):
    parity = asks[number + 1 : number + 2, :]
    ask = [asks_of(ref)[number - 2 : number - 1, :] for ref in (even, odd)]
    relayed[...] = asks[...]
    relayed[number - 2 : number - 1, :] = jnp.where(parity > 0.5, ask[1], ask[0])


def far_pick_kernel(number, pair, relayed, part, tile):
    tile[...] = tile_of(pair, relayed[number - 2 : number - 1, :], tile.shape[0])


def own_kernel(lam, rhs, sides, part):
    rows = rhs.shape[0] // 2
    part[0] = rhs[0:rows].astype(F32) - dot(lam[rows : 2 * rows], sides[0])
    part[1] = rhs[rows:].astype(F32) - dot(lam[0:rows], sides[1])


def source_sums(asks, bands, begin, refs, rows):
    tiles = [tile_of(ref, asks[i : i + 1, :], rows) for i, ref in enumerate(refs, begin)]
    count, width, both = len(refs), bands.shape[1], bands.shape[2]
    band = bands[begin : begin + count].reshape(count * width, both)
    sums = dot(jnp.concatenate(tiles, axis=1), band)
    return sums[:, :width], sums[:, width:]


def beside_sums(number, two, asks, sides, beside, rows):
    if two:
        mine = asks[number : number + 1, :]
        term = dot(tile_of(beside[0], mine, rows), sides[2])
        above = wide(mine, term.shape[1]) > 0.5
        none = jnp.zeros_like(term)
        return jnp.where(above, term, none), jnp.where(above, none, term)
    return [
        dot(tile_of(beside[d], jnp.full((1, 128), 1.0 - d, F32), rows), sides[2 + d])
        for d in range(2)
    ]


def cross_kernel(asks, bands, *refs):
    arrived, out = refs[:-1], refs[-1]
    out[0], out[1] = source_sums(asks, bands, 0, arrived, out.shape[1])


def far_kernel(asks, bands, cross, *refs):
    far, out = refs[:-1], refs[-1]
    low, high = source_sums(asks, bands, bands.shape[0] - len(far), far, out.shape[1])
    out[0] = cross[0] + low
    out[1] = cross[1] + high


def updated(number, two, begin, part, far, asks, bands, sides, near, beside):
    rows = part.shape[1]
    sums = source_sums(asks, bands, begin, near, rows)
    terms = beside_sums(number, two, asks, sides, beside, rows)
    return [part[d] - far[d] - sums[d] - terms[d] for d in range(2)]


def update_kernel(number, two, begin, first, part, far, asks, bands, sides, *refs):
    ends = 1 if two else 2
    here = number - 2 - begin
    near, refs = refs[:here], refs[here:]
    beside, refs = refs[:ends], refs[ends:]
    count = number - 1 if first else 1
    told, refs = refs[:count], refs[count:]
    low, high = updated(number, two, begin, part, far, asks, bands, sides, near, beside)
    lam, sends, refs = refs[0], refs[1 : 1 + number], refs[1 + number :]
    outer, refs = refs[:ends], refs[ends:]
    masks = told[0]
    if first:
        masks = refs[0]
        masks[...] = told[-1][...]
        for i in range(number - 2):
            masks[i : i + 1, :] = asks_of(told[i])[i : i + 1, :]
    rows = low.shape[0]
    lam[0:rows] = low.astype(BF16)
    lam[rows:] = high.astype(BF16)
    for i, send in enumerate(sends):
        send[...] = chosen(masks[i : i + 1, :], low, high)
    if two:
        outer[0][...] = chosen(asks[number : number + 1, :], high, low)
    else:
        outer[0][...] = high.astype(BF16)
        outer[1][...] = low.astype(BF16)


def last_kernel(number, two, begin, part, far, asks, bands, sides, factors, basis, *refs):
    here = number - 2 - begin
    near, beside, (lam, pieces) = refs[:here], refs[here:-2], refs[-2:]
    sums = updated(number, two, begin, part, far, asks, bands, sides, near, beside)
    phases, _, cells = factors.shape
    grads = []
    for d in range(2):
        rounded = sums[d].astype(BF16)
        lam[d] = rounded
        back = rounded.astype(F32)
        grad = back[:, :cells] * factors[0, d : d + 1, :]
        for p in range(1, phases):
            grad = grad + back[:, p * cells : (p + 1) * cells] * factors[p, d : d + 1, :]
        grads.append(grad)
    if two:
        half = grads[0].shape[0] // 2
        none = jnp.zeros((half, cells), F32)
        band = pieces.shape[1]
        for g in range(2):
            cuts = [grad[g * half : (g + 1) * half] for grad in grads]
            top = jnp.concatenate([x for cut in cuts for x in (cut, none)], axis=1)
            low = jnp.concatenate([x for cut in cuts for x in (none, cut)], axis=1)
            wing = jnp.concatenate([top, low], axis=0).astype(BF16)
            share = lax.dot_general(
                basis[...], wing, (((1,), (1,)), ((), ())), preferred_element_type=F32
            )
            for c in range(pieces.shape[0] // 2):
                pieces[2 * c + g] = share[c * band : (c + 1) * band]
    else:
        terms = [dot(grad.astype(BF16), basis[d]) for d, grad in enumerate(grads)]
        pieces[...] = terms[0] + terms[1]


def sum_kernel(pieces, out):
    total = pieces[0]
    for i in range(1, pieces.shape[0]):
        total = total + pieces[i]
    half = total.shape[1] // 2
    out[...] = jnp.concatenate([total[:, :half], total[:, half:]], axis=0).astype(BF16)


def call(kernel, outs, ins, specs, scratch=(), flops=0, moved=0, out_specs=None):
    return pl.pallas_call(
        kernel,
        out_shape=outs,
        in_specs=specs,
        out_specs=out_specs or [VMEM] * len(outs),
        scratch_shapes=list(scratch),
        compiler_params=pltpu.CompilerParams(vmem_limit_bytes=LIMIT),
        cost_estimate=pl.CostEstimate(
            flops=flops, bytes_accessed=moved or flops // 200, transcendentals=0
        ),
    )(*ins)


def moved_by(x, pairs):
    return held(lax.ppermute(x, "areal", pairs))


def shift_pairs(columns, k):
    return [(i, (i - k) % columns) for i in range(columns)]


def beside_layers(tiles):
    groups = lax.axis_size("layer")
    if groups == 2:
        return [held(lax.ppermute(tiles[0], "layer", [(0, 1), (1, 0)]))]
    up = [(i, i + 1) for i in range(groups - 1)]
    down = [(i + 1, i) for i in range(groups - 1)]
    return [held(lax.ppermute(tiles[0], "layer", up)), held(lax.ppermute(tiles[-1], "layer", down))]


def outside(x):
    return pltpu.with_memory_space_constraint(x, pltpu.HBM)


def on_device(
    rhs,
    areal_blocks,
    vertical_blocks,
    conn_src,
    conn_count,
    tile_map,
    well_cells,
    well_gain,
    sens,
    basis,
):
    columns = lax.axis_size("areal")
    groups = lax.axis_size("layer")
    two = groups == 2
    rows, width = rhs.shape[2:]
    modes = basis.shape[-1]
    number = conn_src.shape[-1]
    swaps = near_swaps(number)
    routes = [swap_pairs(columns, k, color) for k, color in swaps]
    routes += [shift_pairs(columns, columns // 2 + 1), shift_pairs(columns, columns // 2)]
    rhs = rhs[0].reshape(2 * rows, width)
    me = lax.axis_index("areal").astype(jnp.int32).reshape(1)
    group = lax.axis_index("layer").astype(jnp.int32).reshape(1)

    tile = pltpu.VMEM((rows, width), BF16)
    pair = pltpu.VMEM((2 * rows, width), BF16)
    sums = pltpu.VMEM((2, rows, width), F32)
    one = 2 * rows * width * width
    partial = functools.partial

    masks_type = pltpu.VMEM((8, 128), F32)
    with jax.named_scope("plan"):
        table, asks, payload, both = call(
            partial(plan_kernel, columns, swaps),
            [
                jax.ShapeDtypeStruct((2 * number,), jnp.int32),
                masks_type,
                pltpu.VMEM((2 * rows + 16, width), BF16),
                pair,
            ],
            (outside(conn_src[0, 0]), conn_count[0], outside(tile_map), me, group, outside(rhs)),
            [SMEM] * 5 + [VMEM],
            out_specs=[SMEM] + [VMEM] * 3,
        )
        asks, payload, both = held(asks), held(payload), held(both)
        far_pair = moved_by(both, routes[-1])

    with jax.named_scope("load"):
        bands, sides = call(
            partial(load_kernel, number, two),
            [
                pltpu.VMEM((number, width, 2 * width), BF16),
                pltpu.VMEM((3 if two else 4, width, width), BF16),
            ],
            (table, group, outside(areal_blocks[0]), outside(vertical_blocks[0])),
            [SMEM] * 2 + [pl.BlockSpec(memory_space=pltpu.HBM)] * 2,
            [pltpu.SemaphoreType.DMA((2 * number + 4,))],
            moved=areal_blocks.size * 2 + vertical_blocks.size * 2,
        )
        bands, sides = held(bands), held(sides)
        (factors,) = call(
            weigh_kernel,
            [pltpu.VMEM((sens.shape[2], 2, sens.shape[3]), F32)],
            (well_cells[0], well_gain[0], sens[0].transpose(1, 0, 2)),
            [SMEM] * 2 + [VMEM],
        )
        weights = held(basis[0])
        if two:
            (weights,) = call(
                partial(turn_kernel, columns),
                [pltpu.VMEM((modes // 2, 4 * sens.shape[3]), BF16)],
                (basis[0],),
                [VMEM],
            )
        factors, weights = held(factors), held(weights)

    rhs_held = lam = both
    sends = [payload] * (number - 2)
    outer = [payload]
    half = len(swaps) // 2
    for step in range(ITERS):
        first = step == 0
        with jax.named_scope("apply"):
            arrived = [moved_by(x, pairs) for x, pairs in zip(sends, routes)]
            (part,) = call(own_kernel, [sums], (lam, rhs_held, sides), [VMEM] * 3, flops=one)
            part = held(part)
            if first:
                even, odd = (arrived[swaps.index((1, color))] for color in (1, 0))
                (relayed,) = call(
                    partial(relay_ask_kernel, number),
                    [masks_type],
                    (even, odd, asks),
                    [VMEM] * 3,
                    flops=4 * one,
                )
                relayed = held(relayed)
                (picked,) = call(
                    partial(far_pick_kernel, number),
                    [tile],
                    (far_pair, relayed, part),
                    [VMEM] * 3,
                )
                arrived = [*arrived, moved_by(picked, shift_pairs(columns, 1)), far_pair]
                told = [*arrived[:-2], moved_by(relayed, routes[-1])]
            beside = beside_layers(outer)
            (cross,) = call(
                cross_kernel,
                [sums],
                (asks, bands, *arrived[:half]),
                [VMEM] * (2 + half),
                flops=4 * one,
            )
            (far,) = call(
                far_kernel,
                [sums],
                (asks, bands, held(cross), *arrived[-2:]),
                [VMEM] * 5,
                flops=4 * one,
            )
            tiles = (part, held(far), asks, bands, sides)
            near = (*arrived[half:-2], *beside)
            if step < ITERS - 1:
                lam, *rest = call(
                    partial(update_kernel, number, two, half, first),
                    [pair] + [tile] * (number + len(beside)) + ([masks_type] if first else []),
                    (*tiles, *near, *told),
                    [VMEM] * (5 + len(near) + len(told)),
                    flops=one,
                )
                lam = held(lam)
                if first:
                    told = [held(rest.pop())]
                sends, outer = rest[:number], rest[number:]
            else:
                adjoint, pieces = call(
                    partial(last_kernel, number, two, half),
                    [
                        jax.ShapeDtypeStruct((2, rows, width), BF16),
                        pltpu.VMEM(
                            (2 * columns, modes // columns // 2, rows) if two else (rows, modes), F32
                        ),
                    ],
                    (*tiles, factors, weights, *near),
                    [VMEM] * (7 + len(near)),
                    flops=one,
                )

    with jax.named_scope("project"):
        if two:
            landed = lax.all_to_all(pieces, ("areal", "layer"), 0, 0, tiled=True)
            (coefficients,) = call(
                sum_kernel,
                [jax.ShapeDtypeStruct((modes // columns, rows // 2), BF16)],
                (held(landed),),
                [VMEM],
            )
            coefficients = coefficients.T
        else:
            cut = pieces.reshape(groups, rows // groups, columns, modes // columns)
            cut = cut.transpose(2, 0, 1, 3).reshape(columns * groups, rows // groups, modes // columns)
            landed = lax.all_to_all(cut, ("areal", "layer"), 0, 0, tiled=True)
            coefficients = jnp.sum(landed, axis=0).astype(BF16)
    return (adjoint[None], coefficients)


def solution(mesh):
    in_specs = (
        P("areal", "layer", None, None),
        P("areal", "layer", None, None, None),
        P("areal", "layer", None, None, None),
        P("areal", "layer", None),
        P("areal", "layer"),
        P(),
        P("areal", "layer", None),
        P("areal", "layer", None),
        P("areal", "layer", None, None),
        P("areal", "layer", None, None),
    )
    out_specs = (P("areal", "layer", None, None), P("layer", "areal"))
    return jax.shard_map(
        on_device, mesh=mesh, in_specs=in_specs, out_specs=out_specs, check_vma=False
    )
```

profile of v0, /device:TPU:0, one launch (start us, length us, event | category | flops | bytes accessed | tf_op | source)
XLA Modules:
  0.0 72.9 jit_solution(17795447183203339172)
XLA Ops:
  1.3 1.6 %plan.1 = (s32[12]{0:T(128)S(1)}, f32[8,128]{1,0:T(8,128)S(1)}, bf16[240,384]{1,0:T(8,128)(2,1)S(1)}, bf16[224,384]{1,0:T(8,128)(2,1)S(1)}) custom-call(s32[6]{0:T(128)} %bitcast.24, s32[1]{0:T(128)} %bitcast.15.count, s32[32]{0:T(128)} %tile_map.1, s32[1]{0:T(128)} %bitcast.2.me, s32[1]{0:T(128)} %bitcast.3.group, bf16[224,384]{1,0:T(8,128)(2,1)} %bitcast.22), custom_call_target="tpu_custom_call" | custom-call | tf_op jit(solution)/shard_map/plan/pallas_call | solution.py:276
  2.9 7.0 %collective-permute-start.1 = (bf16[240,384]{1,0:T(8,128)(2,1)S(1)}, bf16[240,384]{1,0:T(8,128)(2,1)S(1)}, u32[]{:S(2)}, u32[]{:S(2)}) collective-permute-start(bf16[240,384]{1,0:T(8,128)(2,1)S(1)} %get-tuple-element.32), channel_id=1, source_target_pairs={{0,30},{2,4},{4,2},{6,8},{8,6},{10,12},{12,10},{14,16},{16,14},{18... | collective-permute-start | bytes 552968 | tf_op jit(solution)/shard_map/apply/ppermute | solution.py:290
  10.0 2.3 %collective-permute-start = (bf16[240,384]{1,0:T(8,128)(2,1)S(1)}, bf16[240,384]{1,0:T(8,128)(2,1)S(1)}, u32[]{:S(2)}, u32[]{:S(2)}) collective-permute-start(bf16[240,384]{1,0:T(8,128)(2,1)S(1)} %get-tuple-element.32), channel_id=1, source_target_pairs={{0,28},{2,30},{4,8},{6,10},{8,4},{10,6},{12,16},{14,18},{16,12},{1... | collective-permute-start | bytes 552968 | tf_op jit(solution)/shard_map/apply/ppermute | solution.py:290
  12.3 0.7 %collective-permute-start.5 = (bf16[240,384]{1,0:T(8,128)(2,1)S(1)}, bf16[240,384]{1,0:T(8,128)(2,1)S(1)}, u32[]{:S(2)}, u32[]{:S(2)}) collective-permute-start(bf16[240,384]{1,0:T(8,128)(2,1)S(1)} %get-tuple-element.32), channel_id=1, source_target_pairs={{0,4},{2,6},{4,0},{6,2},{8,12},{10,14},{12,8},{14,10},{16,20},{18,... | collective-permute-start | bytes 552968 | tf_op jit(solution)/shard_map/apply/ppermute | solution.py:290
  13.0 2.5 %collective-permute-done.1.refs_1_.even.refs_4_ = bf16[240,384]{1,0:T(8,128)(2,1)S(1)} collective-permute-done((bf16[240,384]{1,0:T(8,128)(2,1)S(1)}, bf16[240,384]{1,0:T(8,128)(2,1)S(1)}, u32[]{:S(2)}, u32[]{:S(2)}) %collective-permute-start.1) | collective-permute-done | bytes 184352 | tf_op jit(solution)/shard_map/apply/ppermute | solution.py:290
  15.5 2.6 %load.3 = (bf16[6,384,768]{2,1,0:T(8,128)(2,1)S(1)}, bf16[3,384,384]{2,1,0:T(8,128)(2,1)S(1)}) custom-call(s32[12]{0:T(128)S(1)} %get-tuple-element.28.table, s32[1]{0:T(128)} %bitcast.3.group, bf16[2,6,384,384]{3,2,1,0:T(8,128)(2,1)} %bitcast.20, bf16[2,2,384,384]{3,2,1,0:T(8,128)(2,1)} %bitcast.21), custom_call_target="tpu_custom_call" | custom-call | bytes 4718592 | tf_op jit(solution)/shard_map/load/pallas_call | solution.py:276
  18.4 3.4 %collective-permute-done.2.pair.refs_1_ = bf16[224,384]{1,0:T(8,128)(2,1)S(1)} collective-permute-done((bf16[224,384]{1,0:T(8,128)(2,1)S(1)}, bf16[224,384]{1,0:T(8,128)(2,1)S(1)}, u32[]{:S(2)}, u32[]{:S(2)}) %collective-permute-start.2) | collective-permute-done | bytes 172064 | tf_op jit(solution)/shard_map/plan/ppermute | solution.py:290
  21.8 2.9 %collective-permute-start.4 = (bf16[112,384]{1,0:T(8,128)(2,1)S(1)}, bf16[112,384]{1,0:T(8,128)(2,1)S(1)}, u32[]{:S(2)}, u32[]{:S(2)}) collective-permute-start(bf16[112,384]{1,0:T(8,128)(2,1)S(1)} %apply.17), channel_id=1, source_target_pairs={{0,30},{2,0},{4,2},{6,4},{8,6},{10,8},{12,10},{14,12},{16,14},{18,... | collective-permute-start | bytes 258056 | tf_op jit(solution)/shard_map/apply/ppermute | solution.py:290
  25.1 1.7 %collective-permute-done.4.refs_0_ = bf16[112,384]{1,0:T(8,128)(2,1)S(1)} collective-permute-done((bf16[112,384]{1,0:T(8,128)(2,1)S(1)}, bf16[112,384]{1,0:T(8,128)(2,1)S(1)}, u32[]{:S(2)}, u32[]{:S(2)}) %collective-permute-start.4) | collective-permute-done | bytes 86048 | tf_op jit(solution)/shard_map/apply/ppermute | solution.py:290
  27.2 2.1 %collective-permute-done.7.refs_7_ = f32[8,128]{1,0:T(8,128)S(1)} collective-permute-done((f32[8,128]{1,0:T(8,128)S(1)}, f32[8,128]{1,0:T(8,128)S(1)}, u32[]{:S(2)}, u32[]{:S(2)}) %collective-permute-start.7) | collective-permute-done | bytes 4128 | tf_op jit(solution)/shard_map/apply/ppermute | solution.py:290
  29.9 2.7 %collective-permute-start.8 = (bf16[112,384]{1,0:T(8,128)(2,1)S(1)}, bf16[112,384]{1,0:T(8,128)(2,1)S(1)}, u32[]{:S(2)}, u32[]{:S(2)}) collective-permute-start(bf16[112,384]{1,0:T(8,128)(2,1)S(1)} %get-tuple-element.34), channel_id=1, source_target_pairs={{0,28},{2,30},{4,8},{6,10},{8,4},{10,6},{12,16},{14,18},{16,12},{1... | collective-permute-start | bytes 258056 | tf_op jit(solution)/shard_map/apply/ppermute | solution.py:290
  32.6 1.4 %collective-permute-start.9 = (bf16[112,384]{1,0:T(8,128)(2,1)S(1)}, bf16[112,384]{1,0:T(8,128)(2,1)S(1)}, u32[]{:S(2)}, u32[]{:S(2)}) collective-permute-start(bf16[112,384]{1,0:T(8,128)(2,1)S(1)} %get-tuple-element.35), channel_id=1, source_target_pairs={{0,30},{2,4},{4,2},{6,8},{8,6},{10,12},{12,10},{14,16},{16,14},{18... | collective-permute-start | bytes 258056 | tf_op jit(solution)/shard_map/apply/ppermute | solution.py:290
  34.0 4.7 %collective-permute-start.11 = (bf16[112,384]{1,0:T(8,128)(2,1)S(1)}, bf16[112,384]{1,0:T(8,128)(2,1)S(1)}, u32[]{:S(2)}, u32[]{:S(2)}) collective-permute-start(bf16[112,384]{1,0:T(8,128)(2,1)S(1)} %get-tuple-element.37), channel_id=1, source_target_pairs={{0,16},{2,18},{4,20},{6,22},{8,24},{10,26},{12,28},{14,30},{16,0},... | collective-permute-start | bytes 258056 | tf_op jit(solution)/shard_map/apply/ppermute | solution.py:290
  38.8 1.0 %collective-permute-start.12 = (bf16[112,384]{1,0:T(8,128)(2,1)S(1)}, bf16[112,384]{1,0:T(8,128)(2,1)S(1)}, u32[]{:S(2)}, u32[]{:S(2)}) collective-permute-start(bf16[112,384]{1,0:T(8,128)(2,1)S(1)} %get-tuple-element.38), channel_id=1, source_target_pairs={{0,4},{2,6},{4,0},{6,2},{8,12},{10,14},{12,8},{14,10},{16,20},{18,... | collective-permute-start | bytes 258056 | tf_op jit(solution)/shard_map/apply/ppermute | solution.py:290
  40.3 1.1 %collective-permute-done.9.refs_1_ = bf16[112,384]{1,0:T(8,128)(2,1)S(1)} collective-permute-done((bf16[112,384]{1,0:T(8,128)(2,1)S(1)}, bf16[112,384]{1,0:T(8,128)(2,1)S(1)}, u32[]{:S(2)}, u32[]{:S(2)}) %collective-permute-start.9) | collective-permute-done | bytes 86048 | tf_op jit(solution)/shard_map/apply/ppermute | solution.py:290
  42.0 0.8 %collective-permute-done.10.refs_0_ = bf16[112,384]{1,0:T(8,128)(2,1)S(1)} collective-permute-done((bf16[112,384]{1,0:T(8,128)(2,1)S(1)}, bf16[112,384]{1,0:T(8,128)(2,1)S(1)}, u32[]{:S(2)}, u32[]{:S(2)}) %collective-permute-start.10) | collective-permute-done | bytes 86048 | tf_op jit(solution)/shard_map/apply/ppermute | solution.py:290
  43.5 0.8 %collective-permute-done.13.refs_1_ = bf16[112,384]{1,0:T(8,128)(2,1)S(1)} collective-permute-done((bf16[112,384]{1,0:T(8,128)(2,1)S(1)}, bf16[112,384]{1,0:T(8,128)(2,1)S(1)}, u32[]{:S(2)}, u32[]{:S(2)}) %collective-permute-start.13) | collective-permute-done | bytes 86048 | tf_op jit(solution)/shard_map/apply/ppermute | solution.py:290
  44.8 3.0 %collective-permute-start.15 = (bf16[112,384]{1,0:T(8,128)(2,1)S(1)}, bf16[112,384]{1,0:T(8,128)(2,1)S(1)}, u32[]{:S(2)}, u32[]{:S(2)}) collective-permute-start(bf16[112,384]{1,0:T(8,128)(2,1)S(1)} %get-tuple-element.43), channel_id=1, source_target_pairs={{0,28},{2,30},{4,8},{6,10},{8,4},{10,6},{12,16},{14,18},{16,12},{1... | collective-permute-start | bytes 258056 | tf_op jit(solution)/shard_map/apply/ppermute | solution.py:290
  47.7 2.6 %collective-permute-start.16 = (bf16[112,384]{1,0:T(8,128)(2,1)S(1)}, bf16[112,384]{1,0:T(8,128)(2,1)S(1)}, u32[]{:S(2)}, u32[]{:S(2)}) collective-permute-start(bf16[112,384]{1,0:T(8,128)(2,1)S(1)} %get-tuple-element.44), channel_id=1, source_target_pairs={{0,30},{2,4},{4,2},{6,8},{8,6},{10,12},{12,10},{14,16},{16,14},{18... | collective-permute-start | bytes 258056 | tf_op jit(solution)/shard_map/apply/ppermute | solution.py:290
  50.4 3.6 %collective-permute-start.18 = (bf16[112,384]{1,0:T(8,128)(2,1)S(1)}, bf16[112,384]{1,0:T(8,128)(2,1)S(1)}, u32[]{:S(2)}, u32[]{:S(2)}) collective-permute-start(bf16[112,384]{1,0:T(8,128)(2,1)S(1)} %get-tuple-element.46), channel_id=1, source_target_pairs={{0,16},{2,18},{4,20},{6,22},{8,24},{10,26},{12,28},{14,30},{16,0},... | collective-permute-start | bytes 258056 | tf_op jit(solution)/shard_map/apply/ppermute | solution.py:290
  53.9 1.4 %collective-permute-start.20 = (bf16[112,384]{1,0:T(8,128)(2,1)S(1)}, bf16[112,384]{1,0:T(8,128)(2,1)S(1)}, u32[]{:S(2)}, u32[]{:S(2)}) collective-permute-start(bf16[112,384]{1,0:T(8,128)(2,1)S(1)} %get-tuple-element.48), channel_id=1, source_target_pairs={{0,2},{2,0},{4,6},{6,4},{8,10},{10,8},{12,14},{14,12},{16,18},{18,... | collective-permute-start | bytes 258056 | tf_op jit(solution)/shard_map/apply/ppermute | solution.py:290
  55.3 1.4 %collective-permute-done.16.refs_1_ = bf16[112,384]{1,0:T(8,128)(2,1)S(1)} collective-permute-done((bf16[112,384]{1,0:T(8,128)(2,1)S(1)}, bf16[112,384]{1,0:T(8,128)(2,1)S(1)}, u32[]{:S(2)}, u32[]{:S(2)}) %collective-permute-start.16) | collective-permute-done | bytes 86048 | tf_op jit(solution)/shard_map/apply/ppermute | solution.py:290
  58.9 1.1 %apply.27 = (bf16[2,112,384]{2,1,0:T(8,128)(2,1)}, f32[32,8,112]{2,1,0:T(8,128)S(1)}) custom-call(f32[2,112,384]{2,1,0:T(8,128)S(1)} %apply.24.part, f32[2,112,384]{2,1,0:T(8,128)S(1)} %apply.26.far, f32[8,128]{1,0:T(8,128)S(1)} %get-tuple-element.30.asks, bf16[6,384,768]{2,1,0:T(8,128)(2,1)S(1)} %get-tuple-element.31.bands, ...), custom_call_target="tpu_custom_call" | custom-call | flops 33030144 | bytes 165150 | tf_op jit(solution)/shard_map/apply/pallas_call | solution.py:276
  60.0 12.1 %all_to_all.5.pieces = f32[32,8,112]{2,1,0:T(8,128)S(1)} all-to-all(f32[32,8,112]{2,1,0:T(8,128)S(1)} %get-tuple-element.51), channel_id=1, replica_groups=mesh['areal'=16,'layer'=2] {'areal','layer'}, dimensions={0} | all-to-all | bytes 229376 | tf_op jit(solution)/shard_map/project/all_to_all | solution.py:460
  (48 shorter events, 6.7 us)
Async XLA Ops:
  2.9 12.6 %collective-permute-start.1 = (bf16[240,384]{1,0:T(8,128)(2,1)S(1)}, bf16[240,384]{1,0:T(8,128)(2,1)S(1)}, u32[]{:S(2)}, u32[]{:S(2)}) collective-permute-start(bf16[240,384]{1,0:T(8,128)(2,1)S(1)} %get-tuple-element.32), channel_id=1, source_target_pairs={{0,30},{2,4},{4,2},{6,8},{8,6},{10,12},{12,10},{14,16},{16,14},{18... | collective-permute-start | bytes 552968 | tf_op jit(solution)/shard_map/apply/ppermute | solution.py:290
  9.9 8.5 %collective-permute-start.3 = (bf16[240,384]{1,0:T(8,128)(2,1)S(1)}, bf16[240,384]{1,0:T(8,128)(2,1)S(1)}, u32[]{:S(2)}, u32[]{:S(2)}) collective-permute-start(bf16[240,384]{1,0:T(8,128)(2,1)S(1)} %get-tuple-element.32), channel_id=1, source_target_pairs={{0,2},{2,0},{4,6},{6,4},{8,10},{10,8},{12,14},{14,12},{16,18},{18,... | collective-permute-start | bytes 552968 | tf_op jit(solution)/shard_map/apply/ppermute | solution.py:290
  9.9 11.9 %collective-permute-start.2 = (bf16[224,384]{1,0:T(8,128)(2,1)S(1)}, bf16[224,384]{1,0:T(8,128)(2,1)S(1)}, u32[]{:S(2)}, u32[]{:S(2)}) collective-permute-start(bf16[224,384]{1,0:T(8,128)(2,1)S(1)} %get-tuple-element.27.lam.rhs), channel_id=1, source_target_pairs={{0,16},{2,18},{4,20},{6,22},{8,24},{10,26},{12,28},{14,30},{16,0},... | collective-permute-start | bytes 516104 | tf_op jit(solution)/shard_map/plan/ppermute | solution.py:290
  10.0 14.8 %collective-permute-start = (bf16[240,384]{1,0:T(8,128)(2,1)S(1)}, bf16[240,384]{1,0:T(8,128)(2,1)S(1)}, u32[]{:S(2)}, u32[]{:S(2)}) collective-permute-start(bf16[240,384]{1,0:T(8,128)(2,1)S(1)} %get-tuple-element.32), channel_id=1, source_target_pairs={{0,28},{2,30},{4,8},{6,10},{8,4},{10,6},{12,16},{14,18},{16,12},{1... | collective-permute-start | bytes 552968 | tf_op jit(solution)/shard_map/apply/ppermute | solution.py:290
  12.3 14.9 %collective-permute-start.5 = (bf16[240,384]{1,0:T(8,128)(2,1)S(1)}, bf16[240,384]{1,0:T(8,128)(2,1)S(1)}, u32[]{:S(2)}, u32[]{:S(2)}) collective-permute-start(bf16[240,384]{1,0:T(8,128)(2,1)S(1)} %get-tuple-element.32), channel_id=1, source_target_pairs={{0,4},{2,6},{4,0},{6,2},{8,12},{10,14},{12,8},{14,10},{16,20},{18,... | collective-permute-start | bytes 552968 | tf_op jit(solution)/shard_map/apply/ppermute | solution.py:290
  15.5 11.7 %collective-permute-start.6 = (bf16[240,384]{1,0:T(8,128)(2,1)S(1)}, bf16[240,384]{1,0:T(8,128)(2,1)S(1)}, u32[]{:S(2)}, u32[]{:S(2)}) collective-permute-start(bf16[240,384]{1,0:T(8,128)(2,1)S(1)} %get-tuple-element.32), channel_id=1, source_target_pairs={{0,1},{1,0},{2,3},{3,2},{4,5},{5,4},{6,7},{7,6},{8,9},{9,8},{10,11... | collective-permute-start | bytes 552968 | tf_op jit(solution)/shard_map/apply/ppermute | solution.py:300
  21.8 5.0 %collective-permute-start.4 = (bf16[112,384]{1,0:T(8,128)(2,1)S(1)}, bf16[112,384]{1,0:T(8,128)(2,1)S(1)}, u32[]{:S(2)}, u32[]{:S(2)}) collective-permute-start(bf16[112,384]{1,0:T(8,128)(2,1)S(1)} %apply.17), channel_id=1, source_target_pairs={{0,30},{2,0},{4,2},{6,4},{8,6},{10,8},{12,10},{14,12},{16,14},{18,... | collective-permute-start | bytes 258056 | tf_op jit(solution)/shard_map/apply/ppermute | solution.py:290
  24.8 4.6 %collective-permute-start.7 = (f32[8,128]{1,0:T(8,128)S(1)}, f32[8,128]{1,0:T(8,128)S(1)}, u32[]{:S(2)}, u32[]{:S(2)}) collective-permute-start(f32[8,128]{1,0:T(8,128)S(1)} %apply.16.relayed), channel_id=1, source_target_pairs={{0,16},{2,18},{4,20},{6,22},{8,24},{10,26},{12,28},{14,30},{16,0},... | collective-permute-start | bytes 12296 | tf_op jit(solution)/shard_map/apply/ppermute | solution.py:290
  29.9 9.9 %collective-permute-start.8 = (bf16[112,384]{1,0:T(8,128)(2,1)S(1)}, bf16[112,384]{1,0:T(8,128)(2,1)S(1)}, u32[]{:S(2)}, u32[]{:S(2)}) collective-permute-start(bf16[112,384]{1,0:T(8,128)(2,1)S(1)} %get-tuple-element.34), channel_id=1, source_target_pairs={{0,28},{2,30},{4,8},{6,10},{8,4},{10,6},{12,16},{14,18},{16,12},{1... | collective-permute-start | bytes 258056 | tf_op jit(solution)/shard_map/apply/ppermute | solution.py:290
  32.6 8.8 %collective-permute-start.9 = (bf16[112,384]{1,0:T(8,128)(2,1)S(1)}, bf16[112,384]{1,0:T(8,128)(2,1)S(1)}, u32[]{:S(2)}, u32[]{:S(2)}) collective-permute-start(bf16[112,384]{1,0:T(8,128)(2,1)S(1)} %get-tuple-element.35), channel_id=1, source_target_pairs={{0,30},{2,4},{4,2},{6,8},{8,6},{10,12},{12,10},{14,16},{16,14},{18... | collective-permute-start | bytes 258056 | tf_op jit(solution)/shard_map/apply/ppermute | solution.py:290
  33.9 8.8 %collective-permute-start.10 = (bf16[112,384]{1,0:T(8,128)(2,1)S(1)}, bf16[112,384]{1,0:T(8,128)(2,1)S(1)}, u32[]{:S(2)}, u32[]{:S(2)}) collective-permute-start(bf16[112,384]{1,0:T(8,128)(2,1)S(1)} %get-tuple-element.36), channel_id=1, source_target_pairs={{0,14},{2,16},{4,18},{6,20},{8,22},{10,24},{12,26},{14,28},{16,30}... | collective-permute-start | bytes 258056 | tf_op jit(solution)/shard_map/apply/ppermute | solution.py:290
  34.0 9.0 %collective-permute-start.11 = (bf16[112,384]{1,0:T(8,128)(2,1)S(1)}, bf16[112,384]{1,0:T(8,128)(2,1)S(1)}, u32[]{:S(2)}, u32[]{:S(2)}) collective-permute-start(bf16[112,384]{1,0:T(8,128)(2,1)S(1)} %get-tuple-element.37), channel_id=1, source_target_pairs={{0,16},{2,18},{4,20},{6,22},{8,24},{10,26},{12,28},{14,30},{16,0},... | collective-permute-start | bytes 258056 | tf_op jit(solution)/shard_map/apply/ppermute | solution.py:290
  38.8 4.7 %collective-permute-start.12 = (bf16[112,384]{1,0:T(8,128)(2,1)S(1)}, bf16[112,384]{1,0:T(8,128)(2,1)S(1)}, u32[]{:S(2)}, u32[]{:S(2)}) collective-permute-start(bf16[112,384]{1,0:T(8,128)(2,1)S(1)} %get-tuple-element.38), channel_id=1, source_target_pairs={{0,4},{2,6},{4,0},{6,2},{8,12},{10,14},{12,8},{14,10},{16,20},{18,... | collective-permute-start | bytes 258056 | tf_op jit(solution)/shard_map/apply/ppermute | solution.py:290
  39.8 4.5 %collective-permute-start.13 = (bf16[112,384]{1,0:T(8,128)(2,1)S(1)}, bf16[112,384]{1,0:T(8,128)(2,1)S(1)}, u32[]{:S(2)}, u32[]{:S(2)}) collective-permute-start(bf16[112,384]{1,0:T(8,128)(2,1)S(1)} %get-tuple-element.39), channel_id=1, source_target_pairs={{0,2},{2,0},{4,6},{6,4},{8,10},{10,8},{12,14},{14,12},{16,18},{18,... | collective-permute-start | bytes 258056 | tf_op jit(solution)/shard_map/apply/ppermute | solution.py:290
  41.4 2.9 %collective-permute-start.14 = (bf16[112,384]{1,0:T(8,128)(2,1)S(1)}, bf16[112,384]{1,0:T(8,128)(2,1)S(1)}, u32[]{:S(2)}, u32[]{:S(2)}) collective-permute-start(bf16[112,384]{1,0:T(8,128)(2,1)S(1)} %get-tuple-element.40), channel_id=1, source_target_pairs={{0,1},{1,0},{2,3},{3,2},{4,5},{5,4},{6,7},{7,6},{8,9},{9,8},{10,11... | collective-permute-start | bytes 258056 | tf_op jit(solution)/shard_map/apply/ppermute | solution.py:300
  43.4 13.5 %copy-start.1 = (f32[1,2,3,128]{3,1,2,0:T(2,128)S(1)}, f32[1,2,3,128]{3,1,2,0:T(2,128)}, u32[]{:S(2)}) copy-start(f32[1,2,3,128]{3,1,2,0:T(2,128)} %param.18) | copy-start | bytes 9220
  43.4 13.5 %copy-start.2 = (s32[1,2,4]{2,1,0:T(2,128)S(1)}, s32[1,2,4]{2,1,0:T(2,128)}, u32[]{:S(2)}) copy-start(s32[1,2,4]{2,1,0:T(2,128)} %param.16) | copy-start | bytes 100
  44.8 9.2 %collective-permute-start.15 = (bf16[112,384]{1,0:T(8,128)(2,1)S(1)}, bf16[112,384]{1,0:T(8,128)(2,1)S(1)}, u32[]{:S(2)}, u32[]{:S(2)}) collective-permute-start(bf16[112,384]{1,0:T(8,128)(2,1)S(1)} %get-tuple-element.43), channel_id=1, source_target_pairs={{0,28},{2,30},{4,8},{6,10},{8,4},{10,6},{12,16},{14,18},{16,12},{1... | collective-permute-start | bytes 258056 | tf_op jit(solution)/shard_map/apply/ppermute | solution.py:290
  47.7 9.0 %collective-permute-start.16 = (bf16[112,384]{1,0:T(8,128)(2,1)S(1)}, bf16[112,384]{1,0:T(8,128)(2,1)S(1)}, u32[]{:S(2)}, u32[]{:S(2)}) collective-permute-start(bf16[112,384]{1,0:T(8,128)(2,1)S(1)} %get-tuple-element.44), channel_id=1, source_target_pairs={{0,30},{2,4},{4,2},{6,8},{8,6},{10,12},{12,10},{14,16},{16,14},{18... | collective-permute-start | bytes 258056 | tf_op jit(solution)/shard_map/apply/ppermute | solution.py:290
  50.4 8.2 %collective-permute-start.17 = (bf16[112,384]{1,0:T(8,128)(2,1)S(1)}, bf16[112,384]{1,0:T(8,128)(2,1)S(1)}, u32[]{:S(2)}, u32[]{:S(2)}) collective-permute-start(bf16[112,384]{1,0:T(8,128)(2,1)S(1)} %get-tuple-element.45), channel_id=1, source_target_pairs={{0,14},{2,16},{4,18},{6,20},{8,22},{10,24},{12,26},{14,28},{16,30}... | collective-permute-start | bytes 258056 | tf_op jit(solution)/shard_map/apply/ppermute | solution.py:290
  50.4 8.2 %collective-permute-start.18 = (bf16[112,384]{1,0:T(8,128)(2,1)S(1)}, bf16[112,384]{1,0:T(8,128)(2,1)S(1)}, u32[]{:S(2)}, u32[]{:S(2)}) collective-permute-start(bf16[112,384]{1,0:T(8,128)(2,1)S(1)} %get-tuple-element.46), channel_id=1, source_target_pairs={{0,16},{2,18},{4,20},{6,22},{8,24},{10,26},{12,28},{14,30},{16,0},... | collective-permute-start | bytes 258056 | tf_op jit(solution)/shard_map/apply/ppermute | solution.py:290
  53.9 5.0 %collective-permute-start.19 = (bf16[112,384]{1,0:T(8,128)(2,1)S(1)}, bf16[112,384]{1,0:T(8,128)(2,1)S(1)}, u32[]{:S(2)}, u32[]{:S(2)}) collective-permute-start(bf16[112,384]{1,0:T(8,128)(2,1)S(1)} %get-tuple-element.47), channel_id=1, source_target_pairs={{0,4},{2,6},{4,0},{6,2},{8,12},{10,14},{12,8},{14,10},{16,20},{18,... | collective-permute-start | bytes 258056 | tf_op jit(solution)/shard_map/apply/ppermute | solution.py:290
  53.9 5.0 %collective-permute-start.20 = (bf16[112,384]{1,0:T(8,128)(2,1)S(1)}, bf16[112,384]{1,0:T(8,128)(2,1)S(1)}, u32[]{:S(2)}, u32[]{:S(2)}) collective-permute-start(bf16[112,384]{1,0:T(8,128)(2,1)S(1)} %get-tuple-element.48), channel_id=1, source_target_pairs={{0,2},{2,0},{4,6},{6,4},{8,10},{10,8},{12,14},{14,12},{16,18},{18,... | collective-permute-start | bytes 258056 | tf_op jit(solution)/shard_map/apply/ppermute | solution.py:290
  56.7 2.2 %collective-permute-start.21 = (bf16[112,384]{1,0:T(8,128)(2,1)S(1)}, bf16[112,384]{1,0:T(8,128)(2,1)S(1)}, u32[]{:S(2)}, u32[]{:S(2)}) collective-permute-start(bf16[112,384]{1,0:T(8,128)(2,1)S(1)} %get-tuple-element.49), channel_id=1, source_target_pairs={{0,1},{1,0},{2,3},{3,2},{4,5},{5,4},{6,7},{7,6},{8,9},{9,8},{10,11... | collective-permute-start | bytes 258056 | tf_op jit(solution)/shard_map/apply/ppermute | solution.py:300
  (2 other events, 26.8 us)
where the time goes:
time: 73.2 us; the launch traced here: 72.9 us
  starting transfers between devices  34 us (46%)
  waiting for transfers between devices  14.7 us (20%)
  blocking collectives  12.1 us (17%)
  Pallas kernels  10.5 us (14%)
  between operations  1.52 us (2%)
    ppermute x19, starting transfers between devices, moved_by(): return held(lax.ppermute(x, 'areal', pairs))  34 us
    ppermute x19, waiting for transfers between devices, moved_by(): return held(lax.ppermute(x, 'areal', pairs))  14.7 us
    all_to_all x1, blocking collectives, on_device(): landed = lax.all_to_all(pieces, ('areal', 'layer'), 0, 0, tiled=True)  12.1 us
    pallas_call x19, Pallas kernels, call(): pl.pallas_call(kernel, out_shape=outs, in_specs=specs, out_specs=out_spec...  10.5 us
  transfers between devices with their start and end apart: 22, of which 10 were waited for; matrix products, arithmetic and copies ran while one was open for 0% of the time, Pallas kernels for 8%

commit v1 on v0

--- a/solution.py
+++ b/solution.py
@@ -258,16 +258,16 @@
                 basis[...], wing, (((1,), (1,)), ((), ())), preferred_element_type=F32
             )
             for c in range(pieces.shape[0] // 2):
-                pieces[2 * c + g] = share[c * band : (c + 1) * band]
+                pieces[2 * c + g] = share[c * band : (c + 1) * band].astype(BF16)
     else:
         terms = [dot(grad.astype(BF16), basis[d]) for d, grad in enumerate(grads)]
         pieces[...] = terms[0] + terms[1]
 
 
 def sum_kernel(pieces, out):
-    total = pieces[0]
+    total = pieces[0].astype(F32)
     for i in range(1, pieces.shape[0]):
-        total = total + pieces[i]
+        total = total + pieces[i].astype(F32)
     half = total.shape[1] // 2
     out[...] = jnp.concatenate([total[:, :half], total[:, half:]], axis=0).astype(BF16)
 
@@ -446,9 +446,9 @@
                     partial(last_kernel, number, two, half),
                     [
                         jax.ShapeDtypeStruct((2, rows, width), BF16),
-                        pltpu.VMEM(
-                            (2 * columns, modes // columns // 2, rows) if two else (rows, modes), F32
-                        ),
+                        pltpu.VMEM((2 * columns, modes // columns // 2, rows), BF16)
+                        if two
+                        else pltpu.VMEM((rows, modes), F32),
                     ],
                     (*tiles, factors, weights, *near),
                     [VMEM] * (7 + len(near)),

time: 73.2 us -> 72.3 us (0.988)
  blocking collectives: 12.1 us -> 11.3 us
    all_to_all x1, blocking collectives: 12.1 us -> 11.3 us  [on_device(): landed = lax.all_to_all(pieces, ('areal', 'layer'), 0, 0, tiled=True)]
where the time goes in v1:
time: 72.3 us; the launch traced here: 72.1 us
  starting transfers between devices  34 us (47%)
  waiting for transfers between devices  15.1 us (21%)
  blocking collectives  11.3 us (16%)
  Pallas kernels  10.1 us (14%)
  between operations  1.52 us (2%)
    ppermute x19, starting transfers between devices, moved_by(): return held(lax.ppermute(x, 'areal', pairs))  34 us
    ppermute x19, waiting for transfers between devices, moved_by(): return held(lax.ppermute(x, 'areal', pairs))  15.1 us
    all_to_all x1, blocking collectives, on_device(): landed = lax.all_to_all(pieces, ('areal', 'layer'), 0, 0, tiled=True)  11.3 us
    pallas_call x19, Pallas kernels, call(): pl.pallas_call(kernel, out_shape=outs, in_specs=specs, out_specs=out_spec...  10.1 us
  transfers between devices with their start and end apart: 22, of which 10 were waited for; matrix products, arithmetic and copies ran while one was open for 0% of the time, Pallas kernels for 8%

profile of v1, /device:TPU:0, one launch (start us, length us, event | category | flops | bytes accessed | tf_op | source)
XLA Modules:
  0.0 72.1 jit_solution(2400179394653327374)
XLA Ops:
  1.3 1.6 %plan.1 = (s32[12]{0:T(128)S(1)}, f32[8,128]{1,0:T(8,128)S(1)}, bf16[240,384]{1,0:T(8,128)(2,1)S(1)}, bf16[224,384]{1,0:T(8,128)(2,1)S(1)}) custom-call(s32[6]{0:T(128)} %bitcast.24, s32[1]{0:T(128)} %bitcast.15.count, s32[32]{0:T(128)} %tile_map.1, s32[1]{0:T(128)} %bitcast.2.me, s32[1]{0:T(128)} %bitcast.3.group, bf16[224,384]{1,0:T(8,128)(2,1)} %bitcast.22), custom_call_target="tpu_custom_call" | custom-call | tf_op jit(solution)/shard_map/plan/pallas_call | solution.py:276
  2.9 7.0 %collective-permute-start.1 = (bf16[240,384]{1,0:T(8,128)(2,1)S(1)}, bf16[240,384]{1,0:T(8,128)(2,1)S(1)}, u32[]{:S(2)}, u32[]{:S(2)}) collective-permute-start(bf16[240,384]{1,0:T(8,128)(2,1)S(1)} %get-tuple-element.32), channel_id=1, source_target_pairs={{0,30},{2,4},{4,2},{6,8},{8,6},{10,12},{12,10},{14,16},{16,14},{18... | collective-permute-start | bytes 552968 | tf_op jit(solution)/shard_map/apply/ppermute | solution.py:290
  10.0 2.3 %collective-permute-start = (bf16[240,384]{1,0:T(8,128)(2,1)S(1)}, bf16[240,384]{1,0:T(8,128)(2,1)S(1)}, u32[]{:S(2)}, u32[]{:S(2)}) collective-permute-start(bf16[240,384]{1,0:T(8,128)(2,1)S(1)} %get-tuple-element.32), channel_id=1, source_target_pairs={{0,28},{2,30},{4,8},{6,10},{8,4},{10,6},{12,16},{14,18},{16,12},{1... | collective-permute-start | bytes 552968 | tf_op jit(solution)/shard_map/apply/ppermute | solution.py:290
  12.3 0.7 %collective-permute-start.5 = (bf16[240,384]{1,0:T(8,128)(2,1)S(1)}, bf16[240,384]{1,0:T(8,128)(2,1)S(1)}, u32[]{:S(2)}, u32[]{:S(2)}) collective-permute-start(bf16[240,384]{1,0:T(8,128)(2,1)S(1)} %get-tuple-element.32), channel_id=1, source_target_pairs={{0,4},{2,6},{4,0},{6,2},{8,12},{10,14},{12,8},{14,10},{16,20},{18,... | collective-permute-start | bytes 552968 | tf_op jit(solution)/shard_map/apply/ppermute | solution.py:290
  13.0 2.5 %collective-permute-done.1.refs_1_.even.refs_4_ = bf16[240,384]{1,0:T(8,128)(2,1)S(1)} collective-permute-done((bf16[240,384]{1,0:T(8,128)(2,1)S(1)}, bf16[240,384]{1,0:T(8,128)(2,1)S(1)}, u32[]{:S(2)}, u32[]{:S(2)}) %collective-permute-start.1) | collective-permute-done | bytes 184352 | tf_op jit(solution)/shard_map/apply/ppermute | solution.py:290
  15.5 2.2 %load.3 = (bf16[6,384,768]{2,1,0:T(8,128)(2,1)S(1)}, bf16[3,384,384]{2,1,0:T(8,128)(2,1)S(1)}) custom-call(s32[12]{0:T(128)S(1)} %get-tuple-element.28.table, s32[1]{0:T(128)} %bitcast.3.group, bf16[2,6,384,384]{3,2,1,0:T(8,128)(2,1)} %bitcast.20, bf16[2,2,384,384]{3,2,1,0:T(8,128)(2,1)} %bitcast.21), custom_call_target="tpu_custom_call" | custom-call | bytes 4718592 | tf_op jit(solution)/shard_map/load/pallas_call | solution.py:276
  18.0 3.8 %collective-permute-done.2.pair.refs_1_ = bf16[224,384]{1,0:T(8,128)(2,1)S(1)} collective-permute-done((bf16[224,384]{1,0:T(8,128)(2,1)S(1)}, bf16[224,384]{1,0:T(8,128)(2,1)S(1)}, u32[]{:S(2)}, u32[]{:S(2)}) %collective-permute-start.2) | collective-permute-done | bytes 172064 | tf_op jit(solution)/shard_map/plan/ppermute | solution.py:290
  21.8 2.9 %collective-permute-start.4 = (bf16[112,384]{1,0:T(8,128)(2,1)S(1)}, bf16[112,384]{1,0:T(8,128)(2,1)S(1)}, u32[]{:S(2)}, u32[]{:S(2)}) collective-permute-start(bf16[112,384]{1,0:T(8,128)(2,1)S(1)} %apply.17), channel_id=1, source_target_pairs={{0,30},{2,0},{4,2},{6,4},{8,6},{10,8},{12,10},{14,12},{16,14},{18,... | collective-permute-start | bytes 258056 | tf_op jit(solution)/shard_map/apply/ppermute | solution.py:290
  25.1 1.7 %collective-permute-done.4.refs_0_ = bf16[112,384]{1,0:T(8,128)(2,1)S(1)} collective-permute-done((bf16[112,384]{1,0:T(8,128)(2,1)S(1)}, bf16[112,384]{1,0:T(8,128)(2,1)S(1)}, u32[]{:S(2)}, u32[]{:S(2)}) %collective-permute-start.4) | collective-permute-done | bytes 86048 | tf_op jit(solution)/shard_map/apply/ppermute | solution.py:290
  27.2 2.1 %collective-permute-done.7.refs_7_ = f32[8,128]{1,0:T(8,128)S(1)} collective-permute-done((f32[8,128]{1,0:T(8,128)S(1)}, f32[8,128]{1,0:T(8,128)S(1)}, u32[]{:S(2)}, u32[]{:S(2)}) %collective-permute-start.7) | collective-permute-done | bytes 4128 | tf_op jit(solution)/shard_map/apply/ppermute | solution.py:290
  29.9 2.7 %collective-permute-start.8 = (bf16[112,384]{1,0:T(8,128)(2,1)S(1)}, bf16[112,384]{1,0:T(8,128)(2,1)S(1)}, u32[]{:S(2)}, u32[]{:S(2)}) collective-permute-start(bf16[112,384]{1,0:T(8,128)(2,1)S(1)} %get-tuple-element.34), channel_id=1, source_target_pairs={{0,28},{2,30},{4,8},{6,10},{8,4},{10,6},{12,16},{14,18},{16,12},{1... | collective-permute-start | bytes 258056 | tf_op jit(solution)/shard_map/apply/ppermute | solution.py:290
  32.6 1.4 %collective-permute-start.9 = (bf16[112,384]{1,0:T(8,128)(2,1)S(1)}, bf16[112,384]{1,0:T(8,128)(2,1)S(1)}, u32[]{:S(2)}, u32[]{:S(2)}) collective-permute-start(bf16[112,384]{1,0:T(8,128)(2,1)S(1)} %get-tuple-element.35), channel_id=1, source_target_pairs={{0,30},{2,4},{4,2},{6,8},{8,6},{10,12},{12,10},{14,16},{16,14},{18... | collective-permute-start | bytes 258056 | tf_op jit(solution)/shard_map/apply/ppermute | solution.py:290
  34.0 4.7 %collective-permute-start.11 = (bf16[112,384]{1,0:T(8,128)(2,1)S(1)}, bf16[112,384]{1,0:T(8,128)(2,1)S(1)}, u32[]{:S(2)}, u32[]{:S(2)}) collective-permute-start(bf16[112,384]{1,0:T(8,128)(2,1)S(1)} %get-tuple-element.37), channel_id=1, source_target_pairs={{0,16},{2,18},{4,20},{6,22},{8,24},{10,26},{12,28},{14,30},{16,0},... | collective-permute-start | bytes 258056 | tf_op jit(solution)/shard_map/apply/ppermute | solution.py:290
  38.8 1.0 %collective-permute-start.12 = (bf16[112,384]{1,0:T(8,128)(2,1)S(1)}, bf16[112,384]{1,0:T(8,128)(2,1)S(1)}, u32[]{:S(2)}, u32[]{:S(2)}) collective-permute-start(bf16[112,384]{1,0:T(8,128)(2,1)S(1)} %get-tuple-element.38), channel_id=1, source_target_pairs={{0,4},{2,6},{4,0},{6,2},{8,12},{10,14},{12,8},{14,10},{16,20},{18,... | collective-permute-start | bytes 258056 | tf_op jit(solution)/shard_map/apply/ppermute | solution.py:290
  40.3 1.1 %collective-permute-done.9.refs_1_ = bf16[112,384]{1,0:T(8,128)(2,1)S(1)} collective-permute-done((bf16[112,384]{1,0:T(8,128)(2,1)S(1)}, bf16[112,384]{1,0:T(8,128)(2,1)S(1)}, u32[]{:S(2)}, u32[]{:S(2)}) %collective-permute-start.9) | collective-permute-done | bytes 86048 | tf_op jit(solution)/shard_map/apply/ppermute | solution.py:290
  42.0 0.8 %collective-permute-done.10.refs_0_ = bf16[112,384]{1,0:T(8,128)(2,1)S(1)} collective-permute-done((bf16[112,384]{1,0:T(8,128)(2,1)S(1)}, bf16[112,384]{1,0:T(8,128)(2,1)S(1)}, u32[]{:S(2)}, u32[]{:S(2)}) %collective-permute-start.10) | collective-permute-done | bytes 86048 | tf_op jit(solution)/shard_map/apply/ppermute | solution.py:290
  43.5 0.8 %collective-permute-done.13.refs_1_ = bf16[112,384]{1,0:T(8,128)(2,1)S(1)} collective-permute-done((bf16[112,384]{1,0:T(8,128)(2,1)S(1)}, bf16[112,384]{1,0:T(8,128)(2,1)S(1)}, u32[]{:S(2)}, u32[]{:S(2)}) %collective-permute-start.13) | collective-permute-done | bytes 86048 | tf_op jit(solution)/shard_map/apply/ppermute | solution.py:290
  44.8 3.0 %collective-permute-start.15 = (bf16[112,384]{1,0:T(8,128)(2,1)S(1)}, bf16[112,384]{1,0:T(8,128)(2,1)S(1)}, u32[]{:S(2)}, u32[]{:S(2)}) collective-permute-start(bf16[112,384]{1,0:T(8,128)(2,1)S(1)} %get-tuple-element.43), channel_id=1, source_target_pairs={{0,28},{2,30},{4,8},{6,10},{8,4},{10,6},{12,16},{14,18},{16,12},{1... | collective-permute-start | bytes 258056 | tf_op jit(solution)/shard_map/apply/ppermute | solution.py:290
  47.7 2.6 %collective-permute-start.16 = (bf16[112,384]{1,0:T(8,128)(2,1)S(1)}, bf16[112,384]{1,0:T(8,128)(2,1)S(1)}, u32[]{:S(2)}, u32[]{:S(2)}) collective-permute-start(bf16[112,384]{1,0:T(8,128)(2,1)S(1)} %get-tuple-element.44), channel_id=1, source_target_pairs={{0,30},{2,4},{4,2},{6,8},{8,6},{10,12},{12,10},{14,16},{16,14},{18... | collective-permute-start | bytes 258056 | tf_op jit(solution)/shard_map/apply/ppermute | solution.py:290
  50.4 3.6 %collective-permute-start.18 = (bf16[112,384]{1,0:T(8,128)(2,1)S(1)}, bf16[112,384]{1,0:T(8,128)(2,1)S(1)}, u32[]{:S(2)}, u32[]{:S(2)}) collective-permute-start(bf16[112,384]{1,0:T(8,128)(2,1)S(1)} %get-tuple-element.46), channel_id=1, source_target_pairs={{0,16},{2,18},{4,20},{6,22},{8,24},{10,26},{12,28},{14,30},{16,0},... | collective-permute-start | bytes 258056 | tf_op jit(solution)/shard_map/apply/ppermute | solution.py:290
  53.9 1.4 %collective-permute-start.20 = (bf16[112,384]{1,0:T(8,128)(2,1)S(1)}, bf16[112,384]{1,0:T(8,128)(2,1)S(1)}, u32[]{:S(2)}, u32[]{:S(2)}) collective-permute-start(bf16[112,384]{1,0:T(8,128)(2,1)S(1)} %get-tuple-element.48), channel_id=1, source_target_pairs={{0,2},{2,0},{4,6},{6,4},{8,10},{10,8},{12,14},{14,12},{16,18},{18,... | collective-permute-start | bytes 258056 | tf_op jit(solution)/shard_map/apply/ppermute | solution.py:290
  55.3 1.4 %collective-permute-done.16.refs_1_ = bf16[112,384]{1,0:T(8,128)(2,1)S(1)} collective-permute-done((bf16[112,384]{1,0:T(8,128)(2,1)S(1)}, bf16[112,384]{1,0:T(8,128)(2,1)S(1)}, u32[]{:S(2)}, u32[]{:S(2)}) %collective-permute-start.16) | collective-permute-done | bytes 86048 | tf_op jit(solution)/shard_map/apply/ppermute | solution.py:290
  58.9 1.1 %apply.27 = (bf16[2,112,384]{2,1,0:T(8,128)(2,1)}, bf16[32,8,112]{2,1,0:T(8,128)(2,1)S(1)}) custom-call(f32[2,112,384]{2,1,0:T(8,128)S(1)} %apply.24.part, f32[2,112,384]{2,1,0:T(8,128)S(1)} %apply.26.far, f32[8,128]{1,0:T(8,128)S(1)} %get-tuple-element.30.asks, bf16[6,384,768]{2,1,0:T(8,128)(2,1)S(1)} %get-tuple-element.31.bands, ...), custom_call_target="tpu_custom_call" | custom-call | flops 33030144 | bytes 165150 | tf_op jit(solution)/shard_map/apply/pallas_call | solution.py:276
  60.0 11.3 %all_to_all.5.pieces = bf16[32,8,112]{2,1,0:T(8,128)(2,1)S(1)} all-to-all(bf16[32,8,112]{2,1,0:T(8,128)(2,1)S(1)} %get-tuple-element.51), channel_id=1, replica_groups=mesh['areal'=16,'layer'=2] {'areal','layer'}, dimensions={0} | all-to-all | bytes 114688 | tf_op jit(solution)/shard_map/project/all_to_all | solution.py:460
  (48 shorter events, 6.8 us)
Async XLA Ops:
  2.9 12.6 %collective-permute-start.1 = (bf16[240,384]{1,0:T(8,128)(2,1)S(1)}, bf16[240,384]{1,0:T(8,128)(2,1)S(1)}, u32[]{:S(2)}, u32[]{:S(2)}) collective-permute-start(bf16[240,384]{1,0:T(8,128)(2,1)S(1)} %get-tuple-element.32), channel_id=1, source_target_pairs={{0,30},{2,4},{4,2},{6,8},{8,6},{10,12},{12,10},{14,16},{16,14},{18... | collective-permute-start | bytes 552968 | tf_op jit(solution)/shard_map/apply/ppermute | solution.py:290
  9.9 8.1 %collective-permute-start.3 = (bf16[240,384]{1,0:T(8,128)(2,1)S(1)}, bf16[240,384]{1,0:T(8,128)(2,1)S(1)}, u32[]{:S(2)}, u32[]{:S(2)}) collective-permute-start(bf16[240,384]{1,0:T(8,128)(2,1)S(1)} %get-tuple-element.32), channel_id=1, source_target_pairs={{0,2},{2,0},{4,6},{6,4},{8,10},{10,8},{12,14},{14,12},{16,18},{18,... | collective-permute-start | bytes 552968 | tf_op jit(solution)/shard_map/apply/ppermute | solution.py:290
  9.9 11.9 %collective-permute-start.2 = (bf16[224,384]{1,0:T(8,128)(2,1)S(1)}, bf16[224,384]{1,0:T(8,128)(2,1)S(1)}, u32[]{:S(2)}, u32[]{:S(2)}) collective-permute-start(bf16[224,384]{1,0:T(8,128)(2,1)S(1)} %get-tuple-element.27.lam.rhs), channel_id=1, source_target_pairs={{0,16},{2,18},{4,20},{6,22},{8,24},{10,26},{12,28},{14,30},{16,0},... | collective-permute-start | bytes 516104 | tf_op jit(solution)/shard_map/plan/ppermute | solution.py:290
  10.0 14.8 %collective-permute-start = (bf16[240,384]{1,0:T(8,128)(2,1)S(1)}, bf16[240,384]{1,0:T(8,128)(2,1)S(1)}, u32[]{:S(2)}, u32[]{:S(2)}) collective-permute-start(bf16[240,384]{1,0:T(8,128)(2,1)S(1)} %get-tuple-element.32), channel_id=1, source_target_pairs={{0,28},{2,30},{4,8},{6,10},{8,4},{10,6},{12,16},{14,18},{16,12},{1... | collective-permute-start | bytes 552968 | tf_op jit(solution)/shard_map/apply/ppermute | solution.py:290
  12.3 14.9 %collective-permute-start.5 = (bf16[240,384]{1,0:T(8,128)(2,1)S(1)}, bf16[240,384]{1,0:T(8,128)(2,1)S(1)}, u32[]{:S(2)}, u32[]{:S(2)}) collective-permute-start(bf16[240,384]{1,0:T(8,128)(2,1)S(1)} %get-tuple-element.32), channel_id=1, source_target_pairs={{0,4},{2,6},{4,0},{6,2},{8,12},{10,14},{12,8},{14,10},{16,20},{18,... | collective-permute-start | bytes 552968 | tf_op jit(solution)/shard_map/apply/ppermute | solution.py:290
  15.5 11.7 %collective-permute-start.6 = (bf16[240,384]{1,0:T(8,128)(2,1)S(1)}, bf16[240,384]{1,0:T(8,128)(2,1)S(1)}, u32[]{:S(2)}, u32[]{:S(2)}) collective-permute-start(bf16[240,384]{1,0:T(8,128)(2,1)S(1)} %get-tuple-element.32), channel_id=1, source_target_pairs={{0,1},{1,0},{2,3},{3,2},{4,5},{5,4},{6,7},{7,6},{8,9},{9,8},{10,11... | collective-permute-start | bytes 552968 | tf_op jit(solution)/shard_map/apply/ppermute | solution.py:300
  21.8 5.0 %collective-permute-start.4 = (bf16[112,384]{1,0:T(8,128)(2,1)S(1)}, bf16[112,384]{1,0:T(8,128)(2,1)S(1)}, u32[]{:S(2)}, u32[]{:S(2)}) collective-permute-start(bf16[112,384]{1,0:T(8,128)(2,1)S(1)} %apply.17), channel_id=1, source_target_pairs={{0,30},{2,0},{4,2},{6,4},{8,6},{10,8},{12,10},{14,12},{16,14},{18,... | collective-permute-start | bytes 258056 | tf_op jit(solution)/shard_map/apply/ppermute | solution.py:290
  24.8 4.6 %collective-permute-start.7 = (f32[8,128]{1,0:T(8,128)S(1)}, f32[8,128]{1,0:T(8,128)S(1)}, u32[]{:S(2)}, u32[]{:S(2)}) collective-permute-start(f32[8,128]{1,0:T(8,128)S(1)} %apply.16.relayed), channel_id=1, source_target_pairs={{0,16},{2,18},{4,20},{6,22},{8,24},{10,26},{12,28},{14,30},{16,0},... | collective-permute-start | bytes 12296 | tf_op jit(solution)/shard_map/apply/ppermute | solution.py:290
  29.9 9.9 %collective-permute-start.8 = (bf16[112,384]{1,0:T(8,128)(2,1)S(1)}, bf16[112,384]{1,0:T(8,128)(2,1)S(1)}, u32[]{:S(2)}, u32[]{:S(2)}) collective-permute-start(bf16[112,384]{1,0:T(8,128)(2,1)S(1)} %get-tuple-element.34), channel_id=1, source_target_pairs={{0,28},{2,30},{4,8},{6,10},{8,4},{10,6},{12,16},{14,18},{16,12},{1... | collective-permute-start | bytes 258056 | tf_op jit(solution)/shard_map/apply/ppermute | solution.py:290
  32.6 8.8 %collective-permute-start.9 = (bf16[112,384]{1,0:T(8,128)(2,1)S(1)}, bf16[112,384]{1,0:T(8,128)(2,1)S(1)}, u32[]{:S(2)}, u32[]{:S(2)}) collective-permute-start(bf16[112,384]{1,0:T(8,128)(2,1)S(1)} %get-tuple-element.35), channel_id=1, source_target_pairs={{0,30},{2,4},{4,2},{6,8},{8,6},{10,12},{12,10},{14,16},{16,14},{18... | collective-permute-start | bytes 258056 | tf_op jit(solution)/shard_map/apply/ppermute | solution.py:290
  33.9 8.8 %collective-permute-start.10 = (bf16[112,384]{1,0:T(8,128)(2,1)S(1)}, bf16[112,384]{1,0:T(8,128)(2,1)S(1)}, u32[]{:S(2)}, u32[]{:S(2)}) collective-permute-start(bf16[112,384]{1,0:T(8,128)(2,1)S(1)} %get-tuple-element.36), channel_id=1, source_target_pairs={{0,14},{2,16},{4,18},{6,20},{8,22},{10,24},{12,26},{14,28},{16,30}... | collective-permute-start | bytes 258056 | tf_op jit(solution)/shard_map/apply/ppermute | solution.py:290
  34.0 9.0 %collective-permute-start.11 = (bf16[112,384]{1,0:T(8,128)(2,1)S(1)}, bf16[112,384]{1,0:T(8,128)(2,1)S(1)}, u32[]{:S(2)}, u32[]{:S(2)}) collective-permute-start(bf16[112,384]{1,0:T(8,128)(2,1)S(1)} %get-tuple-element.37), channel_id=1, source_target_pairs={{0,16},{2,18},{4,20},{6,22},{8,24},{10,26},{12,28},{14,30},{16,0},... | collective-permute-start | bytes 258056 | tf_op jit(solution)/shard_map/apply/ppermute | solution.py:290
  38.8 4.7 %collective-permute-start.12 = (bf16[112,384]{1,0:T(8,128)(2,1)S(1)}, bf16[112,384]{1,0:T(8,128)(2,1)S(1)}, u32[]{:S(2)}, u32[]{:S(2)}) collective-permute-start(bf16[112,384]{1,0:T(8,128)(2,1)S(1)} %get-tuple-element.38), channel_id=1, source_target_pairs={{0,4},{2,6},{4,0},{6,2},{8,12},{10,14},{12,8},{14,10},{16,20},{18,... | collective-permute-start | bytes 258056 | tf_op jit(solution)/shard_map/apply/ppermute | solution.py:290
  39.8 4.5 %collective-permute-start.13 = (bf16[112,384]{1,0:T(8,128)(2,1)S(1)}, bf16[112,384]{1,0:T(8,128)(2,1)S(1)}, u32[]{:S(2)}, u32[]{:S(2)}) collective-permute-start(bf16[112,384]{1,0:T(8,128)(2,1)S(1)} %get-tuple-element.39), channel_id=1, source_target_pairs={{0,2},{2,0},{4,6},{6,4},{8,10},{10,8},{12,14},{14,12},{16,18},{18,... | collective-permute-start | bytes 258056 | tf_op jit(solution)/shard_map/apply/ppermute | solution.py:290
  41.4 2.9 %collective-permute-start.14 = (bf16[112,384]{1,0:T(8,128)(2,1)S(1)}, bf16[112,384]{1,0:T(8,128)(2,1)S(1)}, u32[]{:S(2)}, u32[]{:S(2)}) collective-permute-start(bf16[112,384]{1,0:T(8,128)(2,1)S(1)} %get-tuple-element.40), channel_id=1, source_target_pairs={{0,1},{1,0},{2,3},{3,2},{4,5},{5,4},{6,7},{7,6},{8,9},{9,8},{10,11... | collective-permute-start | bytes 258056 | tf_op jit(solution)/shard_map/apply/ppermute | solution.py:300
  43.4 13.4 %copy-start.1 = (f32[1,2,3,128]{3,1,2,0:T(2,128)S(1)}, f32[1,2,3,128]{3,1,2,0:T(2,128)}, u32[]{:S(2)}) copy-start(f32[1,2,3,128]{3,1,2,0:T(2,128)} %param.18) | copy-start | bytes 9220
  43.4 13.4 %copy-start.2 = (s32[1,2,4]{2,1,0:T(2,128)S(1)}, s32[1,2,4]{2,1,0:T(2,128)}, u32[]{:S(2)}) copy-start(s32[1,2,4]{2,1,0:T(2,128)} %param.16) | copy-start | bytes 100
  44.8 9.2 %collective-permute-start.15 = (bf16[112,384]{1,0:T(8,128)(2,1)S(1)}, bf16[112,384]{1,0:T(8,128)(2,1)S(1)}, u32[]{:S(2)}, u32[]{:S(2)}) collective-permute-start(bf16[112,384]{1,0:T(8,128)(2,1)S(1)} %get-tuple-element.43), channel_id=1, source_target_pairs={{0,28},{2,30},{4,8},{6,10},{8,4},{10,6},{12,16},{14,18},{16,12},{1... | collective-permute-start | bytes 258056 | tf_op jit(solution)/shard_map/apply/ppermute | solution.py:290
  47.7 9.0 %collective-permute-start.16 = (bf16[112,384]{1,0:T(8,128)(2,1)S(1)}, bf16[112,384]{1,0:T(8,128)(2,1)S(1)}, u32[]{:S(2)}, u32[]{:S(2)}) collective-permute-start(bf16[112,384]{1,0:T(8,128)(2,1)S(1)} %get-tuple-element.44), channel_id=1, source_target_pairs={{0,30},{2,4},{4,2},{6,8},{8,6},{10,12},{12,10},{14,16},{16,14},{18... | collective-permute-start | bytes 258056 | tf_op jit(solution)/shard_map/apply/ppermute | solution.py:290
  50.4 8.2 %collective-permute-start.17 = (bf16[112,384]{1,0:T(8,128)(2,1)S(1)}, bf16[112,384]{1,0:T(8,128)(2,1)S(1)}, u32[]{:S(2)}, u32[]{:S(2)}) collective-permute-start(bf16[112,384]{1,0:T(8,128)(2,1)S(1)} %get-tuple-element.45), channel_id=1, source_target_pairs={{0,14},{2,16},{4,18},{6,20},{8,22},{10,24},{12,26},{14,28},{16,30}... | collective-permute-start | bytes 258056 | tf_op jit(solution)/shard_map/apply/ppermute | solution.py:290
  50.4 8.2 %collective-permute-start.18 = (bf16[112,384]{1,0:T(8,128)(2,1)S(1)}, bf16[112,384]{1,0:T(8,128)(2,1)S(1)}, u32[]{:S(2)}, u32[]{:S(2)}) collective-permute-start(bf16[112,384]{1,0:T(8,128)(2,1)S(1)} %get-tuple-element.46), channel_id=1, source_target_pairs={{0,16},{2,18},{4,20},{6,22},{8,24},{10,26},{12,28},{14,30},{16,0},... | collective-permute-start | bytes 258056 | tf_op jit(solution)/shard_map/apply/ppermute | solution.py:290
  53.9 5.0 %collective-permute-start.19 = (bf16[112,384]{1,0:T(8,128)(2,1)S(1)}, bf16[112,384]{1,0:T(8,128)(2,1)S(1)}, u32[]{:S(2)}, u32[]{:S(2)}) collective-permute-start(bf16[112,384]{1,0:T(8,128)(2,1)S(1)} %get-tuple-element.47), channel_id=1, source_target_pairs={{0,4},{2,6},{4,0},{6,2},{8,12},{10,14},{12,8},{14,10},{16,20},{18,... | collective-permute-start | bytes 258056 | tf_op jit(solution)/shard_map/apply/ppermute | solution.py:290
  53.9 5.0 %collective-permute-start.20 = (bf16[112,384]{1,0:T(8,128)(2,1)S(1)}, bf16[112,384]{1,0:T(8,128)(2,1)S(1)}, u32[]{:S(2)}, u32[]{:S(2)}) collective-permute-start(bf16[112,384]{1,0:T(8,128)(2,1)S(1)} %get-tuple-element.48), channel_id=1, source_target_pairs={{0,2},{2,0},{4,6},{6,4},{8,10},{10,8},{12,14},{14,12},{16,18},{18,... | collective-permute-start | bytes 258056 | tf_op jit(solution)/shard_map/apply/ppermute | solution.py:290
  56.7 2.2 %collective-permute-start.21 = (bf16[112,384]{1,0:T(8,128)(2,1)S(1)}, bf16[112,384]{1,0:T(8,128)(2,1)S(1)}, u32[]{:S(2)}, u32[]{:S(2)}) collective-permute-start(bf16[112,384]{1,0:T(8,128)(2,1)S(1)} %get-tuple-element.49), channel_id=1, source_target_pairs={{0,1},{1,0},{2,3},{3,2},{4,5},{5,4},{6,7},{7,6},{8,9},{9,8},{10,11... | collective-permute-start | bytes 258056 | tf_op jit(solution)/shard_map/apply/ppermute | solution.py:300
  (2 other events, 26.7 us)

commit v2 on v1

--- a/solution.py
+++ b/solution.py
@@ -187,6 +187,16 @@
 def cross_kernel(asks, bands, *refs):
     arrived, out = refs[:-1], refs[-1]
     out[0], out[1] = source_sums(asks, bands, 0, arrived, out.shape[1])
+
+
+def nearer_kernel(asks, bands, pair, out):
+    out[0], out[1] = source_sums(asks, bands, bands.shape[0] - 1, [pair], out.shape[1])
+
+
+def farther_kernel(asks, bands, cross, nearer, passed, out):
+    sums = source_sums(asks, bands, bands.shape[0] - 2, [passed], out.shape[1])
+    for d in range(2):
+        out[d] = cross[d] + nearer[d] + sums[d]
 
 
 def far_kernel(asks, bands, cross, *refs):
@@ -420,13 +430,29 @@
                 [VMEM] * (2 + half),
                 flops=4 * one,
             )
-            (far,) = call(
-                far_kernel,
-                [sums],
-                (asks, bands, held(cross), *arrived[-2:]),
-                [VMEM] * 5,
-                flops=4 * one,
-            )
+            if first:
+                (far,) = call(
+                    far_kernel,
+                    [sums],
+                    (asks, bands, held(cross), *arrived[-2:]),
+                    [VMEM] * 5,
+                    flops=4 * one,
+                )
+            else:
+                (nearer,) = call(
+                    nearer_kernel,
+                    [sums],
+                    (asks, bands, arrived[-1]),
+                    [VMEM] * 3,
+                    flops=64 * one,
+                )
+                (far,) = call(
+                    farther_kernel,
+                    [sums],
+                    (asks, bands, held(cross), held(nearer), arrived[-2]),
+                    [VMEM] * 5,
+                    flops=4 * one,
+                )
             tiles = (part, held(far), asks, bands, sides)
             near = (*arrived[half:-2], *beside)
             if step < ITERS - 1:

time: 72.3 us -> 72.6 us (level)
  waiting for transfers between devices: 15.1 us -> 16.3 us
    ppermute x19, waiting for transfers between devices: 15.1 us -> 16.3 us  [moved_by(): return held(lax.ppermute(x, 'areal', pairs))]
    ppermute x19, starting transfers between devices: 34 us -> 33.2 us  [moved_by(): return held(lax.ppermute(x, 'areal', pairs))]
    pallas_call x19 -> x21, Pallas kernels: 10.1 us -> 10.5 us  [call(): pl.pallas_call(kernel, out_shape=outs, in_specs=specs, out_specs=out_spec...]
  transfers between devices with their start and end apart: 22 -> 22, of which waited for: 10 -> 9; matrix products, arithmetic and copies ran while one was open for 0% -> 0% of each run, Pallas kernels for 8% -> 8%
where the time goes in v2:
time: 72.6 us
  starting transfers between devices  33.3 us (46%)
  waiting for transfers between devices  16.3 us (22%)
  blocking collectives  10.9 us (15%)
  Pallas kernels  10.5 us (14%)
  between operations  1.57 us (2%)
    ppermute x19, starting transfers between devices, moved_by(): return held(lax.ppermute(x, 'areal', pairs))  33.2 us
    ppermute x19, waiting for transfers between devices, moved_by(): return held(lax.ppermute(x, 'areal', pairs))  16.3 us
    all_to_all x1, blocking collectives, on_device(): landed = lax.all_to_all(pieces, ('areal', 'layer'), 0, 0, tiled=True)  10.9 us
    pallas_call x21, Pallas kernels, call(): pl.pallas_call(kernel, out_shape=outs, in_specs=specs, out_specs=out_spec...  10.5 us
  transfers between devices with their start and end apart: 22, of which 9 were waited for; matrix products, arithmetic and copies ran while one was open for 0% of the time, Pallas kernels for 8%

profile of v2, /device:TPU:0, one launch (start us, length us, event | category | flops | bytes accessed | tf_op | source)
XLA Modules:
  0.0 72.6 jit_solution(2972918801467879498)
XLA Ops:
  1.3 1.6 %plan.1 = (s32[12]{0:T(128)S(1)}, f32[8,128]{1,0:T(8,128)S(1)}, bf16[240,384]{1,0:T(8,128)(2,1)S(1)}, bf16[224,384]{1,0:T(8,128)(2,1)S(1)}) custom-call(s32[6]{0:T(128)} %bitcast.24, s32[1]{0:T(128)} %bitcast.15.count, s32[32]{0:T(128)} %tile_map.1, s32[1]{0:T(128)} %bitcast.2.me, s32[1]{0:T(128)} %bitcast.3.group, bf16[224,384]{1,0:T(8,128)(2,1)} %bitcast.22), custom_call_target="tpu_custom_call" | custom-call | tf_op jit(solution)/shard_map/plan/pallas_call | solution.py:286
  2.9 7.0 %collective-permute-start.1 = (bf16[240,384]{1,0:T(8,128)(2,1)S(1)}, bf16[240,384]{1,0:T(8,128)(2,1)S(1)}, u32[]{:S(2)}, u32[]{:S(2)}) collective-permute-start(bf16[240,384]{1,0:T(8,128)(2,1)S(1)} %get-tuple-element.32), channel_id=1, source_target_pairs={{0,30},{2,4},{4,2},{6,8},{8,6},{10,12},{12,10},{14,16},{16,14},{18... | collective-permute-start | bytes 552968 | tf_op jit(solution)/shard_map/apply/ppermute | solution.py:300
  10.0 2.3 %collective-permute-start = (bf16[240,384]{1,0:T(8,128)(2,1)S(1)}, bf16[240,384]{1,0:T(8,128)(2,1)S(1)}, u32[]{:S(2)}, u32[]{:S(2)}) collective-permute-start(bf16[240,384]{1,0:T(8,128)(2,1)S(1)} %get-tuple-element.32), channel_id=1, source_target_pairs={{0,28},{2,30},{4,8},{6,10},{8,4},{10,6},{12,16},{14,18},{16,12},{1... | collective-permute-start | bytes 552968 | tf_op jit(solution)/shard_map/apply/ppermute | solution.py:300
  13.0 2.5 %collective-permute-done.1.refs_1_.even.refs_4_ = bf16[240,384]{1,0:T(8,128)(2,1)S(1)} collective-permute-done((bf16[240,384]{1,0:T(8,128)(2,1)S(1)}, bf16[240,384]{1,0:T(8,128)(2,1)S(1)}, u32[]{:S(2)}, u32[]{:S(2)}) %collective-permute-start.1) | collective-permute-done | bytes 184352 | tf_op jit(solution)/shard_map/apply/ppermute | solution.py:300
  15.5 2.2 %load.3 = (bf16[6,384,768]{2,1,0:T(8,128)(2,1)S(1)}, bf16[3,384,384]{2,1,0:T(8,128)(2,1)S(1)}) custom-call(s32[12]{0:T(128)S(1)} %get-tuple-element.28.table, s32[1]{0:T(128)} %bitcast.3.group, bf16[2,6,384,384]{3,2,1,0:T(8,128)(2,1)} %bitcast.20, bf16[2,2,384,384]{3,2,1,0:T(8,128)(2,1)} %bitcast.21), custom_call_target="tpu_custom_call" | custom-call | bytes 4718592 | tf_op jit(solution)/shard_map/load/pallas_call | solution.py:286
  18.0 3.8 %collective-permute-done.2.pair.refs_1_ = bf16[224,384]{1,0:T(8,128)(2,1)S(1)} collective-permute-done((bf16[224,384]{1,0:T(8,128)(2,1)S(1)}, bf16[224,384]{1,0:T(8,128)(2,1)S(1)}, u32[]{:S(2)}, u32[]{:S(2)}) %collective-permute-start.2) | collective-permute-done | bytes 172064 | tf_op jit(solution)/shard_map/plan/ppermute | solution.py:300
  21.8 2.9 %collective-permute-start.4 = (bf16[112,384]{1,0:T(8,128)(2,1)S(1)}, bf16[112,384]{1,0:T(8,128)(2,1)S(1)}, u32[]{:S(2)}, u32[]{:S(2)}) collective-permute-start(bf16[112,384]{1,0:T(8,128)(2,1)S(1)} %apply.19), channel_id=1, source_target_pairs={{0,30},{2,0},{4,2},{6,4},{8,6},{10,8},{12,10},{14,12},{16,14},{18,... | collective-permute-start | bytes 258056 | tf_op jit(solution)/shard_map/apply/ppermute | solution.py:300
  25.1 2.1 %collective-permute-done.4.refs_0_ = bf16[112,384]{1,0:T(8,128)(2,1)S(1)} collective-permute-done((bf16[112,384]{1,0:T(8,128)(2,1)S(1)}, bf16[112,384]{1,0:T(8,128)(2,1)S(1)}, u32[]{:S(2)}, u32[]{:S(2)}) %collective-permute-start.4) | collective-permute-done | bytes 86048 | tf_op jit(solution)/shard_map/apply/ppermute | solution.py:300
  27.6 1.8 %collective-permute-done.7.refs_7_ = f32[8,128]{1,0:T(8,128)S(1)} collective-permute-done((f32[8,128]{1,0:T(8,128)S(1)}, f32[8,128]{1,0:T(8,128)S(1)}, u32[]{:S(2)}, u32[]{:S(2)}) %collective-permute-start.7) | collective-permute-done | bytes 4128 | tf_op jit(solution)/shard_map/apply/ppermute | solution.py:300
  29.9 1.3 %collective-permute-start.10 = (bf16[112,384]{1,0:T(8,128)(2,1)S(1)}, bf16[112,384]{1,0:T(8,128)(2,1)S(1)}, u32[]{:S(2)}, u32[]{:S(2)}) collective-permute-start(bf16[112,384]{1,0:T(8,128)(2,1)S(1)} %get-tuple-element.36), channel_id=1, source_target_pairs={{0,16},{2,18},{4,20},{6,22},{8,24},{10,26},{12,28},{14,30},{16,0},... | collective-permute-start | bytes 258056 | tf_op jit(solution)/shard_map/apply/ppermute | solution.py:300
  31.2 1.5 %collective-permute-start.8 = (bf16[112,384]{1,0:T(8,128)(2,1)S(1)}, bf16[112,384]{1,0:T(8,128)(2,1)S(1)}, u32[]{:S(2)}, u32[]{:S(2)}) collective-permute-start(bf16[112,384]{1,0:T(8,128)(2,1)S(1)} %get-tuple-element.34), channel_id=1, source_target_pairs={{0,28},{2,30},{4,8},{6,10},{8,4},{10,6},{12,16},{14,18},{16,12},{1... | collective-permute-start | bytes 258056 | tf_op jit(solution)/shard_map/apply/ppermute | solution.py:300
  32.6 1.7 %collective-permute-start.9 = (bf16[112,384]{1,0:T(8,128)(2,1)S(1)}, bf16[112,384]{1,0:T(8,128)(2,1)S(1)}, u32[]{:S(2)}, u32[]{:S(2)}) collective-permute-start(bf16[112,384]{1,0:T(8,128)(2,1)S(1)} %get-tuple-element.35), channel_id=1, source_target_pairs={{0,30},{2,4},{4,2},{6,8},{8,6},{10,12},{12,10},{14,16},{16,14},{18... | collective-permute-start | bytes 258056 | tf_op jit(solution)/shard_map/apply/ppermute | solution.py:300
  34.4 2.6 %collective-permute-start.11 = (bf16[112,384]{1,0:T(8,128)(2,1)S(1)}, bf16[112,384]{1,0:T(8,128)(2,1)S(1)}, u32[]{:S(2)}, u32[]{:S(2)}) collective-permute-start(bf16[112,384]{1,0:T(8,128)(2,1)S(1)} %get-tuple-element.37), channel_id=1, source_target_pairs={{0,14},{2,16},{4,18},{6,20},{8,22},{10,24},{12,26},{14,28},{16,30}... | collective-permute-start | bytes 258056 | tf_op jit(solution)/shard_map/apply/ppermute | solution.py:300
  37.0 2.8 %collective-permute-start.12 = (bf16[112,384]{1,0:T(8,128)(2,1)S(1)}, bf16[112,384]{1,0:T(8,128)(2,1)S(1)}, u32[]{:S(2)}, u32[]{:S(2)}) collective-permute-start(bf16[112,384]{1,0:T(8,128)(2,1)S(1)} %get-tuple-element.38), channel_id=1, source_target_pairs={{0,4},{2,6},{4,0},{6,2},{8,12},{10,14},{12,8},{14,10},{16,20},{18,... | collective-permute-start | bytes 258056 | tf_op jit(solution)/shard_map/apply/ppermute | solution.py:300
  40.5 0.9 %collective-permute-done.9.refs_1_ = bf16[112,384]{1,0:T(8,128)(2,1)S(1)} collective-permute-done((bf16[112,384]{1,0:T(8,128)(2,1)S(1)}, bf16[112,384]{1,0:T(8,128)(2,1)S(1)}, u32[]{:S(2)}, u32[]{:S(2)}) %collective-permute-start.9) | collective-permute-done | bytes 86048 | tf_op jit(solution)/shard_map/apply/ppermute | solution.py:300
  42.7 1.9 %collective-permute-done.13.refs_1_ = bf16[112,384]{1,0:T(8,128)(2,1)S(1)} collective-permute-done((bf16[112,384]{1,0:T(8,128)(2,1)S(1)}, bf16[112,384]{1,0:T(8,128)(2,1)S(1)}, u32[]{:S(2)}, u32[]{:S(2)}) %collective-permute-start.13) | collective-permute-done | bytes 86048 | tf_op jit(solution)/shard_map/apply/ppermute | solution.py:300
  45.1 2.6 %collective-permute-start.17 = (bf16[112,384]{1,0:T(8,128)(2,1)S(1)}, bf16[112,384]{1,0:T(8,128)(2,1)S(1)}, u32[]{:S(2)}, u32[]{:S(2)}) collective-permute-start(bf16[112,384]{1,0:T(8,128)(2,1)S(1)} %get-tuple-element.45), channel_id=1, source_target_pairs={{0,16},{2,18},{4,20},{6,22},{8,24},{10,26},{12,28},{14,30},{16,0},... | collective-permute-start | bytes 258056 | tf_op jit(solution)/shard_map/apply/ppermute | solution.py:300
  47.7 1.9 %collective-permute-start.15 = (bf16[112,384]{1,0:T(8,128)(2,1)S(1)}, bf16[112,384]{1,0:T(8,128)(2,1)S(1)}, u32[]{:S(2)}, u32[]{:S(2)}) collective-permute-start(bf16[112,384]{1,0:T(8,128)(2,1)S(1)} %get-tuple-element.43), channel_id=1, source_target_pairs={{0,28},{2,30},{4,8},{6,10},{8,4},{10,6},{12,16},{14,18},{16,12},{1... | collective-permute-start | bytes 258056 | tf_op jit(solution)/shard_map/apply/ppermute | solution.py:300
  50.3 1.9 %collective-permute-start.16 = (bf16[112,384]{1,0:T(8,128)(2,1)S(1)}, bf16[112,384]{1,0:T(8,128)(2,1)S(1)}, u32[]{:S(2)}, u32[]{:S(2)}) collective-permute-start(bf16[112,384]{1,0:T(8,128)(2,1)S(1)} %get-tuple-element.44), channel_id=1, source_target_pairs={{0,30},{2,4},{4,2},{6,8},{8,6},{10,12},{12,10},{14,16},{16,14},{18... | collective-permute-start | bytes 258056 | tf_op jit(solution)/shard_map/apply/ppermute | solution.py:300
  52.3 2.5 %collective-permute-start.18 = (bf16[112,384]{1,0:T(8,128)(2,1)S(1)}, bf16[112,384]{1,0:T(8,128)(2,1)S(1)}, u32[]{:S(2)}, u32[]{:S(2)}) collective-permute-start(bf16[112,384]{1,0:T(8,128)(2,1)S(1)} %get-tuple-element.46), channel_id=1, source_target_pairs={{0,14},{2,16},{4,18},{6,20},{8,22},{10,24},{12,26},{14,28},{16,30}... | collective-permute-start | bytes 258056 | tf_op jit(solution)/shard_map/apply/ppermute | solution.py:300
  55.1 1.2 %collective-permute-start.20 = (bf16[112,384]{1,0:T(8,128)(2,1)S(1)}, bf16[112,384]{1,0:T(8,128)(2,1)S(1)}, u32[]{:S(2)}, u32[]{:S(2)}) collective-permute-start(bf16[112,384]{1,0:T(8,128)(2,1)S(1)} %get-tuple-element.48), channel_id=1, source_target_pairs={{0,2},{2,0},{4,6},{6,4},{8,10},{10,8},{12,14},{14,12},{16,18},{18,... | collective-permute-start | bytes 258056 | tf_op jit(solution)/shard_map/apply/ppermute | solution.py:300
  56.6 2.0 %collective-permute-done.16.refs_1_ = bf16[112,384]{1,0:T(8,128)(2,1)S(1)} collective-permute-done((bf16[112,384]{1,0:T(8,128)(2,1)S(1)}, bf16[112,384]{1,0:T(8,128)(2,1)S(1)}, u32[]{:S(2)}, u32[]{:S(2)}) %collective-permute-start.16) | collective-permute-done | bytes 86048 | tf_op jit(solution)/shard_map/apply/ppermute | solution.py:300
  59.9 1.1 %apply.31 = (bf16[2,112,384]{2,1,0:T(8,128)(2,1)}, bf16[32,8,112]{2,1,0:T(8,128)(2,1)S(1)}) custom-call(f32[2,112,384]{2,1,0:T(8,128)S(1)} %apply.27.part, f32[2,112,384]{2,1,0:T(8,128)S(1)} %apply.30.far, f32[8,128]{1,0:T(8,128)S(1)} %get-tuple-element.30.asks, bf16[6,384,768]{2,1,0:T(8,128)(2,1)S(1)} %get-tuple-element.31.bands, ...), custom_call_target="tpu_custom_call" | custom-call | flops 33030144 | bytes 165150 | tf_op jit(solution)/shard_map/apply/pallas_call | solution.py:286
  61.0 10.9 %all_to_all.5.pieces = bf16[32,8,112]{2,1,0:T(8,128)(2,1)S(1)} all-to-all(bf16[32,8,112]{2,1,0:T(8,128)(2,1)S(1)} %get-tuple-element.51), channel_id=1, replica_groups=mesh['areal'=16,'layer'=2] {'areal','layer'}, dimensions={0} | all-to-all | bytes 114688 | tf_op jit(solution)/shard_map/project/all_to_all | solution.py:486
  (50 shorter events, 7.9 us)
Async XLA Ops:
  2.9 12.6 %collective-permute-start.1 = (bf16[240,384]{1,0:T(8,128)(2,1)S(1)}, bf16[240,384]{1,0:T(8,128)(2,1)S(1)}, u32[]{:S(2)}, u32[]{:S(2)}) collective-permute-start(bf16[240,384]{1,0:T(8,128)(2,1)S(1)} %get-tuple-element.32), channel_id=1, source_target_pairs={{0,30},{2,4},{4,2},{6,8},{8,6},{10,12},{12,10},{14,16},{16,14},{18... | collective-permute-start | bytes 552968 | tf_op jit(solution)/shard_map/apply/ppermute | solution.py:300
  9.9 8.1 %collective-permute-start.3 = (bf16[240,384]{1,0:T(8,128)(2,1)S(1)}, bf16[240,384]{1,0:T(8,128)(2,1)S(1)}, u32[]{:S(2)}, u32[]{:S(2)}) collective-permute-start(bf16[240,384]{1,0:T(8,128)(2,1)S(1)} %get-tuple-element.32), channel_id=1, source_target_pairs={{0,2},{2,0},{4,6},{6,4},{8,10},{10,8},{12,14},{14,12},{16,18},{18,... | collective-permute-start | bytes 552968 | tf_op jit(solution)/shard_map/apply/ppermute | solution.py:300
  9.9 11.9 %collective-permute-start.2 = (bf16[224,384]{1,0:T(8,128)(2,1)S(1)}, bf16[224,384]{1,0:T(8,128)(2,1)S(1)}, u32[]{:S(2)}, u32[]{:S(2)}) collective-permute-start(bf16[224,384]{1,0:T(8,128)(2,1)S(1)} %get-tuple-element.27.lam.rhs), channel_id=1, source_target_pairs={{0,16},{2,18},{4,20},{6,22},{8,24},{10,26},{12,28},{14,30},{16,0},... | collective-permute-start | bytes 516104 | tf_op jit(solution)/shard_map/plan/ppermute | solution.py:300
  10.0 14.8 %collective-permute-start = (bf16[240,384]{1,0:T(8,128)(2,1)S(1)}, bf16[240,384]{1,0:T(8,128)(2,1)S(1)}, u32[]{:S(2)}, u32[]{:S(2)}) collective-permute-start(bf16[240,384]{1,0:T(8,128)(2,1)S(1)} %get-tuple-element.32), channel_id=1, source_target_pairs={{0,28},{2,30},{4,8},{6,10},{8,4},{10,6},{12,16},{14,18},{16,12},{1... | collective-permute-start | bytes 552968 | tf_op jit(solution)/shard_map/apply/ppermute | solution.py:300
  12.3 15.3 %collective-permute-start.5 = (bf16[240,384]{1,0:T(8,128)(2,1)S(1)}, bf16[240,384]{1,0:T(8,128)(2,1)S(1)}, u32[]{:S(2)}, u32[]{:S(2)}) collective-permute-start(bf16[240,384]{1,0:T(8,128)(2,1)S(1)} %get-tuple-element.32), channel_id=1, source_target_pairs={{0,4},{2,6},{4,0},{6,2},{8,12},{10,14},{12,8},{14,10},{16,20},{18,... | collective-permute-start | bytes 552968 | tf_op jit(solution)/shard_map/apply/ppermute | solution.py:300
  15.5 12.1 %collective-permute-start.6 = (bf16[240,384]{1,0:T(8,128)(2,1)S(1)}, bf16[240,384]{1,0:T(8,128)(2,1)S(1)}, u32[]{:S(2)}, u32[]{:S(2)}) collective-permute-start(bf16[240,384]{1,0:T(8,128)(2,1)S(1)} %get-tuple-element.32), channel_id=1, source_target_pairs={{0,1},{1,0},{2,3},{3,2},{4,5},{5,4},{6,7},{7,6},{8,9},{9,8},{10,11... | collective-permute-start | bytes 552968 | tf_op jit(solution)/shard_map/apply/ppermute | solution.py:310
  21.8 5.4 %collective-permute-start.4 = (bf16[112,384]{1,0:T(8,128)(2,1)S(1)}, bf16[112,384]{1,0:T(8,128)(2,1)S(1)}, u32[]{:S(2)}, u32[]{:S(2)}) collective-permute-start(bf16[112,384]{1,0:T(8,128)(2,1)S(1)} %apply.19), channel_id=1, source_target_pairs={{0,30},{2,0},{4,2},{6,4},{8,6},{10,8},{12,10},{14,12},{16,14},{18,... | collective-permute-start | bytes 258056 | tf_op jit(solution)/shard_map/apply/ppermute | solution.py:300
  24.8 4.6 %collective-permute-start.7 = (f32[8,128]{1,0:T(8,128)S(1)}, f32[8,128]{1,0:T(8,128)S(1)}, u32[]{:S(2)}, u32[]{:S(2)}) collective-permute-start(f32[8,128]{1,0:T(8,128)S(1)} %apply.18.relayed), channel_id=1, source_target_pairs={{0,16},{2,18},{4,20},{6,22},{8,24},{10,26},{12,28},{14,30},{16,0},... | collective-permute-start | bytes 12296 | tf_op jit(solution)/shard_map/apply/ppermute | solution.py:300
  29.9 10.2 %collective-permute-start.10 = (bf16[112,384]{1,0:T(8,128)(2,1)S(1)}, bf16[112,384]{1,0:T(8,128)(2,1)S(1)}, u32[]{:S(2)}, u32[]{:S(2)}) collective-permute-start(bf16[112,384]{1,0:T(8,128)(2,1)S(1)} %get-tuple-element.36), channel_id=1, source_target_pairs={{0,16},{2,18},{4,20},{6,22},{8,24},{10,26},{12,28},{14,30},{16,0},... | collective-permute-start | bytes 258056 | tf_op jit(solution)/shard_map/apply/ppermute | solution.py:300
  31.2 9.0 %collective-permute-start.8 = (bf16[112,384]{1,0:T(8,128)(2,1)S(1)}, bf16[112,384]{1,0:T(8,128)(2,1)S(1)}, u32[]{:S(2)}, u32[]{:S(2)}) collective-permute-start(bf16[112,384]{1,0:T(8,128)(2,1)S(1)} %get-tuple-element.34), channel_id=1, source_target_pairs={{0,28},{2,30},{4,8},{6,10},{8,4},{10,6},{12,16},{14,18},{16,12},{1... | collective-permute-start | bytes 258056 | tf_op jit(solution)/shard_map/apply/ppermute | solution.py:300
  32.6 8.7 %collective-permute-start.9 = (bf16[112,384]{1,0:T(8,128)(2,1)S(1)}, bf16[112,384]{1,0:T(8,128)(2,1)S(1)}, u32[]{:S(2)}, u32[]{:S(2)}) collective-permute-start(bf16[112,384]{1,0:T(8,128)(2,1)S(1)} %get-tuple-element.35), channel_id=1, source_target_pairs={{0,30},{2,4},{4,2},{6,8},{8,6},{10,12},{12,10},{14,16},{16,14},{18... | collective-permute-start | bytes 258056 | tf_op jit(solution)/shard_map/apply/ppermute | solution.py:300
  34.4 8.0 %collective-permute-start.11 = (bf16[112,384]{1,0:T(8,128)(2,1)S(1)}, bf16[112,384]{1,0:T(8,128)(2,1)S(1)}, u32[]{:S(2)}, u32[]{:S(2)}) collective-permute-start(bf16[112,384]{1,0:T(8,128)(2,1)S(1)} %get-tuple-element.37), channel_id=1, source_target_pairs={{0,14},{2,16},{4,18},{6,20},{8,22},{10,24},{12,26},{14,28},{16,30}... | collective-permute-start | bytes 258056 | tf_op jit(solution)/shard_map/apply/ppermute | solution.py:300
  37.0 5.7 %collective-permute-start.12 = (bf16[112,384]{1,0:T(8,128)(2,1)S(1)}, bf16[112,384]{1,0:T(8,128)(2,1)S(1)}, u32[]{:S(2)}, u32[]{:S(2)}) collective-permute-start(bf16[112,384]{1,0:T(8,128)(2,1)S(1)} %get-tuple-element.38), channel_id=1, source_target_pairs={{0,4},{2,6},{4,0},{6,2},{8,12},{10,14},{12,8},{14,10},{16,20},{18,... | collective-permute-start | bytes 258056 | tf_op jit(solution)/shard_map/apply/ppermute | solution.py:300
  40.1 4.6 %collective-permute-start.13 = (bf16[112,384]{1,0:T(8,128)(2,1)S(1)}, bf16[112,384]{1,0:T(8,128)(2,1)S(1)}, u32[]{:S(2)}, u32[]{:S(2)}) collective-permute-start(bf16[112,384]{1,0:T(8,128)(2,1)S(1)} %get-tuple-element.39), channel_id=1, source_target_pairs={{0,2},{2,0},{4,6},{6,4},{8,10},{10,8},{12,14},{14,12},{16,18},{18,... | collective-permute-start | bytes 258056 | tf_op jit(solution)/shard_map/apply/ppermute | solution.py:300
  40.2 4.5 %collective-permute-start.14 = (bf16[112,384]{1,0:T(8,128)(2,1)S(1)}, bf16[112,384]{1,0:T(8,128)(2,1)S(1)}, u32[]{:S(2)}, u32[]{:S(2)}) collective-permute-start(bf16[112,384]{1,0:T(8,128)(2,1)S(1)} %get-tuple-element.40), channel_id=1, source_target_pairs={{0,1},{1,0},{2,3},{3,2},{4,5},{5,4},{6,7},{7,6},{8,9},{9,8},{10,11... | collective-permute-start | bytes 258056 | tf_op jit(solution)/shard_map/apply/ppermute | solution.py:310
  42.6 7.1 %copy-start.1 = (f32[1,2,3,128]{3,1,2,0:T(2,128)S(1)}, f32[1,2,3,128]{3,1,2,0:T(2,128)}, u32[]{:S(2)}) copy-start(f32[1,2,3,128]{3,1,2,0:T(2,128)} %param.18) | copy-start | bytes 9220
  42.6 7.1 %copy-start.2 = (s32[1,2,4]{2,1,0:T(2,128)S(1)}, s32[1,2,4]{2,1,0:T(2,128)}, u32[]{:S(2)}) copy-start(s32[1,2,4]{2,1,0:T(2,128)} %param.16) | copy-start | bytes 100
  45.1 10.0 %collective-permute-start.17 = (bf16[112,384]{1,0:T(8,128)(2,1)S(1)}, bf16[112,384]{1,0:T(8,128)(2,1)S(1)}, u32[]{:S(2)}, u32[]{:S(2)}) collective-permute-start(bf16[112,384]{1,0:T(8,128)(2,1)S(1)} %get-tuple-element.45), channel_id=1, source_target_pairs={{0,16},{2,18},{4,20},{6,22},{8,24},{10,26},{12,28},{14,30},{16,0},... | collective-permute-start | bytes 258056 | tf_op jit(solution)/shard_map/apply/ppermute | solution.py:300
  47.7 8.6 %collective-permute-start.15 = (bf16[112,384]{1,0:T(8,128)(2,1)S(1)}, bf16[112,384]{1,0:T(8,128)(2,1)S(1)}, u32[]{:S(2)}, u32[]{:S(2)}) collective-permute-start(bf16[112,384]{1,0:T(8,128)(2,1)S(1)} %get-tuple-element.43), channel_id=1, source_target_pairs={{0,28},{2,30},{4,8},{6,10},{8,4},{10,6},{12,16},{14,18},{16,12},{1... | collective-permute-start | bytes 258056 | tf_op jit(solution)/shard_map/apply/ppermute | solution.py:300
  50.3 8.3 %collective-permute-start.16 = (bf16[112,384]{1,0:T(8,128)(2,1)S(1)}, bf16[112,384]{1,0:T(8,128)(2,1)S(1)}, u32[]{:S(2)}, u32[]{:S(2)}) collective-permute-start(bf16[112,384]{1,0:T(8,128)(2,1)S(1)} %get-tuple-element.44), channel_id=1, source_target_pairs={{0,30},{2,4},{4,2},{6,8},{8,6},{10,12},{12,10},{14,16},{16,14},{18... | collective-permute-start | bytes 258056 | tf_op jit(solution)/shard_map/apply/ppermute | solution.py:300
  52.3 7.3 %collective-permute-start.18 = (bf16[112,384]{1,0:T(8,128)(2,1)S(1)}, bf16[112,384]{1,0:T(8,128)(2,1)S(1)}, u32[]{:S(2)}, u32[]{:S(2)}) collective-permute-start(bf16[112,384]{1,0:T(8,128)(2,1)S(1)} %get-tuple-element.46), channel_id=1, source_target_pairs={{0,14},{2,16},{4,18},{6,20},{8,22},{10,24},{12,26},{14,28},{16,30}... | collective-permute-start | bytes 258056 | tf_op jit(solution)/shard_map/apply/ppermute | solution.py:300
  54.7 5.1 %collective-permute-start.19 = (bf16[112,384]{1,0:T(8,128)(2,1)S(1)}, bf16[112,384]{1,0:T(8,128)(2,1)S(1)}, u32[]{:S(2)}, u32[]{:S(2)}) collective-permute-start(bf16[112,384]{1,0:T(8,128)(2,1)S(1)} %get-tuple-element.47), channel_id=1, source_target_pairs={{0,4},{2,6},{4,0},{6,2},{8,12},{10,14},{12,8},{14,10},{16,20},{18,... | collective-permute-start | bytes 258056 | tf_op jit(solution)/shard_map/apply/ppermute | solution.py:300
  55.1 4.8 %collective-permute-start.20 = (bf16[112,384]{1,0:T(8,128)(2,1)S(1)}, bf16[112,384]{1,0:T(8,128)(2,1)S(1)}, u32[]{:S(2)}, u32[]{:S(2)}) collective-permute-start(bf16[112,384]{1,0:T(8,128)(2,1)S(1)} %get-tuple-element.48), channel_id=1, source_target_pairs={{0,2},{2,0},{4,6},{6,4},{8,10},{10,8},{12,14},{14,12},{16,18},{18,... | collective-permute-start | bytes 258056 | tf_op jit(solution)/shard_map/apply/ppermute | solution.py:300
  56.3 3.5 %collective-permute-start.21 = (bf16[112,384]{1,0:T(8,128)(2,1)S(1)}, bf16[112,384]{1,0:T(8,128)(2,1)S(1)}, u32[]{:S(2)}, u32[]{:S(2)}) collective-permute-start(bf16[112,384]{1,0:T(8,128)(2,1)S(1)} %get-tuple-element.49), channel_id=1, source_target_pairs={{0,1},{1,0},{2,3},{3,2},{4,5},{5,4},{6,7},{7,6},{8,9},{9,8},{10,11... | collective-permute-start | bytes 258056 | tf_op jit(solution)/shard_map/apply/ppermute | solution.py:310
  (2 other events, 14.1 us)

commit v3 on v2

--- a/solution.py
+++ b/solution.py
@@ -153,7 +153,7 @@
     relayed[number - 2 : number - 1, :] = jnp.where(parity > 0.5, ask[1], ask[0])
 
 
-def far_pick_kernel(number, pair, relayed, part, tile):
+def far_pick_kernel(number, pair, relayed, part, factors, weights, tile):
     tile[...] = tile_of(pair, relayed[number - 2 : number - 1, :], tile.shape[0])
 
 
@@ -417,8 +417,8 @@
                 (picked,) = call(
                     partial(far_pick_kernel, number),
                     [tile],
-                    (far_pair, relayed, part),
-                    [VMEM] * 3,
+                    (far_pair, relayed, part, factors, weights),
+                    [VMEM] * 5,
                 )
                 arrived = [*arrived, moved_by(picked, shift_pairs(columns, 1)), far_pair]
                 told = [*arrived[:-2], moved_by(relayed, routes[-1])]

time: 72.6 us -> 72.8 us (level)
  waiting for transfers between devices: 16.3 us -> 11.7 us
  local copies, waits for them, and re-layouts: 0.03 us -> 2.94 us
  starting transfers between devices: 33.3 us -> 34.1 us
    ppermute x19, waiting for transfers between devices: 16.3 us -> 11.7 us  [moved_by(): return held(lax.ppermute(x, 'areal', pairs))]
    unnamed x8, local copies, waits for them, and re-layouts: 0.03 us -> 2.94 us
    ppermute x19, starting transfers between devices: 33.2 us -> 34.1 us  [moved_by(): return held(lax.ppermute(x, 'areal', pairs))]
  transfers between devices with their start and end apart: 22 -> 22, of which waited for: 9 -> 11; matrix products, arithmetic and copies ran while one was open for 0% -> 0% of each run, Pallas kernels for 8% -> 9%
where the time goes in v3:
time: 72.8 us; the launch traced here: 72.5 us
  starting transfers between devices  34.1 us (47%)
  waiting for transfers between devices  11.7 us (16%)
  Pallas kernels  11.1 us (15%)
  blocking collectives  11.1 us (15%)
  local copies, waits for them, and re-layouts  2.94 us (4%)
  between operations  1.48 us (2%)
    ppermute x19, starting transfers between devices, moved_by(): return held(lax.ppermute(x, 'areal', pairs))  34.1 us
    ppermute x19, waiting for transfers between devices, moved_by(): return held(lax.ppermute(x, 'areal', pairs))  11.7 us
    pallas_call x21, Pallas kernels, call(): pl.pallas_call(kernel, out_shape=outs, in_specs=specs, out_specs=out_spec...  11.1 us
    all_to_all x1, blocking collectives, on_device(): landed = lax.all_to_all(pieces, ('areal', 'layer'), 0, 0, tiled=True)  11.1 us
    unnamed x8, local copies, waits for them, and re-layouts  2.94 us
  transfers between devices with their start and end apart: 22, of which 11 were waited for; matrix products, arithmetic and copies ran while one was open for 0% of the time, Pallas kernels for 9%

profile of v3, /device:TPU:0, one launch (start us, length us, event | category | flops | bytes accessed | tf_op | source)
XLA Modules:
  0.0 72.5 jit_solution(1605484374606740116)
XLA Ops:
  1.3 1.6 %plan.1 = (s32[12]{0:T(128)S(1)}, f32[8,128]{1,0:T(8,128)S(1)}, bf16[240,384]{1,0:T(8,128)(2,1)S(1)}, bf16[224,384]{1,0:T(8,128)(2,1)S(1)}) custom-call(s32[6]{0:T(128)} %bitcast.24, s32[1]{0:T(128)} %bitcast.15.count, s32[32]{0:T(128)} %tile_map.1, s32[1]{0:T(128)} %bitcast.2.me, s32[1]{0:T(128)} %bitcast.3.group, bf16[224,384]{1,0:T(8,128)(2,1)} %bitcast.22), custom_call_target="tpu_custom_call" | custom-call | tf_op jit(solution)/shard_map/plan/pallas_call | solution.py:286
  2.9 3.0 %collective-permute-start.3 = (bf16[240,384]{1,0:T(8,128)(2,1)S(1)}, bf16[240,384]{1,0:T(8,128)(2,1)S(1)}, u32[]{:S(2)}, u32[]{:S(2)}) collective-permute-start(bf16[240,384]{1,0:T(8,128)(2,1)S(1)} %get-tuple-element.32), channel_id=1, source_target_pairs={{0,2},{2,0},{4,6},{6,4},{8,10},{10,8},{12,14},{14,12},{16,18},{18,... | collective-permute-start | bytes 552968 | tf_op jit(solution)/shard_map/apply/ppermute | solution.py:300
  5.9 4.5 %collective-permute-start.1 = (bf16[240,384]{1,0:T(8,128)(2,1)S(1)}, bf16[240,384]{1,0:T(8,128)(2,1)S(1)}, u32[]{:S(2)}, u32[]{:S(2)}) collective-permute-start(bf16[240,384]{1,0:T(8,128)(2,1)S(1)} %get-tuple-element.32), channel_id=1, source_target_pairs={{0,30},{2,4},{4,2},{6,8},{8,6},{10,12},{12,10},{14,16},{16,14},{18... | collective-permute-start | bytes 552968 | tf_op jit(solution)/shard_map/apply/ppermute | solution.py:300
  10.4 0.8 %collective-permute-start = (bf16[240,384]{1,0:T(8,128)(2,1)S(1)}, bf16[240,384]{1,0:T(8,128)(2,1)S(1)}, u32[]{:S(2)}, u32[]{:S(2)}) collective-permute-start(bf16[240,384]{1,0:T(8,128)(2,1)S(1)} %get-tuple-element.32), channel_id=1, source_target_pairs={{0,28},{2,30},{4,8},{6,10},{8,4},{10,6},{12,16},{14,18},{16,12},{1... | collective-permute-start | bytes 552968 | tf_op jit(solution)/shard_map/apply/ppermute | solution.py:300
  11.3 2.3 %collective-permute-done.3.odd.refs_1_.refs_6_ = bf16[240,384]{1,0:T(8,128)(2,1)S(1)} collective-permute-done((bf16[240,384]{1,0:T(8,128)(2,1)S(1)}, bf16[240,384]{1,0:T(8,128)(2,1)S(1)}, u32[]{:S(2)}, u32[]{:S(2)}) %collective-permute-start.3) | collective-permute-done | bytes 184352 | tf_op jit(solution)/shard_map/apply/ppermute | solution.py:300
  13.6 0.9 %copy-done = bf16[1,2,128,256]{3,2,1,0:T(8,128)(2,1)S(1)} copy-done((bf16[1,2,128,256]{3,2,1,0:T(8,128)(2,1)S(1)}, bf16[1,2,128,256]{3,2,1,0:T(8,128)(2,1)}, u32[]{:S(2)}) %copy-start) | copy-done | bytes 131096
  17.2 2.9 %load.3 = (bf16[6,384,768]{2,1,0:T(8,128)(2,1)S(1)}, bf16[3,384,384]{2,1,0:T(8,128)(2,1)S(1)}) custom-call(s32[12]{0:T(128)S(1)} %get-tuple-element.28.table, s32[1]{0:T(128)} %bitcast.3.group, bf16[2,6,384,384]{3,2,1,0:T(8,128)(2,1)} %bitcast.20, bf16[2,2,384,384]{3,2,1,0:T(8,128)(2,1)} %bitcast.21), custom_call_target="tpu_custom_call" | custom-call | bytes 4718592 | tf_op jit(solution)/shard_map/load/pallas_call | solution.py:286
  20.4 1.6 %collective-permute-done.2.pair.refs_1_ = bf16[224,384]{1,0:T(8,128)(2,1)S(1)} collective-permute-done((bf16[224,384]{1,0:T(8,128)(2,1)S(1)}, bf16[224,384]{1,0:T(8,128)(2,1)S(1)}, u32[]{:S(2)}, u32[]{:S(2)}) %collective-permute-start.2) | collective-permute-done | bytes 172064 | tf_op jit(solution)/shard_map/plan/ppermute | solution.py:300
  22.1 4.1 %collective-permute-start.4 = (bf16[112,384]{1,0:T(8,128)(2,1)S(1)}, bf16[112,384]{1,0:T(8,128)(2,1)S(1)}, u32[]{:S(2)}, u32[]{:S(2)}) collective-permute-start(bf16[112,384]{1,0:T(8,128)(2,1)S(1)} %apply.19), channel_id=1, source_target_pairs={{0,30},{2,0},{4,2},{6,4},{8,6},{10,8},{12,10},{14,12},{16,14},{18,... | collective-permute-start | bytes 258056 | tf_op jit(solution)/shard_map/apply/ppermute | solution.py:300
  26.2 0.9 %collective-permute-start.7 = (f32[8,128]{1,0:T(8,128)S(1)}, f32[8,128]{1,0:T(8,128)S(1)}, u32[]{:S(2)}, u32[]{:S(2)}) collective-permute-start(f32[8,128]{1,0:T(8,128)S(1)} %apply.18.relayed), channel_id=1, source_target_pairs={{0,16},{2,18},{4,20},{6,22},{8,24},{10,26},{12,28},{14,30},{16,0},... | collective-permute-start | bytes 12296 | tf_op jit(solution)/shard_map/apply/ppermute | solution.py:300
  27.4 0.9 %collective-permute-done.4.refs_0_ = bf16[112,384]{1,0:T(8,128)(2,1)S(1)} collective-permute-done((bf16[112,384]{1,0:T(8,128)(2,1)S(1)}, bf16[112,384]{1,0:T(8,128)(2,1)S(1)}, u32[]{:S(2)}, u32[]{:S(2)}) %collective-permute-start.4) | collective-permute-done | bytes 86048 | tf_op jit(solution)/shard_map/apply/ppermute | solution.py:300
  28.7 2.1 %collective-permute-done.7.refs_7_ = f32[8,128]{1,0:T(8,128)S(1)} collective-permute-done((f32[8,128]{1,0:T(8,128)S(1)}, f32[8,128]{1,0:T(8,128)S(1)}, u32[]{:S(2)}, u32[]{:S(2)}) %collective-permute-start.7) | collective-permute-done | bytes 4128 | tf_op jit(solution)/shard_map/apply/ppermute | solution.py:300
  31.3 2.2 %collective-permute-start.8 = (bf16[112,384]{1,0:T(8,128)(2,1)S(1)}, bf16[112,384]{1,0:T(8,128)(2,1)S(1)}, u32[]{:S(2)}, u32[]{:S(2)}) collective-permute-start(bf16[112,384]{1,0:T(8,128)(2,1)S(1)} %get-tuple-element.34), channel_id=1, source_target_pairs={{0,28},{2,30},{4,8},{6,10},{8,4},{10,6},{12,16},{14,18},{16,12},{1... | collective-permute-start | bytes 258056 | tf_op jit(solution)/shard_map/apply/ppermute | solution.py:300
  33.5 1.9 %collective-permute-start.9 = (bf16[112,384]{1,0:T(8,128)(2,1)S(1)}, bf16[112,384]{1,0:T(8,128)(2,1)S(1)}, u32[]{:S(2)}, u32[]{:S(2)}) collective-permute-start(bf16[112,384]{1,0:T(8,128)(2,1)S(1)} %get-tuple-element.35), channel_id=1, source_target_pairs={{0,30},{2,4},{4,2},{6,8},{8,6},{10,12},{12,10},{14,16},{16,14},{18... | collective-permute-start | bytes 258056 | tf_op jit(solution)/shard_map/apply/ppermute | solution.py:300
  35.4 3.4 %collective-permute-start.11 = (bf16[112,384]{1,0:T(8,128)(2,1)S(1)}, bf16[112,384]{1,0:T(8,128)(2,1)S(1)}, u32[]{:S(2)}, u32[]{:S(2)}) collective-permute-start(bf16[112,384]{1,0:T(8,128)(2,1)S(1)} %get-tuple-element.37), channel_id=1, source_target_pairs={{0,14},{2,16},{4,18},{6,20},{8,22},{10,24},{12,26},{14,28},{16,30}... | collective-permute-start | bytes 258056 | tf_op jit(solution)/shard_map/apply/ppermute | solution.py:300
  38.8 2.1 %collective-permute-start.12 = (bf16[112,384]{1,0:T(8,128)(2,1)S(1)}, bf16[112,384]{1,0:T(8,128)(2,1)S(1)}, u32[]{:S(2)}, u32[]{:S(2)}) collective-permute-start(bf16[112,384]{1,0:T(8,128)(2,1)S(1)} %get-tuple-element.38), channel_id=1, source_target_pairs={{0,4},{2,6},{4,0},{6,2},{8,12},{10,14},{12,8},{14,10},{16,20},{18,... | collective-permute-start | bytes 258056 | tf_op jit(solution)/shard_map/apply/ppermute | solution.py:300
  41.2 0.8 %collective-permute-start.13 = (bf16[112,384]{1,0:T(8,128)(2,1)S(1)}, bf16[112,384]{1,0:T(8,128)(2,1)S(1)}, u32[]{:S(2)}, u32[]{:S(2)}) collective-permute-start(bf16[112,384]{1,0:T(8,128)(2,1)S(1)} %get-tuple-element.39), channel_id=1, source_target_pairs={{0,2},{2,0},{4,6},{6,4},{8,10},{10,8},{12,14},{14,12},{16,18},{18,... | collective-permute-start | bytes 258056 | tf_op jit(solution)/shard_map/apply/ppermute | solution.py:300
  43.7 2.1 %collective-permute-done.13.refs_1_ = bf16[112,384]{1,0:T(8,128)(2,1)S(1)} collective-permute-done((bf16[112,384]{1,0:T(8,128)(2,1)S(1)}, bf16[112,384]{1,0:T(8,128)(2,1)S(1)}, u32[]{:S(2)}, u32[]{:S(2)}) %collective-permute-start.13) | collective-permute-done | bytes 86048 | tf_op jit(solution)/shard_map/apply/ppermute | solution.py:300
  46.2 3.3 %collective-permute-start.15 = (bf16[112,384]{1,0:T(8,128)(2,1)S(1)}, bf16[112,384]{1,0:T(8,128)(2,1)S(1)}, u32[]{:S(2)}, u32[]{:S(2)}) collective-permute-start(bf16[112,384]{1,0:T(8,128)(2,1)S(1)} %get-tuple-element.43), channel_id=1, source_target_pairs={{0,28},{2,30},{4,8},{6,10},{8,4},{10,6},{12,16},{14,18},{16,12},{1... | collective-permute-start | bytes 258056 | tf_op jit(solution)/shard_map/apply/ppermute | solution.py:300
  49.5 1.9 %collective-permute-start.16 = (bf16[112,384]{1,0:T(8,128)(2,1)S(1)}, bf16[112,384]{1,0:T(8,128)(2,1)S(1)}, u32[]{:S(2)}, u32[]{:S(2)}) collective-permute-start(bf16[112,384]{1,0:T(8,128)(2,1)S(1)} %get-tuple-element.44), channel_id=1, source_target_pairs={{0,30},{2,4},{4,2},{6,8},{8,6},{10,12},{12,10},{14,16},{16,14},{18... | collective-permute-start | bytes 258056 | tf_op jit(solution)/shard_map/apply/ppermute | solution.py:300
  51.4 3.4 %collective-permute-start.18 = (bf16[112,384]{1,0:T(8,128)(2,1)S(1)}, bf16[112,384]{1,0:T(8,128)(2,1)S(1)}, u32[]{:S(2)}, u32[]{:S(2)}) collective-permute-start(bf16[112,384]{1,0:T(8,128)(2,1)S(1)} %get-tuple-element.46), channel_id=1, source_target_pairs={{0,14},{2,16},{4,18},{6,20},{8,22},{10,24},{12,26},{14,28},{16,30}... | collective-permute-start | bytes 258056 | tf_op jit(solution)/shard_map/apply/ppermute | solution.py:300
  55.1 1.8 %collective-permute-start.20 = (bf16[112,384]{1,0:T(8,128)(2,1)S(1)}, bf16[112,384]{1,0:T(8,128)(2,1)S(1)}, u32[]{:S(2)}, u32[]{:S(2)}) collective-permute-start(bf16[112,384]{1,0:T(8,128)(2,1)S(1)} %get-tuple-element.48), channel_id=1, source_target_pairs={{0,2},{2,0},{4,6},{6,4},{8,10},{10,8},{12,14},{14,12},{16,18},{18,... | collective-permute-start | bytes 258056 | tf_op jit(solution)/shard_map/apply/ppermute | solution.py:300
  59.6 1.1 %apply.31 = (bf16[2,112,384]{2,1,0:T(8,128)(2,1)}, bf16[32,8,112]{2,1,0:T(8,128)(2,1)S(1)}) custom-call(f32[2,112,384]{2,1,0:T(8,128)S(1)} %apply.27.part, f32[2,112,384]{2,1,0:T(8,128)S(1)} %apply.30.far, f32[8,128]{1,0:T(8,128)S(1)} %get-tuple-element.30.asks, bf16[6,384,768]{2,1,0:T(8,128)(2,1)S(1)} %get-tuple-element.31.bands, ...), custom_call_target="tpu_custom_call" | custom-call | flops 33030144 | bytes 165150 | tf_op jit(solution)/shard_map/apply/pallas_call | solution.py:286
  60.7 11.1 %all_to_all.5.pieces = bf16[32,8,112]{2,1,0:T(8,128)(2,1)S(1)} all-to-all(bf16[32,8,112]{2,1,0:T(8,128)(2,1)S(1)} %get-tuple-element.51), channel_id=1, replica_groups=mesh['areal'=16,'layer'=2] {'areal','layer'}, dimensions={0} | all-to-all | bytes 114688 | tf_op jit(solution)/shard_map/project/all_to_all | solution.py:486
  (50 shorter events, 10.3 us)
Async XLA Ops:
  2.9 10.7 %collective-permute-start.3 = (bf16[240,384]{1,0:T(8,128)(2,1)S(1)}, bf16[240,384]{1,0:T(8,128)(2,1)S(1)}, u32[]{:S(2)}, u32[]{:S(2)}) collective-permute-start(bf16[240,384]{1,0:T(8,128)(2,1)S(1)} %get-tuple-element.32), channel_id=1, source_target_pairs={{0,2},{2,0},{4,6},{6,4},{8,10},{10,8},{12,14},{14,12},{16,18},{18,... | collective-permute-start | bytes 552968 | tf_op jit(solution)/shard_map/apply/ppermute | solution.py:300
  5.9 14.5 %collective-permute-start.1 = (bf16[240,384]{1,0:T(8,128)(2,1)S(1)}, bf16[240,384]{1,0:T(8,128)(2,1)S(1)}, u32[]{:S(2)}, u32[]{:S(2)}) collective-permute-start(bf16[240,384]{1,0:T(8,128)(2,1)S(1)} %get-tuple-element.32), channel_id=1, source_target_pairs={{0,30},{2,4},{4,2},{6,8},{8,6},{10,12},{12,10},{14,16},{16,14},{18... | collective-permute-start | bytes 552968 | tf_op jit(solution)/shard_map/apply/ppermute | solution.py:300
  10.4 11.6 %collective-permute-start.2 = (bf16[224,384]{1,0:T(8,128)(2,1)S(1)}, bf16[224,384]{1,0:T(8,128)(2,1)S(1)}, u32[]{:S(2)}, u32[]{:S(2)}) collective-permute-start(bf16[224,384]{1,0:T(8,128)(2,1)S(1)} %get-tuple-element.27.lam.rhs), channel_id=1, source_target_pairs={{0,16},{2,18},{4,20},{6,22},{8,24},{10,26},{12,28},{14,30},{16,0},... | collective-permute-start | bytes 516104 | tf_op jit(solution)/shard_map/plan/ppermute | solution.py:300
  10.4 16.7 %collective-permute-start = (bf16[240,384]{1,0:T(8,128)(2,1)S(1)}, bf16[240,384]{1,0:T(8,128)(2,1)S(1)}, u32[]{:S(2)}, u32[]{:S(2)}) collective-permute-start(bf16[240,384]{1,0:T(8,128)(2,1)S(1)} %get-tuple-element.32), channel_id=1, source_target_pairs={{0,28},{2,30},{4,8},{6,10},{8,4},{10,6},{12,16},{14,18},{16,12},{1... | collective-permute-start | bytes 552968 | tf_op jit(solution)/shard_map/apply/ppermute | solution.py:300
  11.3 17.4 %collective-permute-start.6 = (bf16[240,384]{1,0:T(8,128)(2,1)S(1)}, bf16[240,384]{1,0:T(8,128)(2,1)S(1)}, u32[]{:S(2)}, u32[]{:S(2)}) collective-permute-start(bf16[240,384]{1,0:T(8,128)(2,1)S(1)} %get-tuple-element.32), channel_id=1, source_target_pairs={{0,1},{1,0},{2,3},{3,2},{4,5},{5,4},{6,7},{7,6},{8,9},{9,8},{10,11... | collective-permute-start | bytes 552968 | tf_op jit(solution)/shard_map/apply/ppermute | solution.py:310
  13.6 15.1 %collective-permute-start.5 = (bf16[240,384]{1,0:T(8,128)(2,1)S(1)}, bf16[240,384]{1,0:T(8,128)(2,1)S(1)}, u32[]{:S(2)}, u32[]{:S(2)}) collective-permute-start(bf16[240,384]{1,0:T(8,128)(2,1)S(1)} %get-tuple-element.32), channel_id=1, source_target_pairs={{0,4},{2,6},{4,0},{6,2},{8,12},{10,14},{12,8},{14,10},{16,20},{18,... | collective-permute-start | bytes 552968 | tf_op jit(solution)/shard_map/apply/ppermute | solution.py:300
  13.6 0.9 %copy-start = (bf16[1,2,128,256]{3,2,1,0:T(8,128)(2,1)S(1)}, bf16[1,2,128,256]{3,2,1,0:T(8,128)(2,1)}, u32[]{:S(2)}) copy-start(bf16[1,2,128,256]{3,2,1,0:T(8,128)(2,1)} %param.19) | copy-start | bytes 393220
  14.6 0.7 copy-start.1
  22.1 6.2 %collective-permute-start.4 = (bf16[112,384]{1,0:T(8,128)(2,1)S(1)}, bf16[112,384]{1,0:T(8,128)(2,1)S(1)}, u32[]{:S(2)}, u32[]{:S(2)}) collective-permute-start(bf16[112,384]{1,0:T(8,128)(2,1)S(1)} %apply.19), channel_id=1, source_target_pairs={{0,30},{2,0},{4,2},{6,4},{8,6},{10,8},{12,10},{14,12},{16,14},{18,... | collective-permute-start | bytes 258056 | tf_op jit(solution)/shard_map/apply/ppermute | solution.py:300
  26.2 4.6 %collective-permute-start.7 = (f32[8,128]{1,0:T(8,128)S(1)}, f32[8,128]{1,0:T(8,128)S(1)}, u32[]{:S(2)}, u32[]{:S(2)}) collective-permute-start(f32[8,128]{1,0:T(8,128)S(1)} %apply.18.relayed), channel_id=1, source_target_pairs={{0,16},{2,18},{4,20},{6,22},{8,24},{10,26},{12,28},{14,30},{16,0},... | collective-permute-start | bytes 12296 | tf_op jit(solution)/shard_map/apply/ppermute | solution.py:300
  31.3 9.9 %collective-permute-start.8 = (bf16[112,384]{1,0:T(8,128)(2,1)S(1)}, bf16[112,384]{1,0:T(8,128)(2,1)S(1)}, u32[]{:S(2)}, u32[]{:S(2)}) collective-permute-start(bf16[112,384]{1,0:T(8,128)(2,1)S(1)} %get-tuple-element.34), channel_id=1, source_target_pairs={{0,28},{2,30},{4,8},{6,10},{8,4},{10,6},{12,16},{14,18},{16,12},{1... | collective-permute-start | bytes 258056 | tf_op jit(solution)/shard_map/apply/ppermute | solution.py:300
  33.5 8.5 %collective-permute-start.10 = (bf16[112,384]{1,0:T(8,128)(2,1)S(1)}, bf16[112,384]{1,0:T(8,128)(2,1)S(1)}, u32[]{:S(2)}, u32[]{:S(2)}) collective-permute-start(bf16[112,384]{1,0:T(8,128)(2,1)S(1)} %get-tuple-element.36), channel_id=1, source_target_pairs={{0,16},{2,18},{4,20},{6,22},{8,24},{10,26},{12,28},{14,30},{16,0},... | collective-permute-start | bytes 258056 | tf_op jit(solution)/shard_map/apply/ppermute | solution.py:300
  33.5 9.1 %collective-permute-start.9 = (bf16[112,384]{1,0:T(8,128)(2,1)S(1)}, bf16[112,384]{1,0:T(8,128)(2,1)S(1)}, u32[]{:S(2)}, u32[]{:S(2)}) collective-permute-start(bf16[112,384]{1,0:T(8,128)(2,1)S(1)} %get-tuple-element.35), channel_id=1, source_target_pairs={{0,30},{2,4},{4,2},{6,8},{8,6},{10,12},{12,10},{14,16},{16,14},{18... | collective-permute-start | bytes 258056 | tf_op jit(solution)/shard_map/apply/ppermute | solution.py:300
  35.4 8.0 %collective-permute-start.11 = (bf16[112,384]{1,0:T(8,128)(2,1)S(1)}, bf16[112,384]{1,0:T(8,128)(2,1)S(1)}, u32[]{:S(2)}, u32[]{:S(2)}) collective-permute-start(bf16[112,384]{1,0:T(8,128)(2,1)S(1)} %get-tuple-element.37), channel_id=1, source_target_pairs={{0,14},{2,16},{4,18},{6,20},{8,22},{10,24},{12,26},{14,28},{16,30}... | collective-permute-start | bytes 258056 | tf_op jit(solution)/shard_map/apply/ppermute | solution.py:300
  38.8 4.8 %collective-permute-start.12 = (bf16[112,384]{1,0:T(8,128)(2,1)S(1)}, bf16[112,384]{1,0:T(8,128)(2,1)S(1)}, u32[]{:S(2)}, u32[]{:S(2)}) collective-permute-start(bf16[112,384]{1,0:T(8,128)(2,1)S(1)} %get-tuple-element.38), channel_id=1, source_target_pairs={{0,4},{2,6},{4,0},{6,2},{8,12},{10,14},{12,8},{14,10},{16,20},{18,... | collective-permute-start | bytes 258056 | tf_op jit(solution)/shard_map/apply/ppermute | solution.py:300
  41.2 4.6 %collective-permute-start.13 = (bf16[112,384]{1,0:T(8,128)(2,1)S(1)}, bf16[112,384]{1,0:T(8,128)(2,1)S(1)}, u32[]{:S(2)}, u32[]{:S(2)}) collective-permute-start(bf16[112,384]{1,0:T(8,128)(2,1)S(1)} %get-tuple-element.39), channel_id=1, source_target_pairs={{0,2},{2,0},{4,6},{6,4},{8,10},{10,8},{12,14},{14,12},{16,18},{18,... | collective-permute-start | bytes 258056 | tf_op jit(solution)/shard_map/apply/ppermute | solution.py:300
  42.0 3.7 %collective-permute-start.14 = (bf16[112,384]{1,0:T(8,128)(2,1)S(1)}, bf16[112,384]{1,0:T(8,128)(2,1)S(1)}, u32[]{:S(2)}, u32[]{:S(2)}) collective-permute-start(bf16[112,384]{1,0:T(8,128)(2,1)S(1)} %get-tuple-element.40), channel_id=1, source_target_pairs={{0,1},{1,0},{2,3},{3,2},{4,5},{5,4},{6,7},{7,6},{8,9},{9,8},{10,11... | collective-permute-start | bytes 258056 | tf_op jit(solution)/shard_map/apply/ppermute | solution.py:310
  46.2 8.9 %collective-permute-start.15 = (bf16[112,384]{1,0:T(8,128)(2,1)S(1)}, bf16[112,384]{1,0:T(8,128)(2,1)S(1)}, u32[]{:S(2)}, u32[]{:S(2)}) collective-permute-start(bf16[112,384]{1,0:T(8,128)(2,1)S(1)} %get-tuple-element.43), channel_id=1, source_target_pairs={{0,28},{2,30},{4,8},{6,10},{8,4},{10,6},{12,16},{14,18},{16,12},{1... | collective-permute-start | bytes 258056 | tf_op jit(solution)/shard_map/apply/ppermute | solution.py:300
  49.5 7.4 %collective-permute-start.17 = (bf16[112,384]{1,0:T(8,128)(2,1)S(1)}, bf16[112,384]{1,0:T(8,128)(2,1)S(1)}, u32[]{:S(2)}, u32[]{:S(2)}) collective-permute-start(bf16[112,384]{1,0:T(8,128)(2,1)S(1)} %get-tuple-element.45), channel_id=1, source_target_pairs={{0,16},{2,18},{4,20},{6,22},{8,24},{10,26},{12,28},{14,30},{16,0},... | collective-permute-start | bytes 258056 | tf_op jit(solution)/shard_map/apply/ppermute | solution.py:300
  49.5 8.2 %collective-permute-start.16 = (bf16[112,384]{1,0:T(8,128)(2,1)S(1)}, bf16[112,384]{1,0:T(8,128)(2,1)S(1)}, u32[]{:S(2)}, u32[]{:S(2)}) collective-permute-start(bf16[112,384]{1,0:T(8,128)(2,1)S(1)} %get-tuple-element.44), channel_id=1, source_target_pairs={{0,30},{2,4},{4,2},{6,8},{8,6},{10,12},{12,10},{14,16},{16,14},{18... | collective-permute-start | bytes 258056 | tf_op jit(solution)/shard_map/apply/ppermute | solution.py:300
  51.4 7.3 %collective-permute-start.18 = (bf16[112,384]{1,0:T(8,128)(2,1)S(1)}, bf16[112,384]{1,0:T(8,128)(2,1)S(1)}, u32[]{:S(2)}, u32[]{:S(2)}) collective-permute-start(bf16[112,384]{1,0:T(8,128)(2,1)S(1)} %get-tuple-element.46), channel_id=1, source_target_pairs={{0,14},{2,16},{4,18},{6,20},{8,22},{10,24},{12,26},{14,28},{16,30}... | collective-permute-start | bytes 258056 | tf_op jit(solution)/shard_map/apply/ppermute | solution.py:300
  54.8 4.5 %collective-permute-start.19 = (bf16[112,384]{1,0:T(8,128)(2,1)S(1)}, bf16[112,384]{1,0:T(8,128)(2,1)S(1)}, u32[]{:S(2)}, u32[]{:S(2)}) collective-permute-start(bf16[112,384]{1,0:T(8,128)(2,1)S(1)} %get-tuple-element.47), channel_id=1, source_target_pairs={{0,4},{2,6},{4,0},{6,2},{8,12},{10,14},{12,8},{14,10},{16,20},{18,... | collective-permute-start | bytes 258056 | tf_op jit(solution)/shard_map/apply/ppermute | solution.py:300
  55.1 4.6 %collective-permute-start.20 = (bf16[112,384]{1,0:T(8,128)(2,1)S(1)}, bf16[112,384]{1,0:T(8,128)(2,1)S(1)}, u32[]{:S(2)}, u32[]{:S(2)}) collective-permute-start(bf16[112,384]{1,0:T(8,128)(2,1)S(1)} %get-tuple-element.48), channel_id=1, source_target_pairs={{0,2},{2,0},{4,6},{6,4},{8,10},{10,8},{12,14},{14,12},{16,18},{18,... | collective-permute-start | bytes 258056 | tf_op jit(solution)/shard_map/apply/ppermute | solution.py:300
  56.9 2.7 %collective-permute-start.21 = (bf16[112,384]{1,0:T(8,128)(2,1)S(1)}, bf16[112,384]{1,0:T(8,128)(2,1)S(1)}, u32[]{:S(2)}, u32[]{:S(2)}) collective-permute-start(bf16[112,384]{1,0:T(8,128)(2,1)S(1)} %get-tuple-element.49), channel_id=1, source_target_pairs={{0,1},{1,0},{2,3},{3,2},{4,5},{5,4},{6,7},{7,6},{8,9},{9,8},{10,11... | collective-permute-start | bytes 258056 | tf_op jit(solution)/shard_map/apply/ppermute | solution.py:310
  (2 other events, 1.4 us)

commit v4 on v2

--- a/solution.py
+++ b/solution.py
@@ -65,7 +65,7 @@
     pair[...] = rhs[...]
 
 
-def load_kernel(number, two, table, group, blocks, vert, bands, sides, sems):
+def load_kernel(number, two, columns, table, group, wells, gains, blocks, vert, sens, basis, bands, sides, factors, turned, sems):
     width = vert.shape[-1]
     mine = group[0]
     ends = [(1 - mine, 1 - mine)] if two else [(0, 0), (1, 1)]
@@ -96,6 +96,12 @@
         @pl.when(table[number + i] == 0)
         def _():
             bands[i] = jnp.zeros(bands.shape[1:], bands.dtype)
+
+    weigh_kernel(wells, gains, sens, factors)
+    if two:
+        turn_kernel(columns, basis, turned)
+    else:
+        turned[...] = basis[...]
 
     for i in range(number):
 
@@ -366,32 +372,30 @@
         far_pair = moved_by(both, routes[-1])
 
     with jax.named_scope("load"):
-        bands, sides = call(
-            partial(load_kernel, number, two),
+        cells = sens.shape[-1]
+        bands, sides, factors, weights = call(
+            partial(load_kernel, number, two, columns),
             [
                 pltpu.VMEM((number, width, 2 * width), BF16),
                 pltpu.VMEM((3 if two else 4, width, width), BF16),
+                pltpu.VMEM((sens.shape[2], 2, cells), F32),
+                pltpu.VMEM((modes // 2, 4 * cells) if two else basis.shape[1:], BF16),
             ],
-            (table, group, outside(areal_blocks[0]), outside(vertical_blocks[0])),
-            [SMEM] * 2 + [pl.BlockSpec(memory_space=pltpu.HBM)] * 2,
+            (
+                table,
+                group,
+                well_cells[0],
+                well_gain[0],
+                outside(areal_blocks[0]),
+                outside(vertical_blocks[0]),
+                sens[0].transpose(1, 0, 2),
+                basis[0],
+            ),
+            [SMEM] * 4 + [pl.BlockSpec(memory_space=pltpu.HBM)] * 2 + [VMEM] * 2,
             [pltpu.SemaphoreType.DMA((2 * number + 4,))],
             moved=areal_blocks.size * 2 + vertical_blocks.size * 2,
         )
         bands, sides = held(bands), held(sides)
-        (factors,) = call(
-            weigh_kernel,
-            [pltpu.VMEM((sens.shape[2], 2, sens.shape[3]), F32)],
-            (well_cells[0], well_gain[0], sens[0].transpose(1, 0, 2)),
-            [SMEM] * 2 + [VMEM],
-        )
-        weights = held(basis[0])
-        if two:
-            (weights,) = call(
-                partial(turn_kernel, columns),
-                [pltpu.VMEM((modes // 2, 4 * sens.shape[3]), BF16)],
-                (basis[0],),
-                [VMEM],
-            )
         factors, weights = held(factors), held(weights)
 
     rhs_held = lam = both

time: 72.6 us -> 73.1 us (level)
  waiting for transfers between devices: 16.3 us -> 13.3 us
  local copies, waits for them, and re-layouts: 0.03 us -> 2.94 us
    ppermute x19, waiting for transfers between devices: 16.3 us -> 13.3 us  [moved_by(): return held(lax.ppermute(x, 'areal', pairs))]
    unnamed x8, local copies, waits for them, and re-layouts: 0.03 us -> 2.94 us
    pallas_call x21 -> x19, Pallas kernels: 10.5 us -> 10.3 us  [call(): pl.pallas_call(kernel, out_shape=outs, in_specs=specs, out_specs=out_spec...]
  transfers between devices with their start and end apart: 22 -> 22, of which waited for: 9 -> 11; matrix products, arithmetic and copies ran while one was open for 0% -> 0% of each run, Pallas kernels for 8% -> 8%
where the time goes in v4:
time: 73.1 us; the launch traced here: 72.8 us
  starting transfers between devices  33.7 us (46%)
  waiting for transfers between devices  13.3 us (18%)
  blocking collectives  11.2 us (15%)
  Pallas kernels  10.3 us (14%)
  local copies, waits for them, and re-layouts  2.94 us (4%)
  between operations  1.46 us (2%)
    ppermute x19, starting transfers between devices, moved_by(): return held(lax.ppermute(x, 'areal', pairs))  33.7 us
    ppermute x19, waiting for transfers between devices, moved_by(): return held(lax.ppermute(x, 'areal', pairs))  13.3 us
    all_to_all x1, blocking collectives, on_device(): landed = lax.all_to_all(pieces, ('areal', 'layer'), 0, 0, tiled=True)  11.2 us
    pallas_call x19, Pallas kernels, call(): pl.pallas_call(kernel, out_shape=outs, in_specs=specs, out_specs=out_spec...  10.3 us
    unnamed x8, local copies, waits for them, and re-layouts  2.94 us
  transfers between devices with their start and end apart: 22, of which 11 were waited for; matrix products, arithmetic and copies ran while one was open for 0% of the time, Pallas kernels for 8%

profile of v4, /device:TPU:0, one launch (start us, length us, event | category | flops | bytes accessed | tf_op | source)
XLA Modules:
  0.0 72.8 jit_solution(3826612924204216323)
XLA Ops:
  1.3 1.6 %plan.1 = (s32[12]{0:T(128)S(1)}, f32[8,128]{1,0:T(8,128)S(1)}, bf16[240,384]{1,0:T(8,128)(2,1)S(1)}, bf16[224,384]{1,0:T(8,128)(2,1)S(1)}) custom-call(s32[6]{0:T(128)} %bitcast.24, s32[1]{0:T(128)} %bitcast.15.count, s32[32]{0:T(128)} %tile_map.1, s32[1]{0:T(128)} %bitcast.2.me, s32[1]{0:T(128)} %bitcast.3.group, bf16[224,384]{1,0:T(8,128)(2,1)} %bitcast.22), custom_call_target="tpu_custom_call" | custom-call | tf_op jit(solution)/shard_map/plan/pallas_call | solution.py:292
  2.9 3.0 %collective-permute-start.3 = (bf16[240,384]{1,0:T(8,128)(2,1)S(1)}, bf16[240,384]{1,0:T(8,128)(2,1)S(1)}, u32[]{:S(2)}, u32[]{:S(2)}) collective-permute-start(bf16[240,384]{1,0:T(8,128)(2,1)S(1)} %get-tuple-element.34), channel_id=1, source_target_pairs={{0,2},{2,0},{4,6},{6,4},{8,10},{10,8},{12,14},{14,12},{16,18},{18,... | collective-permute-start | bytes 552968 | tf_op jit(solution)/shard_map/apply/ppermute | solution.py:306
  5.9 4.5 %collective-permute-start.1 = (bf16[240,384]{1,0:T(8,128)(2,1)S(1)}, bf16[240,384]{1,0:T(8,128)(2,1)S(1)}, u32[]{:S(2)}, u32[]{:S(2)}) collective-permute-start(bf16[240,384]{1,0:T(8,128)(2,1)S(1)} %get-tuple-element.34), channel_id=1, source_target_pairs={{0,30},{2,4},{4,2},{6,8},{8,6},{10,12},{12,10},{14,16},{16,14},{18... | collective-permute-start | bytes 552968 | tf_op jit(solution)/shard_map/apply/ppermute | solution.py:306
  10.4 0.8 %collective-permute-start = (bf16[240,384]{1,0:T(8,128)(2,1)S(1)}, bf16[240,384]{1,0:T(8,128)(2,1)S(1)}, u32[]{:S(2)}, u32[]{:S(2)}) collective-permute-start(bf16[240,384]{1,0:T(8,128)(2,1)S(1)} %get-tuple-element.34), channel_id=1, source_target_pairs={{0,28},{2,30},{4,8},{6,10},{8,4},{10,6},{12,16},{14,18},{16,12},{1... | collective-permute-start | bytes 552968 | tf_op jit(solution)/shard_map/apply/ppermute | solution.py:306
  11.3 2.3 %collective-permute-done.3.odd.refs_1_.refs_6_ = bf16[240,384]{1,0:T(8,128)(2,1)S(1)} collective-permute-done((bf16[240,384]{1,0:T(8,128)(2,1)S(1)}, bf16[240,384]{1,0:T(8,128)(2,1)S(1)}, u32[]{:S(2)}, u32[]{:S(2)}) %collective-permute-start.3) | collective-permute-done | bytes 184352 | tf_op jit(solution)/shard_map/apply/ppermute | solution.py:306
  13.6 0.9 %copy-done = bf16[1,2,128,256]{3,2,1,0:T(8,128)(2,1)S(1)} copy-done((bf16[1,2,128,256]{3,2,1,0:T(8,128)(2,1)S(1)}, bf16[1,2,128,256]{3,2,1,0:T(8,128)(2,1)}, u32[]{:S(2)}) %copy-start) | copy-done | bytes 131096
  16.5 2.8 %load.1 = (bf16[6,384,768]{2,1,0:T(8,128)(2,1)S(1)}, bf16[3,384,384]{2,1,0:T(8,128)(2,1)S(1)}, f32[3,2,128]{2,1,0:T(2,128)S(1)}, bf16[128,512]{1,0:T(8,128)(2,1)S(1)}) custom-call(s32[12]{0:T(128)S(1)} %get-tuple-element.30.table, s32[1]{0:T(128)} %bitcast.3.group, s32[2,4]{1,0:T(2,128)S(1)} %bitcast.18, f32[2,4]{1,0:T(2,128)S(1)} %bitcast.19, ...), custom_call_target="tpu_custom_call" | custom-call | bytes 4718592 | tf_op jit(solution)/shard_map/load/pallas_call | solution.py:292
  19.6 2.4 %collective-permute-done.2.pair.refs_1_ = bf16[224,384]{1,0:T(8,128)(2,1)S(1)} collective-permute-done((bf16[224,384]{1,0:T(8,128)(2,1)S(1)}, bf16[224,384]{1,0:T(8,128)(2,1)S(1)}, u32[]{:S(2)}, u32[]{:S(2)}) %collective-permute-start.2) | collective-permute-done | bytes 172064 | tf_op jit(solution)/shard_map/plan/ppermute | solution.py:306
  22.1 4.1 %collective-permute-start.4 = (bf16[112,384]{1,0:T(8,128)(2,1)S(1)}, bf16[112,384]{1,0:T(8,128)(2,1)S(1)}, u32[]{:S(2)}, u32[]{:S(2)}) collective-permute-start(bf16[112,384]{1,0:T(8,128)(2,1)S(1)} %apply.19), channel_id=1, source_target_pairs={{0,30},{2,0},{4,2},{6,4},{8,6},{10,8},{12,10},{14,12},{16,14},{18,... | collective-permute-start | bytes 258056 | tf_op jit(solution)/shard_map/apply/ppermute | solution.py:306
  26.5 1.7 %collective-permute-done.4.refs_0_ = bf16[112,384]{1,0:T(8,128)(2,1)S(1)} collective-permute-done((bf16[112,384]{1,0:T(8,128)(2,1)S(1)}, bf16[112,384]{1,0:T(8,128)(2,1)S(1)}, u32[]{:S(2)}, u32[]{:S(2)}) %collective-permute-start.4) | collective-permute-done | bytes 86048 | tf_op jit(solution)/shard_map/apply/ppermute | solution.py:306
  28.7 2.1 %collective-permute-done.7.refs_7_ = f32[8,128]{1,0:T(8,128)S(1)} collective-permute-done((f32[8,128]{1,0:T(8,128)S(1)}, f32[8,128]{1,0:T(8,128)S(1)}, u32[]{:S(2)}, u32[]{:S(2)}) %collective-permute-start.7) | collective-permute-done | bytes 4128 | tf_op jit(solution)/shard_map/apply/ppermute | solution.py:306
  31.3 2.2 %collective-permute-start.8 = (bf16[112,384]{1,0:T(8,128)(2,1)S(1)}, bf16[112,384]{1,0:T(8,128)(2,1)S(1)}, u32[]{:S(2)}, u32[]{:S(2)}) collective-permute-start(bf16[112,384]{1,0:T(8,128)(2,1)S(1)} %get-tuple-element.36), channel_id=1, source_target_pairs={{0,28},{2,30},{4,8},{6,10},{8,4},{10,6},{12,16},{14,18},{16,12},{1... | collective-permute-start | bytes 258056 | tf_op jit(solution)/shard_map/apply/ppermute | solution.py:306
  33.5 1.9 %collective-permute-start.9 = (bf16[112,384]{1,0:T(8,128)(2,1)S(1)}, bf16[112,384]{1,0:T(8,128)(2,1)S(1)}, u32[]{:S(2)}, u32[]{:S(2)}) collective-permute-start(bf16[112,384]{1,0:T(8,128)(2,1)S(1)} %get-tuple-element.37), channel_id=1, source_target_pairs={{0,30},{2,4},{4,2},{6,8},{8,6},{10,12},{12,10},{14,16},{16,14},{18... | collective-permute-start | bytes 258056 | tf_op jit(solution)/shard_map/apply/ppermute | solution.py:306
  35.4 3.4 %collective-permute-start.11 = (bf16[112,384]{1,0:T(8,128)(2,1)S(1)}, bf16[112,384]{1,0:T(8,128)(2,1)S(1)}, u32[]{:S(2)}, u32[]{:S(2)}) collective-permute-start(bf16[112,384]{1,0:T(8,128)(2,1)S(1)} %get-tuple-element.39), channel_id=1, source_target_pairs={{0,14},{2,16},{4,18},{6,20},{8,22},{10,24},{12,26},{14,28},{16,30}... | collective-permute-start | bytes 258056 | tf_op jit(solution)/shard_map/apply/ppermute | solution.py:306
  38.8 2.1 %collective-permute-start.12 = (bf16[112,384]{1,0:T(8,128)(2,1)S(1)}, bf16[112,384]{1,0:T(8,128)(2,1)S(1)}, u32[]{:S(2)}, u32[]{:S(2)}) collective-permute-start(bf16[112,384]{1,0:T(8,128)(2,1)S(1)} %get-tuple-element.40), channel_id=1, source_target_pairs={{0,4},{2,6},{4,0},{6,2},{8,12},{10,14},{12,8},{14,10},{16,20},{18,... | collective-permute-start | bytes 258056 | tf_op jit(solution)/shard_map/apply/ppermute | solution.py:306
  41.2 0.8 %collective-permute-start.13 = (bf16[112,384]{1,0:T(8,128)(2,1)S(1)}, bf16[112,384]{1,0:T(8,128)(2,1)S(1)}, u32[]{:S(2)}, u32[]{:S(2)}) collective-permute-start(bf16[112,384]{1,0:T(8,128)(2,1)S(1)} %get-tuple-element.41), channel_id=1, source_target_pairs={{0,2},{2,0},{4,6},{6,4},{8,10},{10,8},{12,14},{14,12},{16,18},{18,... | collective-permute-start | bytes 258056 | tf_op jit(solution)/shard_map/apply/ppermute | solution.py:306
  43.6 2.1 %collective-permute-done.13.refs_1_ = bf16[112,384]{1,0:T(8,128)(2,1)S(1)} collective-permute-done((bf16[112,384]{1,0:T(8,128)(2,1)S(1)}, bf16[112,384]{1,0:T(8,128)(2,1)S(1)}, u32[]{:S(2)}, u32[]{:S(2)}) %collective-permute-start.13) | collective-permute-done | bytes 86048 | tf_op jit(solution)/shard_map/apply/ppermute | solution.py:306
  46.2 3.3 %collective-permute-start.15 = (bf16[112,384]{1,0:T(8,128)(2,1)S(1)}, bf16[112,384]{1,0:T(8,128)(2,1)S(1)}, u32[]{:S(2)}, u32[]{:S(2)}) collective-permute-start(bf16[112,384]{1,0:T(8,128)(2,1)S(1)} %get-tuple-element.45), channel_id=1, source_target_pairs={{0,28},{2,30},{4,8},{6,10},{8,4},{10,6},{12,16},{14,18},{16,12},{1... | collective-permute-start | bytes 258056 | tf_op jit(solution)/shard_map/apply/ppermute | solution.py:306
  49.5 2.2 %collective-permute-start.16 = (bf16[112,384]{1,0:T(8,128)(2,1)S(1)}, bf16[112,384]{1,0:T(8,128)(2,1)S(1)}, u32[]{:S(2)}, u32[]{:S(2)}) collective-permute-start(bf16[112,384]{1,0:T(8,128)(2,1)S(1)} %get-tuple-element.46), channel_id=1, source_target_pairs={{0,30},{2,4},{4,2},{6,8},{8,6},{10,12},{12,10},{14,16},{16,14},{18... | collective-permute-start | bytes 258056 | tf_op jit(solution)/shard_map/apply/ppermute | solution.py:306
  51.7 3.1 %collective-permute-start.18 = (bf16[112,384]{1,0:T(8,128)(2,1)S(1)}, bf16[112,384]{1,0:T(8,128)(2,1)S(1)}, u32[]{:S(2)}, u32[]{:S(2)}) collective-permute-start(bf16[112,384]{1,0:T(8,128)(2,1)S(1)} %get-tuple-element.48), channel_id=1, source_target_pairs={{0,14},{2,16},{4,18},{6,20},{8,22},{10,24},{12,26},{14,28},{16,30}... | collective-permute-start | bytes 258056 | tf_op jit(solution)/shard_map/apply/ppermute | solution.py:306
  55.2 2.1 %collective-permute-start.20 = (bf16[112,384]{1,0:T(8,128)(2,1)S(1)}, bf16[112,384]{1,0:T(8,128)(2,1)S(1)}, u32[]{:S(2)}, u32[]{:S(2)}) collective-permute-start(bf16[112,384]{1,0:T(8,128)(2,1)S(1)} %get-tuple-element.52), channel_id=1, source_target_pairs={{0,2},{2,0},{4,6},{6,4},{8,10},{10,8},{12,14},{14,12},{16,18},{18,... | collective-permute-start | bytes 258056 | tf_op jit(solution)/shard_map/apply/ppermute | solution.py:306
  59.9 1.1 %apply.31 = (bf16[2,112,384]{2,1,0:T(8,128)(2,1)}, bf16[32,8,112]{2,1,0:T(8,128)(2,1)S(1)}) custom-call(f32[2,112,384]{2,1,0:T(8,128)S(1)} %apply.27.part, f32[2,112,384]{2,1,0:T(8,128)S(1)} %apply.30.far, f32[8,128]{1,0:T(8,128)S(1)} %get-tuple-element.32.asks, bf16[6,384,768]{2,1,0:T(8,128)(2,1)S(1)} %get-tuple-element.33.bands, ...), custom_call_target="tpu_custom_call" | custom-call | flops 33030144 | bytes 165150 | tf_op jit(solution)/shard_map/apply/pallas_call | solution.py:292
  61.0 11.2 %all_to_all.5.pieces = bf16[32,8,112]{2,1,0:T(8,128)(2,1)S(1)} all-to-all(bf16[32,8,112]{2,1,0:T(8,128)(2,1)S(1)} %get-tuple-element.55), channel_id=1, replica_groups=mesh['areal'=16,'layer'=2] {'areal','layer'}, dimensions={0} | all-to-all | bytes 114688 | tf_op jit(solution)/shard_map/project/all_to_all | solution.py:490
  72.1 0.7 project.1
  (48 shorter events, 8.8 us)
Async XLA Ops:
  2.9 10.7 %collective-permute-start.3 = (bf16[240,384]{1,0:T(8,128)(2,1)S(1)}, bf16[240,384]{1,0:T(8,128)(2,1)S(1)}, u32[]{:S(2)}, u32[]{:S(2)}) collective-permute-start(bf16[240,384]{1,0:T(8,128)(2,1)S(1)} %get-tuple-element.34), channel_id=1, source_target_pairs={{0,2},{2,0},{4,6},{6,4},{8,10},{10,8},{12,14},{14,12},{16,18},{18,... | collective-permute-start | bytes 552968 | tf_op jit(solution)/shard_map/apply/ppermute | solution.py:306
  5.9 13.7 %collective-permute-start.1 = (bf16[240,384]{1,0:T(8,128)(2,1)S(1)}, bf16[240,384]{1,0:T(8,128)(2,1)S(1)}, u32[]{:S(2)}, u32[]{:S(2)}) collective-permute-start(bf16[240,384]{1,0:T(8,128)(2,1)S(1)} %get-tuple-element.34), channel_id=1, source_target_pairs={{0,30},{2,4},{4,2},{6,8},{8,6},{10,12},{12,10},{14,16},{16,14},{18... | collective-permute-start | bytes 552968 | tf_op jit(solution)/shard_map/apply/ppermute | solution.py:306
  10.4 11.6 %collective-permute-start.2 = (bf16[224,384]{1,0:T(8,128)(2,1)S(1)}, bf16[224,384]{1,0:T(8,128)(2,1)S(1)}, u32[]{:S(2)}, u32[]{:S(2)}) collective-permute-start(bf16[224,384]{1,0:T(8,128)(2,1)S(1)} %get-tuple-element.29.lam.rhs), channel_id=1, source_target_pairs={{0,16},{2,18},{4,20},{6,22},{8,24},{10,26},{12,28},{14,30},{16,0},... | collective-permute-start | bytes 516104 | tf_op jit(solution)/shard_map/plan/ppermute | solution.py:306
  10.4 15.8 %collective-permute-start = (bf16[240,384]{1,0:T(8,128)(2,1)S(1)}, bf16[240,384]{1,0:T(8,128)(2,1)S(1)}, u32[]{:S(2)}, u32[]{:S(2)}) collective-permute-start(bf16[240,384]{1,0:T(8,128)(2,1)S(1)} %get-tuple-element.34), channel_id=1, source_target_pairs={{0,28},{2,30},{4,8},{6,10},{8,4},{10,6},{12,16},{14,18},{16,12},{1... | collective-permute-start | bytes 552968 | tf_op jit(solution)/shard_map/apply/ppermute | solution.py:306
  11.3 17.4 %collective-permute-start.6 = (bf16[240,384]{1,0:T(8,128)(2,1)S(1)}, bf16[240,384]{1,0:T(8,128)(2,1)S(1)}, u32[]{:S(2)}, u32[]{:S(2)}) collective-permute-start(bf16[240,384]{1,0:T(8,128)(2,1)S(1)} %get-tuple-element.34), channel_id=1, source_target_pairs={{0,1},{1,0},{2,3},{3,2},{4,5},{5,4},{6,7},{7,6},{8,9},{9,8},{10,11... | collective-permute-start | bytes 552968 | tf_op jit(solution)/shard_map/apply/ppermute | solution.py:316
  13.6 15.1 %collective-permute-start.5 = (bf16[240,384]{1,0:T(8,128)(2,1)S(1)}, bf16[240,384]{1,0:T(8,128)(2,1)S(1)}, u32[]{:S(2)}, u32[]{:S(2)}) collective-permute-start(bf16[240,384]{1,0:T(8,128)(2,1)S(1)} %get-tuple-element.34), channel_id=1, source_target_pairs={{0,4},{2,6},{4,0},{6,2},{8,12},{10,14},{12,8},{14,10},{16,20},{18,... | collective-permute-start | bytes 552968 | tf_op jit(solution)/shard_map/apply/ppermute | solution.py:306
  13.6 0.9 %copy-start = (bf16[1,2,128,256]{3,2,1,0:T(8,128)(2,1)S(1)}, bf16[1,2,128,256]{3,2,1,0:T(8,128)(2,1)}, u32[]{:S(2)}) copy-start(bf16[1,2,128,256]{3,2,1,0:T(8,128)(2,1)} %param.19) | copy-start | bytes 393220
  14.5 0.7 copy-start.1
  22.1 6.2 %collective-permute-start.4 = (bf16[112,384]{1,0:T(8,128)(2,1)S(1)}, bf16[112,384]{1,0:T(8,128)(2,1)S(1)}, u32[]{:S(2)}, u32[]{:S(2)}) collective-permute-start(bf16[112,384]{1,0:T(8,128)(2,1)S(1)} %apply.19), channel_id=1, source_target_pairs={{0,30},{2,0},{4,2},{6,4},{8,6},{10,8},{12,10},{14,12},{16,14},{18,... | collective-permute-start | bytes 258056 | tf_op jit(solution)/shard_map/apply/ppermute | solution.py:306
  26.2 4.6 %collective-permute-start.7 = (f32[8,128]{1,0:T(8,128)S(1)}, f32[8,128]{1,0:T(8,128)S(1)}, u32[]{:S(2)}, u32[]{:S(2)}) collective-permute-start(f32[8,128]{1,0:T(8,128)S(1)} %apply.18.relayed), channel_id=1, source_target_pairs={{0,16},{2,18},{4,20},{6,22},{8,24},{10,26},{12,28},{14,30},{16,0},... | collective-permute-start | bytes 12296 | tf_op jit(solution)/shard_map/apply/ppermute | solution.py:306
  31.3 9.9 %collective-permute-start.8 = (bf16[112,384]{1,0:T(8,128)(2,1)S(1)}, bf16[112,384]{1,0:T(8,128)(2,1)S(1)}, u32[]{:S(2)}, u32[]{:S(2)}) collective-permute-start(bf16[112,384]{1,0:T(8,128)(2,1)S(1)} %get-tuple-element.36), channel_id=1, source_target_pairs={{0,28},{2,30},{4,8},{6,10},{8,4},{10,6},{12,16},{14,18},{16,12},{1... | collective-permute-start | bytes 258056 | tf_op jit(solution)/shard_map/apply/ppermute | solution.py:306
  33.5 8.5 %collective-permute-start.10 = (bf16[112,384]{1,0:T(8,128)(2,1)S(1)}, bf16[112,384]{1,0:T(8,128)(2,1)S(1)}, u32[]{:S(2)}, u32[]{:S(2)}) collective-permute-start(bf16[112,384]{1,0:T(8,128)(2,1)S(1)} %get-tuple-element.38), channel_id=1, source_target_pairs={{0,16},{2,18},{4,20},{6,22},{8,24},{10,26},{12,28},{14,30},{16,0},... | collective-permute-start | bytes 258056 | tf_op jit(solution)/shard_map/apply/ppermute | solution.py:306
  33.5 9.2 %collective-permute-start.9 = (bf16[112,384]{1,0:T(8,128)(2,1)S(1)}, bf16[112,384]{1,0:T(8,128)(2,1)S(1)}, u32[]{:S(2)}, u32[]{:S(2)}) collective-permute-start(bf16[112,384]{1,0:T(8,128)(2,1)S(1)} %get-tuple-element.37), channel_id=1, source_target_pairs={{0,30},{2,4},{4,2},{6,8},{8,6},{10,12},{12,10},{14,16},{16,14},{18... | collective-permute-start | bytes 258056 | tf_op jit(solution)/shard_map/apply/ppermute | solution.py:306
  35.4 8.0 %collective-permute-start.11 = (bf16[112,384]{1,0:T(8,128)(2,1)S(1)}, bf16[112,384]{1,0:T(8,128)(2,1)S(1)}, u32[]{:S(2)}, u32[]{:S(2)}) collective-permute-start(bf16[112,384]{1,0:T(8,128)(2,1)S(1)} %get-tuple-element.39), channel_id=1, source_target_pairs={{0,14},{2,16},{4,18},{6,20},{8,22},{10,24},{12,26},{14,28},{16,30}... | collective-permute-start | bytes 258056 | tf_op jit(solution)/shard_map/apply/ppermute | solution.py:306
  38.8 4.8 %collective-permute-start.12 = (bf16[112,384]{1,0:T(8,128)(2,1)S(1)}, bf16[112,384]{1,0:T(8,128)(2,1)S(1)}, u32[]{:S(2)}, u32[]{:S(2)}) collective-permute-start(bf16[112,384]{1,0:T(8,128)(2,1)S(1)} %get-tuple-element.40), channel_id=1, source_target_pairs={{0,4},{2,6},{4,0},{6,2},{8,12},{10,14},{12,8},{14,10},{16,20},{18,... | collective-permute-start | bytes 258056 | tf_op jit(solution)/shard_map/apply/ppermute | solution.py:306
  41.2 4.6 %collective-permute-start.13 = (bf16[112,384]{1,0:T(8,128)(2,1)S(1)}, bf16[112,384]{1,0:T(8,128)(2,1)S(1)}, u32[]{:S(2)}, u32[]{:S(2)}) collective-permute-start(bf16[112,384]{1,0:T(8,128)(2,1)S(1)} %get-tuple-element.41), channel_id=1, source_target_pairs={{0,2},{2,0},{4,6},{6,4},{8,10},{10,8},{12,14},{14,12},{16,18},{18,... | collective-permute-start | bytes 258056 | tf_op jit(solution)/shard_map/apply/ppermute | solution.py:306
  42.0 3.7 %collective-permute-start.14 = (bf16[112,384]{1,0:T(8,128)(2,1)S(1)}, bf16[112,384]{1,0:T(8,128)(2,1)S(1)}, u32[]{:S(2)}, u32[]{:S(2)}) collective-permute-start(bf16[112,384]{1,0:T(8,128)(2,1)S(1)} %get-tuple-element.42), channel_id=1, source_target_pairs={{0,1},{1,0},{2,3},{3,2},{4,5},{5,4},{6,7},{7,6},{8,9},{9,8},{10,11... | collective-permute-start | bytes 258056 | tf_op jit(solution)/shard_map/apply/ppermute | solution.py:316
  46.2 9.0 %collective-permute-start.15 = (bf16[112,384]{1,0:T(8,128)(2,1)S(1)}, bf16[112,384]{1,0:T(8,128)(2,1)S(1)}, u32[]{:S(2)}, u32[]{:S(2)}) collective-permute-start(bf16[112,384]{1,0:T(8,128)(2,1)S(1)} %get-tuple-element.45), channel_id=1, source_target_pairs={{0,28},{2,30},{4,8},{6,10},{8,4},{10,6},{12,16},{14,18},{16,12},{1... | collective-permute-start | bytes 258056 | tf_op jit(solution)/shard_map/apply/ppermute | solution.py:306
  49.5 7.7 %collective-permute-start.17 = (bf16[112,384]{1,0:T(8,128)(2,1)S(1)}, bf16[112,384]{1,0:T(8,128)(2,1)S(1)}, u32[]{:S(2)}, u32[]{:S(2)}) collective-permute-start(bf16[112,384]{1,0:T(8,128)(2,1)S(1)} %get-tuple-element.47), channel_id=1, source_target_pairs={{0,16},{2,18},{4,20},{6,22},{8,24},{10,26},{12,28},{14,30},{16,0},... | collective-permute-start | bytes 258056 | tf_op jit(solution)/shard_map/apply/ppermute | solution.py:306
  49.5 8.6 %collective-permute-start.16 = (bf16[112,384]{1,0:T(8,128)(2,1)S(1)}, bf16[112,384]{1,0:T(8,128)(2,1)S(1)}, u32[]{:S(2)}, u32[]{:S(2)}) collective-permute-start(bf16[112,384]{1,0:T(8,128)(2,1)S(1)} %get-tuple-element.46), channel_id=1, source_target_pairs={{0,30},{2,4},{4,2},{6,8},{8,6},{10,12},{12,10},{14,16},{16,14},{18... | collective-permute-start | bytes 258056 | tf_op jit(solution)/shard_map/apply/ppermute | solution.py:306
  51.7 7.2 %collective-permute-start.18 = (bf16[112,384]{1,0:T(8,128)(2,1)S(1)}, bf16[112,384]{1,0:T(8,128)(2,1)S(1)}, u32[]{:S(2)}, u32[]{:S(2)}) collective-permute-start(bf16[112,384]{1,0:T(8,128)(2,1)S(1)} %get-tuple-element.48), channel_id=1, source_target_pairs={{0,14},{2,16},{4,18},{6,20},{8,22},{10,24},{12,26},{14,28},{16,30}... | collective-permute-start | bytes 258056 | tf_op jit(solution)/shard_map/apply/ppermute | solution.py:306
  54.8 4.5 %collective-permute-start.19 = (bf16[112,384]{1,0:T(8,128)(2,1)S(1)}, bf16[112,384]{1,0:T(8,128)(2,1)S(1)}, u32[]{:S(2)}, u32[]{:S(2)}) collective-permute-start(bf16[112,384]{1,0:T(8,128)(2,1)S(1)} %get-tuple-element.51), channel_id=1, source_target_pairs={{0,4},{2,6},{4,0},{6,2},{8,12},{10,14},{12,8},{14,10},{16,20},{18,... | collective-permute-start | bytes 258056 | tf_op jit(solution)/shard_map/apply/ppermute | solution.py:306
  55.2 4.7 %collective-permute-start.20 = (bf16[112,384]{1,0:T(8,128)(2,1)S(1)}, bf16[112,384]{1,0:T(8,128)(2,1)S(1)}, u32[]{:S(2)}, u32[]{:S(2)}) collective-permute-start(bf16[112,384]{1,0:T(8,128)(2,1)S(1)} %get-tuple-element.52), channel_id=1, source_target_pairs={{0,2},{2,0},{4,6},{6,4},{8,10},{10,8},{12,14},{14,12},{16,18},{18,... | collective-permute-start | bytes 258056 | tf_op jit(solution)/shard_map/apply/ppermute | solution.py:306
  57.3 2.6 %collective-permute-start.21 = (bf16[112,384]{1,0:T(8,128)(2,1)S(1)}, bf16[112,384]{1,0:T(8,128)(2,1)S(1)}, u32[]{:S(2)}, u32[]{:S(2)}) collective-permute-start(bf16[112,384]{1,0:T(8,128)(2,1)S(1)} %get-tuple-element.53), channel_id=1, source_target_pairs={{0,1},{1,0},{2,3},{3,2},{4,5},{5,4},{6,7},{7,6},{8,9},{9,8},{10,11... | collective-permute-start | bytes 258056 | tf_op jit(solution)/shard_map/apply/ppermute | solution.py:316
  (2 other events, 1.4 us)

commit v5 on v2

--- a/solution.py
+++ b/solution.py
@@ -184,7 +184,7 @@
     ]
 
 
-def cross_kernel(asks, bands, *refs):
+def cross_kernel(asks, bands, factors, weights, *refs):
     arrived, out = refs[:-1], refs[-1]
     out[0], out[1] = source_sums(asks, bands, 0, arrived, out.shape[1])
 
@@ -426,8 +426,8 @@
             (cross,) = call(
                 cross_kernel,
                 [sums],
-                (asks, bands, *arrived[:half]),
-                [VMEM] * (2 + half),
+                (asks, bands, factors, weights, *arrived[:half]),
+                [VMEM] * (4 + half),
                 flops=4 * one,
             )
             if first:

time: 72.6 us -> 73.7 us (1.015)
  waiting for transfers between devices: 16.3 us -> 17.1 us
    ppermute x19, waiting for transfers between devices: 16.3 us -> 17.1 us  [moved_by(): return held(lax.ppermute(x, 'areal', pairs))]
  transfers between devices with their start and end apart: 22 -> 22, of which waited for: 9 -> 12; matrix products, arithmetic and copies ran while one was open for 0% -> 0% of each run, Pallas kernels for 8% -> 9%
where the time goes in v5:
time: 73.7 us; the launch traced here: 73.6 us
  starting transfers between devices  33.1 us (45%)
  waiting for transfers between devices  17.1 us (23%)
  blocking collectives  11.2 us (15%)
  Pallas kernels  10.7 us (15%)
  between operations  1.53 us (2%)
    ppermute x19, starting transfers between devices, moved_by(): return held(lax.ppermute(x, 'areal', pairs))  33 us
    ppermute x19, waiting for transfers between devices, moved_by(): return held(lax.ppermute(x, 'areal', pairs))  17.1 us
    all_to_all x1, blocking collectives, on_device(): landed = lax.all_to_all(pieces, ('areal', 'layer'), 0, 0, tiled=True)  11.2 us
    pallas_call x21, Pallas kernels, call(): pl.pallas_call(kernel, out_shape=outs, in_specs=specs, out_specs=out_spec...  10.7 us
  transfers between devices with their start and end apart: 22, of which 12 were waited for; matrix products, arithmetic and copies ran while one was open for 0% of the time, Pallas kernels for 9%

profile of v5, /device:TPU:0, one launch (start us, length us, event | category | flops | bytes accessed | tf_op | source)
XLA Modules:
  0.0 73.6 jit_solution(12658467284381525156)
XLA Ops:
  1.3 1.6 %plan.1 = (s32[12]{0:T(128)S(1)}, f32[8,128]{1,0:T(8,128)S(1)}, bf16[240,384]{1,0:T(8,128)(2,1)S(1)}, bf16[224,384]{1,0:T(8,128)(2,1)S(1)}) custom-call(s32[6]{0:T(128)} %bitcast.24, s32[1]{0:T(128)} %bitcast.15.count, s32[32]{0:T(128)} %tile_map.1, s32[1]{0:T(128)} %bitcast.2.me, s32[1]{0:T(128)} %bitcast.3.group, bf16[224,384]{1,0:T(8,128)(2,1)} %bitcast.22), custom_call_target="tpu_custom_call" | custom-call | tf_op jit(solution)/shard_map/plan/pallas_call | solution.py:286
  2.9 3.0 %collective-permute-start.3 = (bf16[240,384]{1,0:T(8,128)(2,1)S(1)}, bf16[240,384]{1,0:T(8,128)(2,1)S(1)}, u32[]{:S(2)}, u32[]{:S(2)}) collective-permute-start(bf16[240,384]{1,0:T(8,128)(2,1)S(1)} %get-tuple-element.32), channel_id=1, source_target_pairs={{0,2},{2,0},{4,6},{6,4},{8,10},{10,8},{12,14},{14,12},{16,18},{18,... | collective-permute-start | bytes 552968 | tf_op jit(solution)/shard_map/apply/ppermute | solution.py:300
  5.9 4.5 %collective-permute-start.1 = (bf16[240,384]{1,0:T(8,128)(2,1)S(1)}, bf16[240,384]{1,0:T(8,128)(2,1)S(1)}, u32[]{:S(2)}, u32[]{:S(2)}) collective-permute-start(bf16[240,384]{1,0:T(8,128)(2,1)S(1)} %get-tuple-element.32), channel_id=1, source_target_pairs={{0,30},{2,4},{4,2},{6,8},{8,6},{10,12},{12,10},{14,16},{16,14},{18... | collective-permute-start | bytes 552968 | tf_op jit(solution)/shard_map/apply/ppermute | solution.py:300
  10.4 0.8 %collective-permute-start = (bf16[240,384]{1,0:T(8,128)(2,1)S(1)}, bf16[240,384]{1,0:T(8,128)(2,1)S(1)}, u32[]{:S(2)}, u32[]{:S(2)}) collective-permute-start(bf16[240,384]{1,0:T(8,128)(2,1)S(1)} %get-tuple-element.32), channel_id=1, source_target_pairs={{0,28},{2,30},{4,8},{6,10},{8,4},{10,6},{12,16},{14,18},{16,12},{1... | collective-permute-start | bytes 552968 | tf_op jit(solution)/shard_map/apply/ppermute | solution.py:300
  11.3 2.3 %collective-permute-done.3.odd.refs_1_.refs_6_ = bf16[240,384]{1,0:T(8,128)(2,1)S(1)} collective-permute-done((bf16[240,384]{1,0:T(8,128)(2,1)S(1)}, bf16[240,384]{1,0:T(8,128)(2,1)S(1)}, u32[]{:S(2)}, u32[]{:S(2)}) %collective-permute-start.3) | collective-permute-done | bytes 184352 | tf_op jit(solution)/shard_map/apply/ppermute | solution.py:300
  13.6 2.4 %load.3 = (bf16[6,384,768]{2,1,0:T(8,128)(2,1)S(1)}, bf16[3,384,384]{2,1,0:T(8,128)(2,1)S(1)}) custom-call(s32[12]{0:T(128)S(1)} %get-tuple-element.28.table, s32[1]{0:T(128)} %bitcast.3.group, bf16[2,6,384,384]{3,2,1,0:T(8,128)(2,1)} %bitcast.20, bf16[2,2,384,384]{3,2,1,0:T(8,128)(2,1)} %bitcast.21), custom_call_target="tpu_custom_call" | custom-call | bytes 4718592 | tf_op jit(solution)/shard_map/load/pallas_call | solution.py:286
  16.3 1.7 %collective-permute-done.1.refs_1_.even.refs_4_ = bf16[240,384]{1,0:T(8,128)(2,1)S(1)} collective-permute-done((bf16[240,384]{1,0:T(8,128)(2,1)S(1)}, bf16[240,384]{1,0:T(8,128)(2,1)S(1)}, u32[]{:S(2)}, u32[]{:S(2)}) %collective-permute-start.1) | collective-permute-done | bytes 184352 | tf_op jit(solution)/shard_map/apply/ppermute | solution.py:300
  18.0 4.0 %collective-permute-done.2.pair.refs_1_ = bf16[224,384]{1,0:T(8,128)(2,1)S(1)} collective-permute-done((bf16[224,384]{1,0:T(8,128)(2,1)S(1)}, bf16[224,384]{1,0:T(8,128)(2,1)S(1)}, u32[]{:S(2)}, u32[]{:S(2)}) %collective-permute-start.2) | collective-permute-done | bytes 172064 | tf_op jit(solution)/shard_map/plan/ppermute | solution.py:300
  22.1 4.1 %collective-permute-start.4 = (bf16[112,384]{1,0:T(8,128)(2,1)S(1)}, bf16[112,384]{1,0:T(8,128)(2,1)S(1)}, u32[]{:S(2)}, u32[]{:S(2)}) collective-permute-start(bf16[112,384]{1,0:T(8,128)(2,1)S(1)} %apply.19), channel_id=1, source_target_pairs={{0,30},{2,0},{4,2},{6,4},{8,6},{10,8},{12,10},{14,12},{16,14},{18,... | collective-permute-start | bytes 258056 | tf_op jit(solution)/shard_map/apply/ppermute | solution.py:300
  27.4 0.9 %collective-permute-done.4.refs_0_ = bf16[112,384]{1,0:T(8,128)(2,1)S(1)} collective-permute-done((bf16[112,384]{1,0:T(8,128)(2,1)S(1)}, bf16[112,384]{1,0:T(8,128)(2,1)S(1)}, u32[]{:S(2)}, u32[]{:S(2)}) %collective-permute-start.4) | collective-permute-done | bytes 86048 | tf_op jit(solution)/shard_map/apply/ppermute | solution.py:300
  28.7 2.9 %collective-permute-done.7.refs_7_ = f32[8,128]{1,0:T(8,128)S(1)} collective-permute-done((f32[8,128]{1,0:T(8,128)S(1)}, f32[8,128]{1,0:T(8,128)S(1)}, u32[]{:S(2)}, u32[]{:S(2)}) %collective-permute-start.7) | collective-permute-done | bytes 4128 | tf_op jit(solution)/shard_map/apply/ppermute | solution.py:300
  32.1 2.2 %collective-permute-start.8 = (bf16[112,384]{1,0:T(8,128)(2,1)S(1)}, bf16[112,384]{1,0:T(8,128)(2,1)S(1)}, u32[]{:S(2)}, u32[]{:S(2)}) collective-permute-start(bf16[112,384]{1,0:T(8,128)(2,1)S(1)} %get-tuple-element.34), channel_id=1, source_target_pairs={{0,28},{2,30},{4,8},{6,10},{8,4},{10,6},{12,16},{14,18},{16,12},{1... | collective-permute-start | bytes 258056 | tf_op jit(solution)/shard_map/apply/ppermute | solution.py:300
  34.3 1.1 %collective-permute-start.9 = (bf16[112,384]{1,0:T(8,128)(2,1)S(1)}, bf16[112,384]{1,0:T(8,128)(2,1)S(1)}, u32[]{:S(2)}, u32[]{:S(2)}) collective-permute-start(bf16[112,384]{1,0:T(8,128)(2,1)S(1)} %get-tuple-element.35), channel_id=1, source_target_pairs={{0,30},{2,4},{4,2},{6,8},{8,6},{10,12},{12,10},{14,16},{16,14},{18... | collective-permute-start | bytes 258056 | tf_op jit(solution)/shard_map/apply/ppermute | solution.py:300
  35.4 4.2 %collective-permute-start.11 = (bf16[112,384]{1,0:T(8,128)(2,1)S(1)}, bf16[112,384]{1,0:T(8,128)(2,1)S(1)}, u32[]{:S(2)}, u32[]{:S(2)}) collective-permute-start(bf16[112,384]{1,0:T(8,128)(2,1)S(1)} %get-tuple-element.37), channel_id=1, source_target_pairs={{0,14},{2,16},{4,18},{6,20},{8,22},{10,24},{12,26},{14,28},{16,30}... | collective-permute-start | bytes 258056 | tf_op jit(solution)/shard_map/apply/ppermute | solution.py:300
  39.6 2.1 %collective-permute-start.12 = (bf16[112,384]{1,0:T(8,128)(2,1)S(1)}, bf16[112,384]{1,0:T(8,128)(2,1)S(1)}, u32[]{:S(2)}, u32[]{:S(2)}) collective-permute-start(bf16[112,384]{1,0:T(8,128)(2,1)S(1)} %get-tuple-element.38), channel_id=1, source_target_pairs={{0,4},{2,6},{4,0},{6,2},{8,12},{10,14},{12,8},{14,10},{16,20},{18,... | collective-permute-start | bytes 258056 | tf_op jit(solution)/shard_map/apply/ppermute | solution.py:300
  44.1 2.4 %collective-permute-done.13.refs_1_ = bf16[112,384]{1,0:T(8,128)(2,1)S(1)} collective-permute-done((bf16[112,384]{1,0:T(8,128)(2,1)S(1)}, bf16[112,384]{1,0:T(8,128)(2,1)S(1)}, u32[]{:S(2)}, u32[]{:S(2)}) %collective-permute-start.13) | collective-permute-done | bytes 86048 | tf_op jit(solution)/shard_map/apply/ppermute | solution.py:300
  47.0 2.8 %collective-permute-start.15 = (bf16[112,384]{1,0:T(8,128)(2,1)S(1)}, bf16[112,384]{1,0:T(8,128)(2,1)S(1)}, u32[]{:S(2)}, u32[]{:S(2)}) collective-permute-start(bf16[112,384]{1,0:T(8,128)(2,1)S(1)} %get-tuple-element.43), channel_id=1, source_target_pairs={{0,28},{2,30},{4,8},{6,10},{8,4},{10,6},{12,16},{14,18},{16,12},{1... | collective-permute-start | bytes 258056 | tf_op jit(solution)/shard_map/apply/ppermute | solution.py:300
  49.8 2.3 %collective-permute-start.16 = (bf16[112,384]{1,0:T(8,128)(2,1)S(1)}, bf16[112,384]{1,0:T(8,128)(2,1)S(1)}, u32[]{:S(2)}, u32[]{:S(2)}) collective-permute-start(bf16[112,384]{1,0:T(8,128)(2,1)S(1)} %get-tuple-element.44), channel_id=1, source_target_pairs={{0,30},{2,4},{4,2},{6,8},{8,6},{10,12},{12,10},{14,16},{16,14},{18... | collective-permute-start | bytes 258056 | tf_op jit(solution)/shard_map/apply/ppermute | solution.py:300
  52.2 2.9 %collective-permute-start.18 = (bf16[112,384]{1,0:T(8,128)(2,1)S(1)}, bf16[112,384]{1,0:T(8,128)(2,1)S(1)}, u32[]{:S(2)}, u32[]{:S(2)}) collective-permute-start(bf16[112,384]{1,0:T(8,128)(2,1)S(1)} %get-tuple-element.46), channel_id=1, source_target_pairs={{0,14},{2,16},{4,18},{6,20},{8,22},{10,24},{12,26},{14,28},{16,30}... | collective-permute-start | bytes 258056 | tf_op jit(solution)/shard_map/apply/ppermute | solution.py:300
  56.0 2.1 %collective-permute-start.20 = (bf16[112,384]{1,0:T(8,128)(2,1)S(1)}, bf16[112,384]{1,0:T(8,128)(2,1)S(1)}, u32[]{:S(2)}, u32[]{:S(2)}) collective-permute-start(bf16[112,384]{1,0:T(8,128)(2,1)S(1)} %get-tuple-element.48), channel_id=1, source_target_pairs={{0,2},{2,0},{4,6},{6,4},{8,10},{10,8},{12,14},{14,12},{16,18},{18,... | collective-permute-start | bytes 258056 | tf_op jit(solution)/shard_map/apply/ppermute | solution.py:300
  58.8 0.8 %collective-permute-done.18.passed = bf16[112,384]{1,0:T(8,128)(2,1)S(1)} collective-permute-done((bf16[112,384]{1,0:T(8,128)(2,1)S(1)}, bf16[112,384]{1,0:T(8,128)(2,1)S(1)}, u32[]{:S(2)}, u32[]{:S(2)}) %collective-permute-start.18) | collective-permute-done | bytes 86048 | tf_op jit(solution)/shard_map/apply/ppermute | solution.py:300
  60.6 1.1 %apply.31 = (bf16[2,112,384]{2,1,0:T(8,128)(2,1)}, bf16[32,8,112]{2,1,0:T(8,128)(2,1)S(1)}) custom-call(f32[2,112,384]{2,1,0:T(8,128)S(1)} %apply.27.part, f32[2,112,384]{2,1,0:T(8,128)S(1)} %apply.30.far, f32[8,128]{1,0:T(8,128)S(1)} %get-tuple-element.30.asks, bf16[6,384,768]{2,1,0:T(8,128)(2,1)S(1)} %get-tuple-element.31.bands, ...), custom_call_target="tpu_custom_call" | custom-call | flops 33030144 | bytes 165150 | tf_op jit(solution)/shard_map/apply/pallas_call | solution.py:286
  61.7 11.2 %all_to_all.5.pieces = bf16[32,8,112]{2,1,0:T(8,128)(2,1)S(1)} all-to-all(bf16[32,8,112]{2,1,0:T(8,128)(2,1)S(1)} %get-tuple-element.51), channel_id=1, replica_groups=mesh['areal'=16,'layer'=2] {'areal','layer'}, dimensions={0} | all-to-all | bytes 114688 | tf_op jit(solution)/shard_map/project/all_to_all | solution.py:486
  72.9 0.7 project.1
  (50 shorter events, 7.7 us)
Async XLA Ops:
  2.9 10.7 %collective-permute-start.3 = (bf16[240,384]{1,0:T(8,128)(2,1)S(1)}, bf16[240,384]{1,0:T(8,128)(2,1)S(1)}, u32[]{:S(2)}, u32[]{:S(2)}) collective-permute-start(bf16[240,384]{1,0:T(8,128)(2,1)S(1)} %get-tuple-element.32), channel_id=1, source_target_pairs={{0,2},{2,0},{4,6},{6,4},{8,10},{10,8},{12,14},{14,12},{16,18},{18,... | collective-permute-start | bytes 552968 | tf_op jit(solution)/shard_map/apply/ppermute | solution.py:300
  5.9 12.2 %collective-permute-start.1 = (bf16[240,384]{1,0:T(8,128)(2,1)S(1)}, bf16[240,384]{1,0:T(8,128)(2,1)S(1)}, u32[]{:S(2)}, u32[]{:S(2)}) collective-permute-start(bf16[240,384]{1,0:T(8,128)(2,1)S(1)} %get-tuple-element.32), channel_id=1, source_target_pairs={{0,30},{2,4},{4,2},{6,8},{8,6},{10,12},{12,10},{14,16},{16,14},{18... | collective-permute-start | bytes 552968 | tf_op jit(solution)/shard_map/apply/ppermute | solution.py:300
  10.4 11.6 %collective-permute-start.2 = (bf16[224,384]{1,0:T(8,128)(2,1)S(1)}, bf16[224,384]{1,0:T(8,128)(2,1)S(1)}, u32[]{:S(2)}, u32[]{:S(2)}) collective-permute-start(bf16[224,384]{1,0:T(8,128)(2,1)S(1)} %get-tuple-element.27.lam.rhs), channel_id=1, source_target_pairs={{0,16},{2,18},{4,20},{6,22},{8,24},{10,26},{12,28},{14,30},{16,0},... | collective-permute-start | bytes 516104 | tf_op jit(solution)/shard_map/plan/ppermute | solution.py:300
  10.4 16.6 %collective-permute-start = (bf16[240,384]{1,0:T(8,128)(2,1)S(1)}, bf16[240,384]{1,0:T(8,128)(2,1)S(1)}, u32[]{:S(2)}, u32[]{:S(2)}) collective-permute-start(bf16[240,384]{1,0:T(8,128)(2,1)S(1)} %get-tuple-element.32), channel_id=1, source_target_pairs={{0,28},{2,30},{4,8},{6,10},{8,4},{10,6},{12,16},{14,18},{16,12},{1... | collective-permute-start | bytes 552968 | tf_op jit(solution)/shard_map/apply/ppermute | solution.py:300
  11.3 17.4 %collective-permute-start.6 = (bf16[240,384]{1,0:T(8,128)(2,1)S(1)}, bf16[240,384]{1,0:T(8,128)(2,1)S(1)}, u32[]{:S(2)}, u32[]{:S(2)}) collective-permute-start(bf16[240,384]{1,0:T(8,128)(2,1)S(1)} %get-tuple-element.32), channel_id=1, source_target_pairs={{0,1},{1,0},{2,3},{3,2},{4,5},{5,4},{6,7},{7,6},{8,9},{9,8},{10,11... | collective-permute-start | bytes 552968 | tf_op jit(solution)/shard_map/apply/ppermute | solution.py:310
  13.6 15.1 %collective-permute-start.5 = (bf16[240,384]{1,0:T(8,128)(2,1)S(1)}, bf16[240,384]{1,0:T(8,128)(2,1)S(1)}, u32[]{:S(2)}, u32[]{:S(2)}) collective-permute-start(bf16[240,384]{1,0:T(8,128)(2,1)S(1)} %get-tuple-element.32), channel_id=1, source_target_pairs={{0,4},{2,6},{4,0},{6,2},{8,12},{10,14},{12,8},{14,10},{16,20},{18,... | collective-permute-start | bytes 552968 | tf_op jit(solution)/shard_map/apply/ppermute | solution.py:300
  13.6 12.7 %copy-start.2 = (s32[1,2,4]{2,1,0:T(2,128)S(1)}, s32[1,2,4]{2,1,0:T(2,128)}, u32[]{:S(2)}) copy-start(s32[1,2,4]{2,1,0:T(2,128)} %param.16) | copy-start | bytes 100
  13.6 12.7 %copy-start.3 = (f32[1,2,4]{2,1,0:T(2,128)S(1)}, f32[1,2,4]{2,1,0:T(2,128)}, u32[]{:S(2)}) copy-start(f32[1,2,4]{2,1,0:T(2,128)} %param.17) | copy-start | bytes 100
  22.1 6.2 %collective-permute-start.4 = (bf16[112,384]{1,0:T(8,128)(2,1)S(1)}, bf16[112,384]{1,0:T(8,128)(2,1)S(1)}, u32[]{:S(2)}, u32[]{:S(2)}) collective-permute-start(bf16[112,384]{1,0:T(8,128)(2,1)S(1)} %apply.19), channel_id=1, source_target_pairs={{0,30},{2,0},{4,2},{6,4},{8,6},{10,8},{12,10},{14,12},{16,14},{18,... | collective-permute-start | bytes 258056 | tf_op jit(solution)/shard_map/apply/ppermute | solution.py:300
  26.9 4.6 %collective-permute-start.7 = (f32[8,128]{1,0:T(8,128)S(1)}, f32[8,128]{1,0:T(8,128)S(1)}, u32[]{:S(2)}, u32[]{:S(2)}) collective-permute-start(f32[8,128]{1,0:T(8,128)S(1)} %apply.18.relayed), channel_id=1, source_target_pairs={{0,16},{2,18},{4,20},{6,22},{8,24},{10,26},{12,28},{14,30},{16,0},... | collective-permute-start | bytes 12296 | tf_op jit(solution)/shard_map/apply/ppermute | solution.py:300
  32.1 9.9 %collective-permute-start.8 = (bf16[112,384]{1,0:T(8,128)(2,1)S(1)}, bf16[112,384]{1,0:T(8,128)(2,1)S(1)}, u32[]{:S(2)}, u32[]{:S(2)}) collective-permute-start(bf16[112,384]{1,0:T(8,128)(2,1)S(1)} %get-tuple-element.34), channel_id=1, source_target_pairs={{0,28},{2,30},{4,8},{6,10},{8,4},{10,6},{12,16},{14,18},{16,12},{1... | collective-permute-start | bytes 258056 | tf_op jit(solution)/shard_map/apply/ppermute | solution.py:300
  34.3 7.7 %collective-permute-start.10 = (bf16[112,384]{1,0:T(8,128)(2,1)S(1)}, bf16[112,384]{1,0:T(8,128)(2,1)S(1)}, u32[]{:S(2)}, u32[]{:S(2)}) collective-permute-start(bf16[112,384]{1,0:T(8,128)(2,1)S(1)} %get-tuple-element.36), channel_id=1, source_target_pairs={{0,16},{2,18},{4,20},{6,22},{8,24},{10,26},{12,28},{14,30},{16,0},... | collective-permute-start | bytes 258056 | tf_op jit(solution)/shard_map/apply/ppermute | solution.py:300
  34.3 8.3 %collective-permute-start.9 = (bf16[112,384]{1,0:T(8,128)(2,1)S(1)}, bf16[112,384]{1,0:T(8,128)(2,1)S(1)}, u32[]{:S(2)}, u32[]{:S(2)}) collective-permute-start(bf16[112,384]{1,0:T(8,128)(2,1)S(1)} %get-tuple-element.35), channel_id=1, source_target_pairs={{0,30},{2,4},{4,2},{6,8},{8,6},{10,12},{12,10},{14,16},{16,14},{18... | collective-permute-start | bytes 258056 | tf_op jit(solution)/shard_map/apply/ppermute | solution.py:300
  35.4 8.1 %collective-permute-start.11 = (bf16[112,384]{1,0:T(8,128)(2,1)S(1)}, bf16[112,384]{1,0:T(8,128)(2,1)S(1)}, u32[]{:S(2)}, u32[]{:S(2)}) collective-permute-start(bf16[112,384]{1,0:T(8,128)(2,1)S(1)} %get-tuple-element.37), channel_id=1, source_target_pairs={{0,14},{2,16},{4,18},{6,20},{8,22},{10,24},{12,26},{14,28},{16,30}... | collective-permute-start | bytes 258056 | tf_op jit(solution)/shard_map/apply/ppermute | solution.py:300
  39.6 4.5 %collective-permute-start.12 = (bf16[112,384]{1,0:T(8,128)(2,1)S(1)}, bf16[112,384]{1,0:T(8,128)(2,1)S(1)}, u32[]{:S(2)}, u32[]{:S(2)}) collective-permute-start(bf16[112,384]{1,0:T(8,128)(2,1)S(1)} %get-tuple-element.38), channel_id=1, source_target_pairs={{0,4},{2,6},{4,0},{6,2},{8,12},{10,14},{12,8},{14,10},{16,20},{18,... | collective-permute-start | bytes 258056 | tf_op jit(solution)/shard_map/apply/ppermute | solution.py:300
  42.0 4.6 %collective-permute-start.13 = (bf16[112,384]{1,0:T(8,128)(2,1)S(1)}, bf16[112,384]{1,0:T(8,128)(2,1)S(1)}, u32[]{:S(2)}, u32[]{:S(2)}) collective-permute-start(bf16[112,384]{1,0:T(8,128)(2,1)S(1)} %get-tuple-element.39), channel_id=1, source_target_pairs={{0,2},{2,0},{4,6},{6,4},{8,10},{10,8},{12,14},{14,12},{16,18},{18,... | collective-permute-start | bytes 258056 | tf_op jit(solution)/shard_map/apply/ppermute | solution.py:300
  42.0 4.5 %collective-permute-start.14 = (bf16[112,384]{1,0:T(8,128)(2,1)S(1)}, bf16[112,384]{1,0:T(8,128)(2,1)S(1)}, u32[]{:S(2)}, u32[]{:S(2)}) collective-permute-start(bf16[112,384]{1,0:T(8,128)(2,1)S(1)} %get-tuple-element.40), channel_id=1, source_target_pairs={{0,1},{1,0},{2,3},{3,2},{4,5},{5,4},{6,7},{7,6},{8,9},{9,8},{10,11... | collective-permute-start | bytes 258056 | tf_op jit(solution)/shard_map/apply/ppermute | solution.py:310
  47.0 9.0 %collective-permute-start.15 = (bf16[112,384]{1,0:T(8,128)(2,1)S(1)}, bf16[112,384]{1,0:T(8,128)(2,1)S(1)}, u32[]{:S(2)}, u32[]{:S(2)}) collective-permute-start(bf16[112,384]{1,0:T(8,128)(2,1)S(1)} %get-tuple-element.43), channel_id=1, source_target_pairs={{0,28},{2,30},{4,8},{6,10},{8,4},{10,6},{12,16},{14,18},{16,12},{1... | collective-permute-start | bytes 258056 | tf_op jit(solution)/shard_map/apply/ppermute | solution.py:300
  49.8 8.2 %collective-permute-start.17 = (bf16[112,384]{1,0:T(8,128)(2,1)S(1)}, bf16[112,384]{1,0:T(8,128)(2,1)S(1)}, u32[]{:S(2)}, u32[]{:S(2)}) collective-permute-start(bf16[112,384]{1,0:T(8,128)(2,1)S(1)} %get-tuple-element.45), channel_id=1, source_target_pairs={{0,16},{2,18},{4,20},{6,22},{8,24},{10,26},{12,28},{14,30},{16,0},... | collective-permute-start | bytes 258056 | tf_op jit(solution)/shard_map/apply/ppermute | solution.py:300
  49.8 8.7 %collective-permute-start.16 = (bf16[112,384]{1,0:T(8,128)(2,1)S(1)}, bf16[112,384]{1,0:T(8,128)(2,1)S(1)}, u32[]{:S(2)}, u32[]{:S(2)}) collective-permute-start(bf16[112,384]{1,0:T(8,128)(2,1)S(1)} %get-tuple-element.44), channel_id=1, source_target_pairs={{0,30},{2,4},{4,2},{6,8},{8,6},{10,12},{12,10},{14,16},{16,14},{18... | collective-permute-start | bytes 258056 | tf_op jit(solution)/shard_map/apply/ppermute | solution.py:300
  52.2 7.5 %collective-permute-start.18 = (bf16[112,384]{1,0:T(8,128)(2,1)S(1)}, bf16[112,384]{1,0:T(8,128)(2,1)S(1)}, u32[]{:S(2)}, u32[]{:S(2)}) collective-permute-start(bf16[112,384]{1,0:T(8,128)(2,1)S(1)} %get-tuple-element.46), channel_id=1, source_target_pairs={{0,14},{2,16},{4,18},{6,20},{8,22},{10,24},{12,26},{14,28},{16,30}... | collective-permute-start | bytes 258056 | tf_op jit(solution)/shard_map/apply/ppermute | solution.py:300
  55.1 4.8 %collective-permute-start.19 = (bf16[112,384]{1,0:T(8,128)(2,1)S(1)}, bf16[112,384]{1,0:T(8,128)(2,1)S(1)}, u32[]{:S(2)}, u32[]{:S(2)}) collective-permute-start(bf16[112,384]{1,0:T(8,128)(2,1)S(1)} %get-tuple-element.47), channel_id=1, source_target_pairs={{0,4},{2,6},{4,0},{6,2},{8,12},{10,14},{12,8},{14,10},{16,20},{18,... | collective-permute-start | bytes 258056 | tf_op jit(solution)/shard_map/apply/ppermute | solution.py:300
  56.0 4.6 %collective-permute-start.20 = (bf16[112,384]{1,0:T(8,128)(2,1)S(1)}, bf16[112,384]{1,0:T(8,128)(2,1)S(1)}, u32[]{:S(2)}, u32[]{:S(2)}) collective-permute-start(bf16[112,384]{1,0:T(8,128)(2,1)S(1)} %get-tuple-element.48), channel_id=1, source_target_pairs={{0,2},{2,0},{4,6},{6,4},{8,10},{10,8},{12,14},{14,12},{16,18},{18,... | collective-permute-start | bytes 258056 | tf_op jit(solution)/shard_map/apply/ppermute | solution.py:300
  58.1 2.5 %collective-permute-start.21 = (bf16[112,384]{1,0:T(8,128)(2,1)S(1)}, bf16[112,384]{1,0:T(8,128)(2,1)S(1)}, u32[]{:S(2)}, u32[]{:S(2)}) collective-permute-start(bf16[112,384]{1,0:T(8,128)(2,1)S(1)} %get-tuple-element.49), channel_id=1, source_target_pairs={{0,1},{1,0},{2,3},{3,2},{4,5},{5,4},{6,7},{7,6},{8,9},{9,8},{10,11... | collective-permute-start | bytes 258056 | tf_op jit(solution)/shard_map/apply/ppermute | solution.py:310
  (2 other events, 25.3 us)
